TPU v7x, 32 devices: a whole 2x2x4 slice. The times are simulated.
32 devices in a mesh: seq: 16 (over z, y, x), blk: 2 (over core).
Axes of the slice: x: 2, y: 2, z: 4, core: 2. Of those that a mesh axis runs over, the one named last changes fastest.
Arguments:
- base_ids: int32 [8192], P('seq'), may hold values from 0 to 3
- span_start: int32 [1024], replicated, may hold values from 0 to 8184
- span_length: int32 [1024], replicated, may hold values from 1 to 8
- embedding: bfloat16 [5, 2048], P(None, 'blk'), may hold values from -6 to 6
- conv_kernel: bfloat16 [2, 9, 2048], P(None, None, 'blk'), may hold values from -2 to 2
- mix_weight: bfloat16 [2, 2048, 2048], P(None, 'blk'), may hold values from -0.125 to 0.125
- saved_input: bfloat16 [8192, 2048], P('seq', 'blk'), may hold values from -6 to 6
- cotangent: bfloat16 [8192, 2048], P('seq', 'blk'), may hold values from -6 to 6
Outputs:
- input_grad: bfloat16 [8192, 2048], P('seq', 'blk')
- weight_grad: float32 [2, 2048, 2048], P(None, ('blk', 'seq'))
- kernel_grad: float32 [2, 9, 2048], P(None, None, 'blk')
- embed_grad: float32 [5, 2048], P(None, 'blk')
Inputs may be any that keep to these rules, and one draw needn't show every extreme that they name: Span j masks the positions span_start[j] to span_start[j] + span_length[j] - 1, all inside the window; spans may share positions or touch.
All inputs are finite; a program needn't handle non-finite values.
Results may differ from a plain program's by a relative error of at most 0.007.
Values may be sent and summed in bfloat16 or wider, within the bound.
A program may use at most 64 MiB of HBM per device.

v0:
```python
import math

import jax
import jax.numpy as jnp
from jax import lax
from jax.sharding import PartitionSpec as P

BASE_DILATION = 4


mask_token = 4
gelu_scale = 0.7978845608028654
gelu_cubic = 0.044715


def extended(cells, sides, width):
    for axis, dim in sides:
        count = lax.axis_size(axis)
        ends = count - 1
        head = lax.slice_in_dim(cells, 0, width, axis=dim)
        tail = lax.slice_in_dim(cells, cells.shape[dim] - width, cells.shape[dim], axis=dim)
        cells = jnp.concatenate(
            [
                lax.ppermute(tail, axis, [(i, (i + 1) % count) for i in range(ends)]),
                cells,
                lax.ppermute(head, axis, [((i + 1) % count, i) for i in range(ends)]),
            ],
            axis=dim,
        )
    return cells


def gelu_pair(pre_act):
    inner_arg = gelu_scale * (pre_act + gelu_cubic * pre_act * pre_act * pre_act)
    tangent = jnp.tanh(inner_arg)
    activation = 0.5 * pre_act * (1.0 + tangent)
    derivative = 0.5 * (1.0 + tangent) + 0.5 * pre_act * (1.0 - tangent * tangent) * gelu_scale * (
        1.0 + 3.0 * gelu_cubic * pre_act * pre_act
    )
    return (activation, derivative)


def tap_sum(padded, kernel, tap_spacing, row_count, flipped):
    tap_count = kernel.shape[0]
    running = jnp.zeros((row_count, padded.shape[1]), jnp.float32)
    for tap_index in range(tap_count):
        source = tap_count - 1 - tap_index if flipped else tap_index
        window = padded[source * tap_spacing : source * tap_spacing + row_count].astype(jnp.float32)
        running = running + kernel[tap_index].astype(jnp.float32) * window
    return running


def tap_products(grad_pre, padded, tap_spacing, tap_count):
    row_count = grad_pre.shape[0]
    grad_wide = grad_pre.astype(jnp.float32)
    output_rows = []
    for tap_index in range(tap_count):
        window = padded[tap_index * tap_spacing : tap_index * tap_spacing + row_count].astype(
            jnp.float32
        )
        output_rows.append(jnp.sum(grad_wide * window, axis=0))
    return jnp.stack(output_rows)


def covered_at(positions, span_start, span_length):
    span_end = span_start + span_length
    within = (positions[:, None] >= span_start[None, :]) & (positions[:, None] < span_end[None, :])
    return jnp.any(within, axis=1)


def lookup(hot_rows, table_rows):
    return jnp.einsum("vt,vc->tc", hot_rows, table_rows, preferred_element_type=jnp.float32).astype(
        jnp.bfloat16
    )


def on_device(
    base_ids, span_start, span_length, embedding, conv_kernel, mix_weight, saved_input, cotangent
):
    row_count = saved_input.shape[0]
    block_count = conv_kernel.shape[0]
    tap_count = conv_kernel.shape[1]
    taps_per_side = tap_count // 2
    vocab_rows = embedding.shape[0]
    total_rows = row_count * lax.axis_size("seq")
    grad_scale = 1.0 / math.sqrt(total_rows)
    first_row = lax.axis_index("seq") * row_count
    positions = first_row + jnp.arange(row_count, dtype=jnp.int32)
    covered = covered_at(positions, span_start, span_length)
    masked_ids = jnp.where(covered, mask_token, base_ids)
    vocab_ids = jnp.arange(vocab_rows, dtype=jnp.int32)
    one_hot = (vocab_ids[:, None] == masked_ids[None, :]).astype(jnp.bfloat16)
    initial_reach = taps_per_side * BASE_DILATION
    first_input = lookup(one_hot, embedding)
    first_padded = extended(first_input, (("seq", 0),), initial_reach)
    upstream = jnp.where(covered[:, None], cotangent, jnp.zeros_like(cotangent))
    weight_parts = [None] * block_count
    kernel_parts = [None] * block_count
    for block_number in range(block_count - 1, -1, -1):
        tap_spacing = BASE_DILATION * 2**block_number
        reach_rows = taps_per_side * tap_spacing
        if block_number == 0:
            padded_in = first_padded
        else:
            padded_in = extended(saved_input, (("seq", 0),), reach_rows)
        kernel = conv_kernel[block_number]
        weight_rows = mix_weight[block_number]
        pre_act = tap_sum(padded_in, kernel, tap_spacing, row_count, False)
        activation, derivative = gelu_pair(pre_act)
        act_half = activation.astype(jnp.bfloat16)
        column_piece = lax.all_gather(upstream, "blk", axis=1, tiled=True)
        grad_held = lax.dot_general(
            column_piece, weight_rows, (((1,), (1,)), ((), ())), preferred_element_type=jnp.float32
        )
        block_part = lax.dot_general(
            act_half, column_piece, (((0,), (0,)), ((), ())), preferred_element_type=jnp.float32
        )
        weight_part = block_part
        grad_pre = (grad_held * derivative).astype(jnp.bfloat16)
        kernel_parts[block_number] = (
            tap_products(grad_pre, padded_in, tap_spacing, tap_count) * grad_scale
        )
        padded_grad = extended(grad_pre, (("seq", 0),), reach_rows)
        upstream = (
            upstream.astype(jnp.float32)
            + tap_sum(padded_grad, kernel, tap_spacing, row_count, True)
        ).astype(jnp.bfloat16)
        weight_part = weight_part * grad_scale
        weight_parts[block_number] = lax.psum_scatter(
            weight_part, "seq", scatter_dimension=0, tiled=True
        )
    weight_grad = jnp.stack(weight_parts)
    embed_part = jnp.dot(one_hot, upstream, preferred_element_type=jnp.float32) * grad_scale
    kernel_grad, embed_grad = lax.psum((jnp.stack(kernel_parts), embed_part), "seq")
    return (upstream, weight_grad, kernel_grad, embed_grad)


def solution(mesh):
    placed = (
        P("seq"),
        P(),
        P(),
        P(None, "blk"),
        P(None, None, "blk"),
        P(None, "blk", None),
        P("seq", "blk"),
        P("seq", "blk"),
    )
    return jax.shard_map(
        on_device,
        mesh=mesh,
        in_specs=placed,
        out_specs=(
            P("seq", "blk"),
            P(None, ("blk", "seq"), None),
            P(None, None, "blk"),
            P(None, "blk"),
        ),
        check_vma=False,
    )
```

profile of v0, /device:TPU:0, one launch (start us, length us, event | category | flops | bytes accessed | tf_op | source)
XLA Modules:
  0.0 551.7 jit_solution(16082361016227673953)
XLA Ops:
  7.2 0.0 all-gather.3.cloned.1.call-start
  7.3 0.8 add.151
  8.0 1.3 and_reduce_fusion
  9.4 2.3 broadcast_select_fusion
  11.7 0.0 all-gather.3.cloned.1.call-update
  11.8 0.0 all-gather.5.cloned.1.call-start
  11.8 4.8 collective-permute-start
  16.7 1.3 collective-permute-start.1
  18.0 0.1 slice_convert_fusion.17
  18.1 0.5 collective-permute-done
  18.6 0.3 constant_dynamic-update-slice_fusion
  18.9 4.0 collective-permute-done.1
  22.9 3.4 fusion.13
  26.3 8.3 %fusion.51 = (f32[1024]{0:T(1024)S(1)}, f32[1024]{0:T(1024)S(1)}, f32[1024]{0:T(1024)S(1)}, f32[1024]{0:T(1024)S(1)}, f32[1024]{0:T(1024)S(1)}, /*index=5*/f32[1...) fusion(bf16[544,1024]{1,0:T(8,128)(2,1)S(1)} %constant_dynamic-update-slic, ...), kind=kOutput, calls=%fused_computation.95 | convolution fusion | flops 2172115968 | bytes 18911232 | tf_op jit(solution)/shard_map/dot_general | solution.py:112
  34.7 4.3 collective-permute-start.3
  39.0 1.4 collective-permute-start.2
  40.4 0.4 collective-permute-done.3
  40.9 4.4 collective-permute-done.2
  45.3 6.9 %fusion.42 = bf16[512,1024]{1,0:T(8,128)(2,1)} fusion(bf16[512,1024]{1,0:T(8,128)(2,1)S(1)} %get-tuple-element.58, bf16[32,1024]{1,0:T(8,128)(2,1)S(1)} %collective-permute-done.3, bf16[32,1024]{1,0:T(8,128)(2,1)S(1)} %collective-permute-done.2, f32[1024]{0:T(1024)S(1)} %bitcast.63, f32[1024]{0:T(1024)S(1)} %bitcast.65, f32[1024]{0:T(1024)S(1)} %bitcast.67, ...), kind=kLoop, calls=%fused_computation.86 | loop fusion | flops 28311552 | bytes 3314176 | tf_op jit(solution)/shard_map/convert_element_type | solution.py:127
  52.1 0.0 all-gather.5.cloned.1.call-update
  52.2 0.0 reduce-scatter.5.cloned.1.call-start
  52.2 7.4 %convolution_multiply_fusion = f32[1024,2048]{1,0:T(8,128)} fusion(bf16[512,2048]{1,0:T(8,128)(2,1)} %all-gather.3.cloned.1.call-done, f32[512,1024]{1,0:T(8,128)S(1)} %copy-done.5), kind=kOutput, calls=%fused_computation.20 | convolution fusion | flops 2154299392 | bytes 12582912 | tf_op jit(solution)/shard_map/dot_general | solution.py:115
  59.7 0.0 reduce-scatter.5.cloned.1.call-update
  59.7 0.0 reduce-scatter.3.cloned.1.call-start
  59.7 0.6 copy-done.7
  60.3 0.5 convolution_convert_fusion
  60.9 1.3 collective-permute-start.5
  62.2 4.5 collective-permute-start.4
  66.7 1.6 collective-permute-done.4
  68.3 8.6 %convolution_multiply_fusion.1 = f32[1024,2048]{1,0:T(8,128)} fusion(bf16[512,2048]{1,0:T(8,128)(2,1)} %all-gather.5.cloned.1.call-done, bf16[512,1024]{1,0:T(8,128)(2,1)S(1)} %convolution_convert_fusion, bf16[16,1024]{1,0:T(8,128)(2,1)S(1)} %collective-permute-done.5, bf16[16,1024]{1,0:T(8,128)(2,1)S(1)} %collective-permute-done.4, f32[1024]{0:T(1024)S(1)} %bitcast.99, ...), kind=kOutput, calls=%fused_computation.21 | convolution fusion | flops 2180513792 | bytes 11636736 | tf_op jit(solution)/shard_map/dot_general | solution.py:115
  76.9 0.0 reduce-scatter.3.cloned.1.call-update
  76.9 0.2 all-reduce.2.cloned.1.call-start
  77.2 9.9 %fusion.67 = (f32[1024]{0:T(1024)S(1)}, f32[1024]{0:T(1024)S(1)}, f32[1024]{0:T(1024)S(1)}, f32[1024]{0:T(1024)S(1)}, f32[1024]{0:T(1024)S(1)}, /*index=5*/f32[1...) fusion(bf16[16,1024]{1,0:T(8,128)(2,1)S(1)} %collective-permute-done.5, ...), kind=kOutput, calls=%fused_computation.111 | convolution fusion | flops 2206194688 | bytes 8527872 | tf_op jit(solution)/shard_map/dot_general | solution.py:112
  87.1 4.7 collective-permute-start.7
  91.8 1.3 collective-permute-start.6
  93.2 0.1 broadcast_multiply_fusion
  93.3 0.7 pad_maximum_fusion.7
  94.0 0.0 all-reduce.2.cloned.1.call-update
  94.0 0.1 collective-permute-done.7
  94.1 5.6 %collective-permute-done.6 = bf16[16,1024]{1,0:T(8,128)(2,1)S(1)} collective-permute-done((bf16[16,1024]{1,0:T(8,128)(2,1)S(1)}, bf16[16,1024]{1,0:T(8,128)(2,1)S(1)}, u32[]{:S(2)}, u32[]{:S(2)}) %collective-permute-start.6) | collective-permute-done | bytes 32800 | tf_op jit(solution)/shard_map/ppermute | solution.py:26
  99.7 2.5 fusion.58
  102.2 0.2 convolution_multiply_fusion.2
  102.4 77.2 %psum.15 = f32[5,1024]{1,0:T(8,128)} all-reduce(f32[5,1024]{1,0:T(8,128)S(1)} %convolution_multiply_fusion.2), channel_id=1, replica_groups=mesh['seq'=16,'blk'=2] {'seq'}, use_global_device_ids=true, to_apply=%region_22.23 | all-reduce | flops 5120 | bytes 40960 | tf_op jit(solution)/shard_map/psum | solution.py:134
  179.6 70.2 %reduce-scatter.5.cloned.1.call-done = f32[64,2048]{1,0:T(8,128)} async-done(((f32[1024,2048]{1,0:T(8,128)}), f32[64,2048]{1,0:T(8,128)}) %reduce-scatter.5.cloned.1.call-update) | async-done | bytes 524304 | tf_op jit(solution)/shard_map/reduce_scatter | solution.py:129
  249.7 182.4 %reduce-scatter.3.cloned.1.call-done = f32[64,2048]{1,0:T(8,128)} async-done(((f32[1024,2048]{1,0:T(8,128)}), f32[64,2048]{1,0:T(8,128)}) %reduce-scatter.3.cloned.1.call-update) | async-done | bytes 524304 | tf_op jit(solution)/shard_map/reduce_scatter | solution.py:129
  432.1 2.3 pad_maximum_fusion.6
  434.4 109.3 %all-reduce.2.cloned.1.call-done = f32[2,9,1024]{2,0,1:T(2,128)} async-done(((f32[2,9,1024]{2,0,1:T(2,128)}), f32[2,9,1024]{2,0,1:T(2,128)}) %all-reduce.2.cloned.1.call-update) | async-done | bytes 73744 | tf_op jit(solution)/shard_map/psum | solution.py:134
  543.6 1.5 copy.31
  (44 shorter events, 0.2 us)
Async XLA Ops:
  7.2 53.2 %copy-start = (bf16[5,1024]{1,0:T(8,128)(2,1)S(1)}, bf16[5,1024]{1,0:T(8,128)(2,1)}, u32[]{:S(2)}) copy-start(bf16[5,1024]{1,0:T(8,128)(2,1)} %param.11) | copy-start | bytes 30724
  7.2 4.6 copy-start.2
  7.2 10.8 %copy-start.6 = (bf16[2,9,1024]{2,0,1:T(2,128)(2,1)S(1)}, bf16[2,9,1024]{2,0,1:T(2,128)(2,1)}, u32[]{:S(2)}) copy-start(bf16[2,9,1024]{2,0,1:T(2,128)(2,1)} %param.12) | copy-start | bytes 110596
  7.2 19.1 %all-gather.3.cloned.1.call-start = ((), (), s32[]{:S(2)}) async-start(), calls=%async_computation.2 | async-start | bytes 3145728 | tf_op jit(solution)/shard_map/all_gather | solution.py:111
  11.8 56.5 %all-gather.5.cloned.1.call-start = ((), (), s32[]{:S(2)}) async-start(), calls=%async_computation.3 | async-start | bytes 3145728 | tf_op jit(solution)/shard_map/all_gather | solution.py:111
  11.8 6.7 %collective-permute-start = (bf16[32,1024]{1,0:T(8,128)(2,1)S(1)}, bf16[32,1024]{1,0:T(8,128)(2,1)S(1)}, u32[]{:S(2)}, u32[]{:S(2)}) collective-permute-start(bf16[32,1024]{1,0:T(8,128)(2,1)S(1)} %get-tuple-element.36), channel_id=1, source_target_pairs={{0,2},{2,4},{4,6},{6,8},{8,10},{10,12},{12,14},{14,16},{16,18},{18... | collective-permute-start | bytes 196616 | tf_op jit(solution)/shard_map/ppermute | solution.py:24
  16.7 6.2 %collective-permute-start.1 = (bf16[32,1024]{1,0:T(8,128)(2,1)S(1)}, bf16[32,1024]{1,0:T(8,128)(2,1)S(1)}, u32[]{:S(2)}, u32[]{:S(2)}) collective-permute-start(bf16[32,1024]{1,0:T(8,128)(2,1)S(1)} %get-tuple-element.37), channel_id=1, source_target_pairs={{2,0},{4,2},{6,4},{8,6},{10,8},{12,10},{14,12},{16,14},{18,16},{20... | collective-permute-start | bytes 196616 | tf_op jit(solution)/shard_map/ppermute | solution.py:26
  26.3 19.0 %copy-start.4 = (bf16[512,1024]{1,0:T(8,128)(2,1)S(1)}, bf16[512,1024]{1,0:T(8,128)(2,1)}, u32[]{:S(2)}) copy-start(bf16[512,1024]{1,0:T(8,128)(2,1)} %param.15) | copy-start | bytes 3145732
  34.7 6.2 %collective-permute-start.3 = (bf16[32,1024]{1,0:T(8,128)(2,1)S(1)}, bf16[32,1024]{1,0:T(8,128)(2,1)S(1)}, u32[]{:S(2)}, u32[]{:S(2)}) collective-permute-start(bf16[32,1024]{1,0:T(8,128)(2,1)S(1)} %get-tuple-element.33), channel_id=1, source_target_pairs={{0,2},{2,4},{4,6},{6,8},{8,10},{10,12},{12,14},{14,16},{16,18},{18... | collective-permute-start | bytes 196616 | tf_op jit(solution)/shard_map/ppermute | solution.py:24
  39.0 13.2 %copy-start.5 = (f32[512,1024]{1,0:T(8,128)S(1)}, f32[512,1024]{1,0:T(8,128)}, u32[]{:S(2)}) copy-start(f32[512,1024]{1,0:T(8,128)} %fusion.13) | copy-start | bytes 6291460
  39.0 6.3 %collective-permute-start.2 = (bf16[32,1024]{1,0:T(8,128)(2,1)S(1)}, bf16[32,1024]{1,0:T(8,128)(2,1)S(1)}, u32[]{:S(2)}, u32[]{:S(2)}) collective-permute-start(bf16[32,1024]{1,0:T(8,128)(2,1)S(1)} %get-tuple-element.32), channel_id=1, source_target_pairs={{2,0},{4,2},{6,4},{8,6},{10,8},{12,10},{14,12},{16,14},{18,16},{20... | collective-permute-start | bytes 196616 | tf_op jit(solution)/shard_map/ppermute | solution.py:26
  52.2 197.6 %reduce-scatter.5.cloned.1.call-start = ((), (), s32[]{:S(2)}) async-start(), calls=%async_computation.5 | async-start | bytes 8912896 | tf_op jit(solution)/shard_map/reduce_scatter | solution.py:129
  59.7 0.7 copy-start.7
  59.7 372.4 %reduce-scatter.3.cloned.1.call-start = ((), (), s32[]{:S(2)}) async-start(), calls=%async_computation.4 | async-start | bytes 8912896 | tf_op jit(solution)/shard_map/reduce_scatter | solution.py:129
  60.9 5.9 %collective-permute-start.5 = (bf16[16,1024]{1,0:T(8,128)(2,1)S(1)}, bf16[16,1024]{1,0:T(8,128)(2,1)S(1)}, u32[]{:S(2)}, u32[]{:S(2)}) collective-permute-start(bf16[16,1024]{1,0:T(8,128)(2,1)S(1)} %get-tuple-element.39), channel_id=1, source_target_pairs={{2,0},{4,2},{6,4},{8,6},{10,8},{12,10},{14,12},{16,14},{18,16},{20... | collective-permute-start | bytes 98312 | tf_op jit(solution)/shard_map/ppermute | solution.py:26
  62.2 6.1 %collective-permute-start.4 = (bf16[16,1024]{1,0:T(8,128)(2,1)S(1)}, bf16[16,1024]{1,0:T(8,128)(2,1)S(1)}, u32[]{:S(2)}, u32[]{:S(2)}) collective-permute-start(bf16[16,1024]{1,0:T(8,128)(2,1)S(1)} %get-tuple-element.38), channel_id=1, source_target_pairs={{0,2},{2,4},{4,6},{6,8},{8,10},{10,12},{12,14},{14,16},{16,18},{18... | collective-permute-start | bytes 98312 | tf_op jit(solution)/shard_map/ppermute | solution.py:24
  76.9 466.8 %all-reduce.2.cloned.1.call-start = ((), (), s32[]{:S(2)}) async-start(), calls=%async_computation.6 | async-start | bytes 147456 | tf_op jit(solution)/shard_map/psum | solution.py:134
  77.2 22.4 %copy-start.1 = (bf16[512,1024]{1,0:T(8,128)(2,1)S(1)}, bf16[512,1024]{1,0:T(8,128)(2,1)}, u32[]{:S(2)}) copy-start(bf16[512,1024]{1,0:T(8,128)(2,1)} %fusion.42) | copy-start | bytes 3145732
  87.1 7.0 %collective-permute-start.7 = (bf16[16,1024]{1,0:T(8,128)(2,1)S(1)}, bf16[16,1024]{1,0:T(8,128)(2,1)S(1)}, u32[]{:S(2)}, u32[]{:S(2)}) collective-permute-start(bf16[16,1024]{1,0:T(8,128)(2,1)S(1)} %get-tuple-element.31), channel_id=1, source_target_pairs={{0,2},{2,4},{4,6},{6,8},{8,10},{10,12},{12,14},{14,16},{16,18},{18... | collective-permute-start | bytes 98312 | tf_op jit(solution)/shard_map/ppermute | solution.py:24
  91.8 7.9 %collective-permute-start.6 = (bf16[16,1024]{1,0:T(8,128)(2,1)S(1)}, bf16[16,1024]{1,0:T(8,128)(2,1)S(1)}, u32[]{:S(2)}, u32[]{:S(2)}) collective-permute-start(bf16[16,1024]{1,0:T(8,128)(2,1)S(1)} %get-tuple-element.30), channel_id=1, source_target_pairs={{2,0},{4,2},{6,4},{8,6},{10,8},{12,10},{14,12},{16,14},{18,16},{20... | collective-permute-start | bytes 98312 | tf_op jit(solution)/shard_map/ppermute | solution.py:26
  102.1 443.0 %copy-start.3 = (bf16[512,1024]{1,0:T(8,128)(2,1)}, bf16[512,1024]{1,0:T(8,128)(2,1)S(1)}, u32[]{:S(2)}) copy-start(bf16[512,1024]{1,0:T(8,128)(2,1)S(1)} %fusion.58) | copy-start | bytes 3145732
Sparse Core Ops, SparseCore 0:
  11.9 13.2 all-gather.2
  52.3 12.0 all-gather.4
  66.6 183.0 reduce-scatter.4
  251.9 180.1 reduce-scatter.2
  438.0 105.5 all-reduce.1
where the time goes:
time: 552 us
  waiting for transfers between devices  378 us (68%)
  blocking collectives  77.2 us (14%)
  matrix products  35 us (6%)
  starting transfers between devices  24 us (4%)
  other arithmetic  20.3 us (4%)
  between operations  14.1 us (3%)
    reduce_scatter x2, waiting for transfers between devices, on_device(): lax.psum_scatter(weight_part, 'seq', scatter_dimension=0, tiled=True)  253 us
    psum x1, waiting for transfers between devices, on_device(): lax.psum((jnp.stack(kernel_parts), embed_part), 'seq')  109 us
    psum x1, blocking collectives, on_device(): lax.psum((jnp.stack(kernel_parts), embed_part), 'seq')  77.2 us
    ppermute x4, starting transfers between devices, extended(): lax.ppermute(tail, axis, [(i, (i + 1) % count) for i in range(ends)])  18.4 us
    dot_general x2, matrix products, on_device(): lax.dot_general(column_piece, weight_rows, (((1,), (1,)), ((), ())), pref...  18.2 us
    dot_general x2, matrix products, on_device(): lax.dot_general(act_half, column_piece, (((0,), (0,)), ((), ())), preferr...  16 us
    ppermute x4, waiting for transfers between devices, extended(): lax.ppermute(head, axis, [((i + 1) % count, i) for i in range(ends)])  14 us
  transfers between devices with their start and end apart: 13, of which 10 were waited for; matrix products, arithmetic and copies ran while one was open for 7% of the time, Pallas kernels for 0%

commit v1 on v0

--- a/solution.py
+++ b/solution.py
@@ -74,6 +74,33 @@
     )
 
 
+def exchanged(cells, axis, bit):
+    count = lax.axis_size(axis)
+    return lax.ppermute(cells, axis, [(i, i ^ (1 << bit)) for i in range(count)])
+
+
+def halved_sum(part, order):
+    bits = len(order)
+    me = lax.axis_index("seq")
+    part = part.reshape((2,) * bits + (part.shape[0] >> bits, part.shape[1]))
+    axes = list(range(bits - 1, -1, -1))
+    for step, bit in enumerate(order):
+        dim = axes.index(bit)
+        mine = (me >> bit) & 1
+        send = lax.dynamic_index_in_dim(part, 1 - mine, dim, keepdims=False)
+        keep = lax.dynamic_index_in_dim(part, mine, dim, keepdims=False)
+        axes.remove(bit)
+        total = keep.astype(jnp.float32) + exchanged(send, "seq", bit).astype(jnp.float32)
+        part = total if step == bits - 1 else total.astype(jnp.bfloat16)
+    return part
+
+
+def doubled_sum(part, order):
+    for bit in order:
+        part = part + exchanged(part, "seq", bit)
+    return part
+
+
 def on_device(
     base_ids, span_start, span_length, embedding, conv_kernel, mix_weight, saved_input, cotangent
 ):
@@ -90,6 +117,8 @@
     masked_ids = jnp.where(covered, mask_token, base_ids)
     vocab_ids = jnp.arange(vocab_rows, dtype=jnp.int32)
     one_hot = (vocab_ids[:, None] == masked_ids[None, :]).astype(jnp.bfloat16)
+    bits = (lax.axis_size("seq") - 1).bit_length()
+    orders = (tuple(range(bits)), (1, 0) + tuple(range(2, bits)))
     initial_reach = taps_per_side * BASE_DILATION
     first_input = lookup(one_hot, embedding)
     first_padded = extended(first_input, (("seq", 0),), initial_reach)
@@ -112,10 +141,16 @@
         grad_held = lax.dot_general(
             column_piece, weight_rows, (((1,), (1,)), ((), ())), preferred_element_type=jnp.float32
         )
-        block_part = lax.dot_general(
-            act_half, column_piece, (((0,), (0,)), ((), ())), preferred_element_type=jnp.float32
-        )
-        weight_part = block_part
+        halves = []
+        for chunk, order in enumerate(orders):
+            width = column_piece.shape[1] // len(orders)
+            part = lax.dot_general(
+                act_half,
+                lax.slice_in_dim(column_piece, chunk * width, (chunk + 1) * width, axis=1),
+                (((0,), (0,)), ((), ())),
+                preferred_element_type=jnp.float32,
+            ).astype(jnp.bfloat16)
+            halves.append(halved_sum(part, order))
         grad_pre = (grad_held * derivative).astype(jnp.bfloat16)
         kernel_parts[block_number] = (
             tap_products(grad_pre, padded_in, tap_spacing, tap_count) * grad_scale
@@ -125,13 +160,13 @@
             upstream.astype(jnp.float32)
             + tap_sum(padded_grad, kernel, tap_spacing, row_count, True)
         ).astype(jnp.bfloat16)
-        weight_part = weight_part * grad_scale
-        weight_parts[block_number] = lax.psum_scatter(
-            weight_part, "seq", scatter_dimension=0, tiled=True
-        )
+        weight_parts[block_number] = jnp.concatenate(halves, axis=1) * grad_scale
     weight_grad = jnp.stack(weight_parts)
     embed_part = jnp.dot(one_hot, upstream, preferred_element_type=jnp.float32) * grad_scale
-    kernel_grad, embed_grad = lax.psum((jnp.stack(kernel_parts), embed_part), "seq")
+    sums = [doubled_sum(part, orders[0]) for part in kernel_parts[1:]]
+    last = doubled_sum(jnp.concatenate([kernel_parts[0], embed_part]), orders[1])
+    kernel_grad = jnp.stack([last[:tap_count]] + sums)
+    embed_grad = last[tap_count:]
     return (upstream, weight_grad, kernel_grad, embed_grad)
 
 

time: 552 us -> 216 us (0.39)
  waiting for transfers between devices: 378 us -> 69.9 us
  blocking collectives: 77.2 us -> 0 us
  starting transfers between devices: 24 us -> 72.9 us
  matrix products: 35 us -> 28.3 us
    reduce_scatter x2 -> x0, waiting for transfers between devices: 253 us -> none  [on_device(): lax.psum_scatter(weight_part, 'seq', scatter_dimension=0, tiled=True)]
    psum x1 -> x0, waiting for transfers between devices: 109 us -> none  [on_device(): lax.psum((jnp.stack(kernel_parts), embed_part), 'seq')]
    psum x1 -> x0, blocking collectives: 77.2 us -> none  [on_device(): lax.psum((jnp.stack(kernel_parts), embed_part), 'seq')]
    ppermute x0 -> x24, waiting for transfers between devices: none -> 62.5 us  [exchanged(): return lax.ppermute(cells, axis, [(i, i ^ 1 << bit) for i in range(count)])]
    ppermute x0 -> x24, starting transfers between devices: none -> 46.3 us  [exchanged(): return lax.ppermute(cells, axis, [(i, i ^ 1 << bit) for i in range(count)])]
    ppermute x4, waiting for transfers between devices: 14 us -> 5.5 us  [extended(): lax.ppermute(head, axis, [((i + 1) % count, i) for i in range(ends)])]
    dot_general x2 -> x4, matrix products: 16 us -> 10.5 us  [on_device(): lax.dot_general(act_half, lax.slice_in_dim(column_piece, chunk * width, (...]
  transfers between devices with their start and end apart: 13 -> 34, of which waited for: 10 -> 20; matrix products, arithmetic and copies ran while one was open for 7% -> 17% of each run, Pallas kernels for 0% -> 0%
where the time goes in v1:
time: 216 us; the launch traced here: 215 us
  starting transfers between devices  72.9 us (34%)
  waiting for transfers between devices  69.9 us (32%)
  matrix products  28.3 us (13%)
  other arithmetic  24.7 us (11%)
  between operations  14.8 us (7%)
  local copies, waits for them, and re-layouts  4.88 us (2%)
    ppermute x24, waiting for transfers between devices, exchanged(): return lax.ppermute(cells, axis, [(i, i ^ 1 << bit) for i in range(count)])  62.5 us
    ppermute x24, starting transfers between devices, exchanged(): return lax.ppermute(cells, axis, [(i, i ^ 1 << bit) for i in range(count)])  46.3 us
    ppermute x4, starting transfers between devices, extended(): lax.ppermute(tail, axis, [(i, (i + 1) % count) for i in range(ends)])  21.2 us
    dot_general x2, matrix products, on_device(): lax.dot_general(column_piece, weight_rows, (((1,), (1,)), ((), ())), pref...  17 us
    dot_general x4, matrix products, on_device(): lax.dot_general(act_half, lax.slice_in_dim(column_piece, chunk * width, (...  10.5 us
    convert_element_type x2, other arithmetic, on_device(): upstream = (upstream.astype(jnp.float32) + tap_sum(padded_grad, kernel, t...  9.35 us
    add x2, other arithmetic, tap_sum(): running = running + kernel[tap_index].astype(jnp.float32) * window  6.65 us
    ppermute x4, waiting for transfers between devices, extended(): lax.ppermute(head, axis, [((i + 1) % count, i) for i in range(ends)])  5.5 us
  transfers between devices with their start and end apart: 34, of which 20 were waited for; matrix products, arithmetic and copies ran while one was open for 17% of the time, Pallas kernels for 0%

profile of v1, /device:TPU:0, one launch (start us, length us, event | category | flops | bytes accessed | tf_op | source)
XLA Modules:
  0.0 215.4 jit_solution(8818584806518652490)
XLA Ops:
  8.1 1.3 and_reduce_fusion
  9.4 2.3 %broadcast_select_fusion = bf16[512,1024]{1,0:T(8,128)(2,1)} fusion(bf16[512,1024]{1,0:T(8,128)(2,1)} %param.15, pred[512]{0:T(512)(128)(4,1)S(1)} %and_reduce_fusion), kind=kLoop, calls=%fused_computation.194 | loop fusion | flops 524288 | bytes 2097664 | tf_op jit(solution)/shard_map/jit(_where)/select_n | solution.py:125
  11.8 4.8 %collective-permute-start = (bf16[32,1024]{1,0:T(8,128)(2,1)S(1)}, bf16[32,1024]{1,0:T(8,128)(2,1)S(1)}, u32[]{:S(2)}, u32[]{:S(2)}) collective-permute-start(bf16[32,1024]{1,0:T(8,128)(2,1)S(1)} %get-tuple-element.52), channel_id=1, source_target_pairs={{0,2},{2,4},{4,6},{6,8},{8,10},{10,12},{12,14},{14,16},{16,18},{18... | collective-permute-start | bytes 196616 | tf_op jit(solution)/shard_map/ppermute | solution.py:24
  16.7 1.3 collective-permute-start.1
  18.9 4.0 %collective-permute-done.1 = bf16[32,1024]{1,0:T(8,128)(2,1)S(1)} collective-permute-done((bf16[32,1024]{1,0:T(8,128)(2,1)S(1)}, bf16[32,1024]{1,0:T(8,128)(2,1)S(1)}, u32[]{:S(2)}, u32[]{:S(2)}) %collective-permute-start.1) | collective-permute-done | bytes 65568 | tf_op jit(solution)/shard_map/ppermute | solution.py:26
  22.9 3.5 %fusion.13 = f32[512,1024]{1,0:T(8,128)} fusion(bf16[512,1024]{1,0:T(8,128)(2,1)S(1)} %copy-done.3, f32[1024]{0:T(1024)S(1)} %bitcast.190, f32[1024]{0:T(1024)S(1)} %bitcast.192, f32[1024]{0:T(1024)S(1)} %bitcast.194, f32[1024]{0:T(1024)S(1)} %bitcast.196, f32[1024]{0:T(1024)S(1)} %bitcast.198, f32[1024]{0:T(1024)S(1)} %bitcast.200, f32[1024]{0:T(1024)S(1)} %bitcast.202, ...), kind=kLoop, calls=%fused_computation.55 | loop fusion | flops 13631488 | bytes 11571200 | tf_op jit(solution)/shard_map/add | solution.py:49
  26.3 8.3 %fusion.51 = (f32[1024]{0:T(1024)S(1)}, f32[1024]{0:T(1024)S(1)}, f32[1024]{0:T(1024)S(1)}, f32[1024]{0:T(1024)S(1)}, f32[1024]{0:T(1024)S(1)}, /*index=5*/f32[1...) fusion(bf16[544,1024]{1,0:T(8,128)(2,1)S(1)} %constant_dynamic-update-slic, ...), kind=kOutput, calls=%fused_computation.93 | convolution fusion | flops 2172115968 | bytes 18911232 | tf_op jit(solution)/shard_map/dot_general | solution.py:141
  34.7 1.3 collective-permute-start.2
  36.0 4.9 %collective-permute-start.3 = (bf16[32,1024]{1,0:T(8,128)(2,1)S(1)}, bf16[32,1024]{1,0:T(8,128)(2,1)S(1)}, u32[]{:S(2)}, u32[]{:S(2)}) collective-permute-start(bf16[32,1024]{1,0:T(8,128)(2,1)S(1)} %get-tuple-element.49), channel_id=1, source_target_pairs={{0,2},{2,4},{4,6},{6,8},{8,10},{10,12},{12,14},{14,16},{16,18},{18... | collective-permute-start | bytes 196616 | tf_op jit(solution)/shard_map/ppermute | solution.py:24
  41.5 1.4 collective-permute-done.3
  42.8 6.9 %fusion.42 = bf16[512,1024]{1,0:T(8,128)(2,1)} fusion(bf16[512,1024]{1,0:T(8,128)(2,1)S(1)} %get-tuple-element.74, bf16[32,1024]{1,0:T(8,128)(2,1)S(1)} %collective-permute-done.3, bf16[32,1024]{1,0:T(8,128)(2,1)S(1)} %collective-permute-done.2, f32[1024]{0:T(1024)S(1)} %bitcast.191, f32[1024]{0:T(1024)S(1)} %bitcast.193, f32[1024]{0:T(1024)S(1)} %bitcast.195, ...), kind=kLoop, calls=%fused_computation.84 | loop fusion | flops 28311552 | bytes 3314176 | tf_op jit(solution)/shard_map/convert_element_type | solution.py:162
  49.7 5.0 %collective-permute-start.4 = (bf16[16,1024]{1,0:T(8,128)(2,1)S(1)}, bf16[16,1024]{1,0:T(8,128)(2,1)S(1)}, u32[]{:S(2)}, u32[]{:S(2)}) collective-permute-start(bf16[16,1024]{1,0:T(8,128)(2,1)S(1)} %get-tuple-element.54), channel_id=1, source_target_pairs={{0,2},{2,4},{4,6},{6,8},{8,10},{10,12},{12,14},{14,16},{16,18},{18... | collective-permute-start | bytes 98312 | tf_op jit(solution)/shard_map/ppermute | solution.py:24
  54.7 1.5 collective-permute-start.5
  56.3 4.0 %collective-permute-start.28 = (f32[9,1024]{1,0:T(8,128)S(1)}, f32[9,1024]{1,0:T(8,128)S(1)}, u32[]{:S(2)}, u32[]{:S(2)}) collective-permute-start(f32[9,1024]{1,0:T(8,128)S(1)} %broadcast_multiply_fusion), channel_id=1, source_target_pairs={{0,2},{2,0},{4,6},{6,4},{8,10},{10,8},{12,14},{14,12},{16,18},{18,... | collective-permute-start | bytes 110600 | tf_op jit(solution)/shard_map/ppermute | solution.py:79
  60.2 1.5 collective-permute-done.5
  61.7 3.2 %fusion.21 = f32[512,1024]{1,0:T(8,128)} fusion(bf16[512,1024]{1,0:T(8,128)(2,1)S(1)} %convolution_convert_fusion.4, bf16[16,1024]{1,0:T(8,128)(2,1)S(1)} %collective-permute-done.5, bf16[16,1024]{1,0:T(8,128)(2,1)S(1)} %collective-permute-done.4, f32[1024]{0:T(1024)S(1)} %bitcast.184, f32[1024]{0:T(1024)S(1)} %bitcast.186, f32[1024]{0:T(1024)S(1)} %bitcast.170, ...), kind=kLoop, calls=%fused_computation.63 | loop fusion | flops 26214400 | bytes 3248128 | tf_op jit(solution)/shard_map/add | solution.py:49
  65.0 4.3 %collective-permute-start.29 = (f32[9,1024]{1,0:T(8,128)S(1)}, f32[9,1024]{1,0:T(8,128)S(1)}, u32[]{:S(2)}, u32[]{:S(2)}) collective-permute-start(f32[9,1024]{1,0:T(8,128)S(1)} %fusion.112), channel_id=1, source_target_pairs={{0,4},{2,6},{4,0},{6,2},{8,12},{10,14},{12,8},{14,10},{16,20},{18,... | collective-permute-start | bytes 110600 | tf_op jit(solution)/shard_map/ppermute | solution.py:79
  69.3 4.1 %convolution_convert_fusion = bf16[1024,1024]{1,0:T(8,128)(2,1)} fusion(bf16[512,2048]{1,0:T(8,128)(2,1)} %all-gather.3.cloned.1.call-done, f32[512,1024]{1,0:T(8,128)S(1)} %copy-done.8), kind=kOutput, calls=%fused_computation.127 | convolution fusion | flops 1079508992 | bytes 5242880 | tf_op jit(solution)/shard_map/dot_general | solution.py:147
  73.3 1.8 collective-permute-start.30
  75.2 1.5 convolution_convert_fusion.1
  77.7 2.8 %collective-permute-start.31 = (f32[9,1024]{1,0:T(8,128)S(1)}, f32[9,1024]{1,0:T(8,128)S(1)}, u32[]{:S(2)}, u32[]{:S(2)}) collective-permute-start(f32[9,1024]{1,0:T(8,128)S(1)} %add.345), channel_id=1, source_target_pairs={{0,16},{2,18},{4,20},{6,22},{8,24},{10,26},{12,28},{14,30},{16,0},... | collective-permute-start | bytes 110600 | tf_op jit(solution)/shard_map/ppermute | solution.py:79
  80.5 8.6 %fusion.67 = (f32[1024]{0:T(1024)S(1)}, f32[1024]{0:T(1024)S(1)}, f32[1024]{0:T(1024)S(1)}, f32[1024]{0:T(1024)S(1)}, f32[1024]{0:T(1024)S(1)}, /*index=5*/f32[1...) fusion(bf16[16,1024]{1,0:T(8,128)(2,1)S(1)} %collective-permute-done.5, ...), kind=kOutput, calls=%fused_computation.109 | convolution fusion | flops 2184698880 | bytes 10588160 | tf_op jit(solution)/shard_map/dot_general | solution.py:141
  90.2 1.3 collective-permute-start.6
  91.4 6.4 %collective-permute-start.7 = (bf16[16,1024]{1,0:T(8,128)(2,1)S(1)}, bf16[16,1024]{1,0:T(8,128)(2,1)S(1)}, u32[]{:S(2)}, u32[]{:S(2)}) collective-permute-start(bf16[16,1024]{1,0:T(8,128)(2,1)S(1)} %get-tuple-element.47), channel_id=1, source_target_pairs={{0,2},{2,4},{4,6},{6,8},{8,10},{10,12},{12,14},{14,16},{16,18},{18... | collective-permute-start | bytes 98312 | tf_op jit(solution)/shard_map/ppermute | solution.py:24
  98.0 3.5 %convolution_convert_fusion.2 = bf16[1024,1024]{1,0:T(8,128)(2,1)S(1)} fusion(bf16[512,2048]{1,0:T(8,128)(2,1)} %all-gather.5.cloned.1.call-done, f32[512,1024]{1,0:T(8,128)} %fusion.21), kind=kOutput, calls=%fused_computation.129 | convolution fusion | flops 1079508992 | bytes 5242880 | tf_op jit(solution)/shard_map/dot_general | solution.py:147
  101.5 2.5 %fusion.58 = bf16[512,1024]{1,0:T(8,128)(2,1)S(1)} fusion(bf16[512,1024]{1,0:T(8,128)(2,1)S(1)} %copy-done.11, bf16[512,1024]{1,0:T(8,128)(2,1)S(1)} %copy-done.2, bf16[16,1024]{1,0:T(8,128)(2,1)S(1)} %collective-permute-done.7, bf16[16,1024]{1,0:T(8,128)(2,1)S(1)} %collective-permute-done.6, f32[1024]{0:T(1024)S(1)} %bitcast.185, f32[1024]{0:T(1024)S(1)} %bitcast.187, ...), kind=kLoop, calls=%fused_computation.100 | loop fusion | flops 27787264 | bytes 3248128 | tf_op jit(solution)/shard_map/convert_element_type | solution.py:162
  104.3 2.5 %collective-permute-start.24 = (f32[14,1024]{1,0:T(8,128)S(1)}, f32[14,1024]{1,0:T(8,128)S(1)}, u32[]{:S(2)}, u32[]{:S(2)}) collective-permute-start(f32[14,1024]{1,0:T(8,128)S(1)} %pad_maximum_fusion.8), channel_id=1, source_target_pairs={{0,4},{2,6},{4,0},{6,2},{8,12},{10,14},{12,8},{14,10},{16,20},{18,... | collective-permute-start | bytes 172040 | tf_op jit(solution)/shard_map/ppermute | solution.py:79
  108.0 1.9 collective-permute-done.24
  109.9 2.6 %collective-permute-start.25 = (f32[14,1024]{1,0:T(8,128)S(1)}, f32[14,1024]{1,0:T(8,128)S(1)}, u32[]{:S(2)}, u32[]{:S(2)}) collective-permute-start(f32[14,1024]{1,0:T(8,128)S(1)} %fusion.121), channel_id=1, source_target_pairs={{0,2},{2,0},{4,6},{6,4},{8,10},{10,8},{12,14},{14,12},{16,18},{18,... | collective-permute-start | bytes 172040 | tf_op jit(solution)/shard_map/ppermute | solution.py:79
  113.7 1.8 collective-permute-done.25
  115.5 2.1 collective-permute-start.26
  117.6 1.5 convolution_convert_fusion.3
  119.9 1.4 collective-permute-start.27
  122.9 1.3 collective-permute-start.16
  126.5 7.4 %collective-permute-done.12 = bf16[2,2,2,64,1024]{4,3,0,1,2:T(8,128)(2,1)S(1)} collective-permute-done((bf16[2,2,2,64,1024]{4,3,0,1,2:T(8,128)(2,1)S(1)}, bf16[2,2,2,64,1024]{4,3,0,1,2:T(8,128)(2,1)S(1)}, u32[]{:S(2)}, u32[]{:S(2)}) %collective-permute-start.12) | collective-permute-done | bytes 1048608 | tf_op jit(solution)/shard_map/ppermute | solution.py:79
  134.3 1.6 collective-permute-start.13
  135.9 13.3 %collective-permute-done.20 = bf16[2,2,2,64,1024]{4,3,0,1,2:T(8,128)(2,1)S(1)} collective-permute-done((bf16[2,2,2,64,1024]{4,3,0,1,2:T(8,128)(2,1)S(1)}, bf16[2,2,2,64,1024]{4,3,0,1,2:T(8,128)(2,1)S(1)}, u32[]{:S(2)}, u32[]{:S(2)}) %collective-permute-start.20) | collective-permute-done | bytes 1048608 | tf_op jit(solution)/shard_map/ppermute | solution.py:79
  149.7 4.8 %collective-permute-start.21 = (bf16[2,2,64,1024]{3,2,0,1:T(8,128)(2,1)S(1)}, bf16[2,2,64,1024]{3,2,0,1:T(8,128)(2,1)S(1)}, u32[]{:S(2)}, u32[]{:S(2)}) collective-permute-start(bf16[2,2,64,1024]{3,2,0,1:T(8,128)(2,1)S(1)} %dynamic-slice_bitcast_fusion), channel_id=1, source_target_pairs={{0,2},{2,0},{4,6},{6,4},{8,10},{10,8},{12,14},{14,12},{16,18},{18,... | collective-permute-start | bytes 1572872 | tf_op jit(solution)/shard_map/ppermute | solution.py:79
  156.0 13.4 %collective-permute-done.16 = bf16[2,2,2,64,1024]{4,3,0,1,2:T(8,128)(2,1)S(1)} collective-permute-done((bf16[2,2,2,64,1024]{4,3,0,1,2:T(8,128)(2,1)S(1)}, bf16[2,2,2,64,1024]{4,3,0,1,2:T(8,128)(2,1)S(1)}, u32[]{:S(2)}, u32[]{:S(2)}) %collective-permute-start.16) | collective-permute-done | bytes 1048608 | tf_op jit(solution)/shard_map/ppermute | solution.py:79
  170.8 4.2 %collective-permute-done.13 = bf16[2,2,64,1024]{3,2,0,1:T(8,128)(2,1)S(1)} collective-permute-done((bf16[2,2,64,1024]{3,2,0,1:T(8,128)(2,1)S(1)}, bf16[2,2,64,1024]{3,2,0,1:T(8,128)(2,1)S(1)}, u32[]{:S(2)}, u32[]{:S(2)}) %collective-permute-start.13) | collective-permute-done | bytes 524320 | tf_op jit(solution)/shard_map/ppermute | solution.py:79
  176.4 4.2 %collective-permute-done.21 = bf16[2,2,64,1024]{3,2,0,1:T(8,128)(2,1)S(1)} collective-permute-done((bf16[2,2,64,1024]{3,2,0,1:T(8,128)(2,1)S(1)}, bf16[2,2,64,1024]{3,2,0,1:T(8,128)(2,1)S(1)}, u32[]{:S(2)}, u32[]{:S(2)}) %collective-permute-start.21) | collective-permute-done | bytes 524320 | tf_op jit(solution)/shard_map/ppermute | solution.py:79
  184.7 1.8 collective-permute-done.14
  187.1 2.1 collective-permute-done.22
  189.3 3.4 %collective-permute-start.23 = (bf16[64,1024]{1,0:T(8,128)(2,1)S(1)}, bf16[64,1024]{1,0:T(8,128)(2,1)S(1)}, u32[]{:S(2)}, u32[]{:S(2)}) collective-permute-start(bf16[64,1024]{1,0:T(8,128)(2,1)S(1)} %dynamic-slice_bitcast_fusion.8), channel_id=1, source_target_pairs={{0,16},{2,18},{4,20},{6,22},{8,24},{10,26},{12,28},{14,30},{16,0},... | collective-permute-start | bytes 393224 | tf_op jit(solution)/shard_map/ppermute | solution.py:79
  192.8 1.5 collective-permute-done.10
  194.3 3.2 %collective-permute-start.11 = (bf16[64,1024]{1,0:T(8,128)(2,1)S(1)}, bf16[64,1024]{1,0:T(8,128)(2,1)S(1)}, u32[]{:S(2)}, u32[]{:S(2)}) collective-permute-start(bf16[64,1024]{1,0:T(8,128)(2,1)S(1)} %dynamic-slice_bitcast_fusion.11), channel_id=1, source_target_pairs={{0,16},{2,18},{4,20},{6,22},{8,24},{10,26},{12,28},{14,30},{16,0},... | collective-permute-start | bytes 393224 | tf_op jit(solution)/shard_map/ppermute | solution.py:79
  197.5 1.6 collective-permute-done.18
  200.3 5.6 %collective-permute-done.11 = bf16[64,1024]{1,0:T(8,128)(2,1)S(1)} collective-permute-done((bf16[64,1024]{1,0:T(8,128)(2,1)S(1)}, bf16[64,1024]{1,0:T(8,128)(2,1)S(1)}, u32[]{:S(2)}, u32[]{:S(2)}) %collective-permute-start.11) | collective-permute-done | bytes 131104 | tf_op jit(solution)/shard_map/ppermute | solution.py:79
  (133 shorter events, 25.5 us)
Async XLA Ops:
  7.2 33.8 %copy-start = (bf16[5,1024]{1,0:T(8,128)(2,1)S(1)}, bf16[5,1024]{1,0:T(8,128)(2,1)}, u32[]{:S(2)}) copy-start(bf16[5,1024]{1,0:T(8,128)(2,1)} %param.11) | copy-start | bytes 30724
  7.2 4.6 %copy-start.3 = (bf16[512,1024]{1,0:T(8,128)(2,1)S(1)}, bf16[512,1024]{1,0:T(8,128)(2,1)}, u32[]{:S(2)}) copy-start(bf16[512,1024]{1,0:T(8,128)(2,1)} %param.14) | copy-start | bytes 3145732
  7.2 10.8 %copy-start.12 = (bf16[2,9,1024]{2,0,1:T(2,128)(2,1)S(1)}, bf16[2,9,1024]{2,0,1:T(2,128)(2,1)}, u32[]{:S(2)}) copy-start(bf16[2,9,1024]{2,0,1:T(2,128)(2,1)} %param.12) | copy-start | bytes 110596
  7.2 10.9 %copy-start.13 = (s32[512]{0:T(512)S(1)}, s32[512]{0:T(512)}, u32[]{:S(2)}) copy-start(s32[512]{0:T(512)} %param.8) | copy-start | bytes 6148
  7.2 19.1 %all-gather.3.cloned.1.call-start = ((), (), s32[]{:S(2)}) async-start(), calls=%async_computation | async-start | bytes 3145728 | tf_op jit(solution)/shard_map/all_gather | solution.py:140
  11.8 68.8 %all-gather.5.cloned.1.call-start = ((), (), s32[]{:S(2)}) async-start(), calls=%async_computation.1 | async-start | bytes 3145728 | tf_op jit(solution)/shard_map/all_gather | solution.py:140
  11.8 6.7 %collective-permute-start = (bf16[32,1024]{1,0:T(8,128)(2,1)S(1)}, bf16[32,1024]{1,0:T(8,128)(2,1)S(1)}, u32[]{:S(2)}, u32[]{:S(2)}) collective-permute-start(bf16[32,1024]{1,0:T(8,128)(2,1)S(1)} %get-tuple-element.52), channel_id=1, source_target_pairs={{0,2},{2,4},{4,6},{6,8},{8,10},{10,12},{12,14},{14,16},{16,18},{18... | collective-permute-start | bytes 196616 | tf_op jit(solution)/shard_map/ppermute | solution.py:24
  16.7 6.2 %collective-permute-start.1 = (bf16[32,1024]{1,0:T(8,128)(2,1)S(1)}, bf16[32,1024]{1,0:T(8,128)(2,1)S(1)}, u32[]{:S(2)}, u32[]{:S(2)}) collective-permute-start(bf16[32,1024]{1,0:T(8,128)(2,1)S(1)} %get-tuple-element.53), channel_id=1, source_target_pairs={{2,0},{4,2},{6,4},{8,6},{10,8},{12,10},{14,12},{16,14},{18,16},{20... | collective-permute-start | bytes 196616 | tf_op jit(solution)/shard_map/ppermute | solution.py:26
  26.3 16.5 %copy-start.5 = (bf16[512,1024]{1,0:T(8,128)(2,1)S(1)}, bf16[512,1024]{1,0:T(8,128)(2,1)}, u32[]{:S(2)}) copy-start(bf16[512,1024]{1,0:T(8,128)(2,1)} %param.15) | copy-start | bytes 3145732
  34.7 6.8 %collective-permute-start.2 = (bf16[32,1024]{1,0:T(8,128)(2,1)S(1)}, bf16[32,1024]{1,0:T(8,128)(2,1)S(1)}, u32[]{:S(2)}, u32[]{:S(2)}) collective-permute-start(bf16[32,1024]{1,0:T(8,128)(2,1)S(1)} %get-tuple-element.48), channel_id=1, source_target_pairs={{2,0},{4,2},{6,4},{8,6},{10,8},{12,10},{14,12},{16,14},{18,16},{20... | collective-permute-start | bytes 196616 | tf_op jit(solution)/shard_map/ppermute | solution.py:26
  36.0 6.8 %collective-permute-start.3 = (bf16[32,1024]{1,0:T(8,128)(2,1)S(1)}, bf16[32,1024]{1,0:T(8,128)(2,1)S(1)}, u32[]{:S(2)}, u32[]{:S(2)}) collective-permute-start(bf16[32,1024]{1,0:T(8,128)(2,1)S(1)} %get-tuple-element.49), channel_id=1, source_target_pairs={{0,2},{2,4},{4,6},{6,8},{8,10},{10,12},{12,14},{14,16},{16,18},{18... | collective-permute-start | bytes 196616 | tf_op jit(solution)/shard_map/ppermute | solution.py:24
  49.7 19.6 %copy-start.8 = (f32[512,1024]{1,0:T(8,128)S(1)}, f32[512,1024]{1,0:T(8,128)}, u32[]{:S(2)}) copy-start(f32[512,1024]{1,0:T(8,128)} %fusion.13) | copy-start | bytes 6291460
  49.7 10.5 %collective-permute-start.4 = (bf16[16,1024]{1,0:T(8,128)(2,1)S(1)}, bf16[16,1024]{1,0:T(8,128)(2,1)S(1)}, u32[]{:S(2)}, u32[]{:S(2)}) collective-permute-start(bf16[16,1024]{1,0:T(8,128)(2,1)S(1)} %get-tuple-element.54), channel_id=1, source_target_pairs={{0,2},{2,4},{4,6},{6,8},{8,10},{10,12},{12,14},{14,16},{16,18},{18... | collective-permute-start | bytes 98312 | tf_op jit(solution)/shard_map/ppermute | solution.py:24
  54.7 7.1 %collective-permute-start.5 = (bf16[16,1024]{1,0:T(8,128)(2,1)S(1)}, bf16[16,1024]{1,0:T(8,128)(2,1)S(1)}, u32[]{:S(2)}, u32[]{:S(2)}) collective-permute-start(bf16[16,1024]{1,0:T(8,128)(2,1)S(1)} %get-tuple-element.55), channel_id=1, source_target_pairs={{2,0},{4,2},{6,4},{8,6},{10,8},{12,10},{14,12},{16,14},{18,16},{20... | collective-permute-start | bytes 98312 | tf_op jit(solution)/shard_map/ppermute | solution.py:26
  56.3 8.7 %collective-permute-start.28 = (f32[9,1024]{1,0:T(8,128)S(1)}, f32[9,1024]{1,0:T(8,128)S(1)}, u32[]{:S(2)}, u32[]{:S(2)}) collective-permute-start(f32[9,1024]{1,0:T(8,128)S(1)} %broadcast_multiply_fusion), channel_id=1, source_target_pairs={{0,2},{2,0},{4,6},{6,4},{8,10},{10,8},{12,14},{14,12},{16,18},{18,... | collective-permute-start | bytes 110600 | tf_op jit(solution)/shard_map/ppermute | solution.py:79
  65.0 10.2 %copy-start.9 = (f32[512,1024]{1,0:T(8,128)S(1)}, f32[512,1024]{1,0:T(8,128)}, u32[]{:S(2)}) copy-start(f32[512,1024]{1,0:T(8,128)} %fusion.13) | copy-start | bytes 6291460
  65.0 10.2 %copy-start.15 = (bf16[512,2048]{1,0:T(8,128)(2,1)S(1)}, bf16[512,2048]{1,0:T(8,128)(2,1)}, u32[]{:S(2)}) copy-start(bf16[512,2048]{1,0:T(8,128)(2,1)} %all-gather.3.cloned.1.call-done) | copy-start | bytes 6291460
  65.0 8.3 %collective-permute-start.29 = (f32[9,1024]{1,0:T(8,128)S(1)}, f32[9,1024]{1,0:T(8,128)S(1)}, u32[]{:S(2)}, u32[]{:S(2)}) collective-permute-start(f32[9,1024]{1,0:T(8,128)S(1)} %fusion.112), channel_id=1, source_target_pairs={{0,4},{2,6},{4,0},{6,2},{8,12},{10,14},{12,8},{14,10},{16,20},{18,... | collective-permute-start | bytes 110600 | tf_op jit(solution)/shard_map/ppermute | solution.py:79
  73.3 4.3 %collective-permute-start.30 = (f32[9,1024]{1,0:T(8,128)S(1)}, f32[9,1024]{1,0:T(8,128)S(1)}, u32[]{:S(2)}, u32[]{:S(2)}) collective-permute-start(f32[9,1024]{1,0:T(8,128)S(1)} %add.344), channel_id=1, source_target_pairs={{0,8},{2,10},{4,12},{6,14},{8,0},{10,2},{12,4},{14,6},{16,24},{18,... | collective-permute-start | bytes 110600 | tf_op jit(solution)/shard_map/ppermute | solution.py:79
  77.7 34.8 %collective-permute-start.31 = (f32[9,1024]{1,0:T(8,128)S(1)}, f32[9,1024]{1,0:T(8,128)S(1)}, u32[]{:S(2)}, u32[]{:S(2)}) collective-permute-start(f32[9,1024]{1,0:T(8,128)S(1)} %add.345), channel_id=1, source_target_pairs={{0,16},{2,18},{4,20},{6,22},{8,24},{10,26},{12,28},{14,30},{16,0},... | collective-permute-start | bytes 110600 | tf_op jit(solution)/shard_map/ppermute | solution.py:79
  90.2 11.4 %collective-permute-start.6 = (bf16[16,1024]{1,0:T(8,128)(2,1)S(1)}, bf16[16,1024]{1,0:T(8,128)(2,1)S(1)}, u32[]{:S(2)}, u32[]{:S(2)}) collective-permute-start(bf16[16,1024]{1,0:T(8,128)(2,1)S(1)} %get-tuple-element.46), channel_id=1, source_target_pairs={{2,0},{4,2},{6,4},{8,6},{10,8},{12,10},{14,12},{16,14},{18,16},{20... | collective-permute-start | bytes 98312 | tf_op jit(solution)/shard_map/ppermute | solution.py:26
  91.4 10.1 %collective-permute-start.7 = (bf16[16,1024]{1,0:T(8,128)(2,1)S(1)}, bf16[16,1024]{1,0:T(8,128)(2,1)S(1)}, u32[]{:S(2)}, u32[]{:S(2)}) collective-permute-start(bf16[16,1024]{1,0:T(8,128)(2,1)S(1)} %get-tuple-element.47), channel_id=1, source_target_pairs={{0,2},{2,4},{4,6},{6,8},{8,10},{10,12},{12,14},{14,16},{16,18},{18... | collective-permute-start | bytes 98312 | tf_op jit(solution)/shard_map/ppermute | solution.py:24
  98.0 3.6 %copy-start.2 = (bf16[512,1024]{1,0:T(8,128)(2,1)S(1)}, bf16[512,1024]{1,0:T(8,128)(2,1)}, u32[]{:S(2)}) copy-start(bf16[512,1024]{1,0:T(8,128)(2,1)} %fusion.42) | copy-start | bytes 3145732
  98.0 3.6 %copy-start.11 = (bf16[512,1024]{1,0:T(8,128)(2,1)S(1)}, bf16[512,1024]{1,0:T(8,128)(2,1)}, u32[]{:S(2)}) copy-start(bf16[512,1024]{1,0:T(8,128)(2,1)} %copy-done.10) | copy-start | bytes 3145732
  101.5 5.4 %copy-start.6 = (bf16[1024,1024]{1,0:T(8,128)(2,1)S(1)}, bf16[1024,1024]{1,0:T(8,128)(2,1)}, u32[]{:S(2)}) copy-start(bf16[1024,1024]{1,0:T(8,128)(2,1)} %convolution_convert_fusion) | copy-start | bytes 6291460
  104.1 3.5 %copy-start.4 = (bf16[512,1024]{1,0:T(8,128)(2,1)}, bf16[512,1024]{1,0:T(8,128)(2,1)S(1)}, u32[]{:S(2)}) copy-start(bf16[512,1024]{1,0:T(8,128)(2,1)S(1)} %fusion.58) | copy-start | bytes 3145732
  104.3 5.5 %collective-permute-start.24 = (f32[14,1024]{1,0:T(8,128)S(1)}, f32[14,1024]{1,0:T(8,128)S(1)}, u32[]{:S(2)}, u32[]{:S(2)}) collective-permute-start(f32[14,1024]{1,0:T(8,128)S(1)} %pad_maximum_fusion.8), channel_id=1, source_target_pairs={{0,4},{2,6},{4,0},{6,2},{8,12},{10,14},{12,8},{14,10},{16,20},{18,... | collective-permute-start | bytes 172040 | tf_op jit(solution)/shard_map/ppermute | solution.py:79
  107.6 10.0 %copy-start.7 = (f32[512,1024]{1,0:T(8,128)S(1)}, f32[512,1024]{1,0:T(8,128)}, u32[]{:S(2)}) copy-start(f32[512,1024]{1,0:T(8,128)} %fusion.21) | copy-start | bytes 6291460
  107.6 10.0 %copy-start.14 = (bf16[512,2048]{1,0:T(8,128)(2,1)S(1)}, bf16[512,2048]{1,0:T(8,128)(2,1)}, u32[]{:S(2)}) copy-start(bf16[512,2048]{1,0:T(8,128)(2,1)} %all-gather.5.cloned.1.call-done) | copy-start | bytes 6291460
  107.7 26.2 %collective-permute-start.12 = (bf16[2,2,2,64,1024]{4,3,0,1,2:T(8,128)(2,1)S(1)}, bf16[2,2,2,64,1024]{4,3,0,1,2:T(8,128)(2,1)S(1)}, u32[]{:S(2)}, u32[]{:S(2)}) collective-permute-start(bf16[2,2,2,64,1024]{4,3,0,1,2:T(8,128)(2,1)S(1)} %bitcast.166), channel_id=1, source_target_pairs={{0,4},{2,6},{4,0},{6,2},{8,12},{10,14},{12,8},{14,10},{16,20},{18,... | collective-permute-start | bytes 3145736 | tf_op jit(solution)/shard_map/ppermute | solution.py:79
  109.9 5.6 %collective-permute-start.25 = (f32[14,1024]{1,0:T(8,128)S(1)}, f32[14,1024]{1,0:T(8,128)S(1)}, u32[]{:S(2)}, u32[]{:S(2)}) collective-permute-start(f32[14,1024]{1,0:T(8,128)S(1)} %fusion.121), channel_id=1, source_target_pairs={{0,2},{2,0},{4,6},{6,4},{8,10},{10,8},{12,14},{14,12},{16,18},{18,... | collective-permute-start | bytes 172040 | tf_op jit(solution)/shard_map/ppermute | solution.py:79
  112.5 36.7 %collective-permute-start.20 = (bf16[2,2,2,64,1024]{4,3,0,1,2:T(8,128)(2,1)S(1)}, bf16[2,2,2,64,1024]{4,3,0,1,2:T(8,128)(2,1)S(1)}, u32[]{:S(2)}, u32[]{:S(2)}) collective-permute-start(bf16[2,2,2,64,1024]{4,3,0,1,2:T(8,128)(2,1)S(1)} %bitcast.167), channel_id=1, source_target_pairs={{0,4},{2,6},{4,0},{6,2},{8,12},{10,14},{12,8},{14,10},{16,20},{18,... | collective-permute-start | bytes 3145736 | tf_op jit(solution)/shard_map/ppermute | solution.py:79
  115.5 4.4 %collective-permute-start.26 = (f32[14,1024]{1,0:T(8,128)S(1)}, f32[14,1024]{1,0:T(8,128)S(1)}, u32[]{:S(2)}, u32[]{:S(2)}) collective-permute-start(f32[14,1024]{1,0:T(8,128)S(1)} %add.340), channel_id=1, source_target_pairs={{0,8},{2,10},{4,12},{6,14},{8,0},{10,2},{12,4},{14,6},{16,24},{18,... | collective-permute-start | bytes 172040 | tf_op jit(solution)/shard_map/ppermute | solution.py:79
  119.9 5.2 %collective-permute-start.27 = (f32[14,1024]{1,0:T(8,128)S(1)}, f32[14,1024]{1,0:T(8,128)S(1)}, u32[]{:S(2)}, u32[]{:S(2)}) collective-permute-start(f32[14,1024]{1,0:T(8,128)S(1)} %add.341), channel_id=1, source_target_pairs={{0,16},{2,18},{4,20},{6,22},{8,24},{10,26},{12,28},{14,30},{16,0},... | collective-permute-start | bytes 172040 | tf_op jit(solution)/shard_map/ppermute | solution.py:79
  122.2 32.4 %collective-permute-start.8 = (bf16[2,2,2,64,1024]{4,3,0,1,2:T(8,128)(2,1)S(1)}, bf16[2,2,2,64,1024]{4,3,0,1,2:T(8,128)(2,1)S(1)}, u32[]{:S(2)}, u32[]{:S(2)}) collective-permute-start(bf16[2,2,2,64,1024]{4,3,0,1,2:T(8,128)(2,1)S(1)} %bitcast.169), channel_id=1, source_target_pairs={{0,2},{2,0},{4,6},{6,4},{8,10},{10,8},{12,14},{14,12},{16,18},{18,... | collective-permute-start | bytes 3145736 | tf_op jit(solution)/shard_map/ppermute | solution.py:79
  122.9 46.4 %collective-permute-start.16 = (bf16[2,2,2,64,1024]{4,3,0,1,2:T(8,128)(2,1)S(1)}, bf16[2,2,2,64,1024]{4,3,0,1,2:T(8,128)(2,1)S(1)}, u32[]{:S(2)}, u32[]{:S(2)}) collective-permute-start(bf16[2,2,2,64,1024]{4,3,0,1,2:T(8,128)(2,1)S(1)} %bitcast.168), channel_id=1, source_target_pairs={{0,2},{2,0},{4,6},{6,4},{8,10},{10,8},{12,14},{14,12},{16,18},{18,... | collective-permute-start | bytes 3145736 | tf_op jit(solution)/shard_map/ppermute | solution.py:79
  134.3 40.7 %collective-permute-start.13 = (bf16[2,2,64,1024]{3,2,0,1:T(8,128)(2,1)S(1)}, bf16[2,2,64,1024]{3,2,0,1:T(8,128)(2,1)S(1)}, u32[]{:S(2)}, u32[]{:S(2)}) collective-permute-start(bf16[2,2,64,1024]{3,2,0,1:T(8,128)(2,1)S(1)} %dynamic-slice_bitcast_fusion.2), channel_id=1, source_target_pairs={{0,2},{2,0},{4,6},{6,4},{8,10},{10,8},{12,14},{14,12},{16,18},{18,... | collective-permute-start | bytes 1572872 | tf_op jit(solution)/shard_map/ppermute | solution.py:79
  149.7 30.9 %collective-permute-start.21 = (bf16[2,2,64,1024]{3,2,0,1:T(8,128)(2,1)S(1)}, bf16[2,2,64,1024]{3,2,0,1:T(8,128)(2,1)S(1)}, u32[]{:S(2)}, u32[]{:S(2)}) collective-permute-start(bf16[2,2,64,1024]{3,2,0,1:T(8,128)(2,1)S(1)} %dynamic-slice_bitcast_fusion), channel_id=1, source_target_pairs={{0,2},{2,0},{4,6},{6,4},{8,10},{10,8},{12,14},{14,12},{16,18},{18,... | collective-permute-start | bytes 1572872 | tf_op jit(solution)/shard_map/ppermute | solution.py:79
  155.0 27.0 %collective-permute-start.9 = (bf16[2,2,64,1024]{3,2,0,1:T(8,128)(2,1)S(1)}, bf16[2,2,64,1024]{3,2,0,1:T(8,128)(2,1)S(1)}, u32[]{:S(2)}, u32[]{:S(2)}) collective-permute-start(bf16[2,2,64,1024]{3,2,0,1:T(8,128)(2,1)S(1)} %dynamic-slice_bitcast_fusion.3), channel_id=1, source_target_pairs={{0,4},{2,6},{4,0},{6,2},{8,12},{10,14},{12,8},{14,10},{16,20},{18,... | collective-permute-start | bytes 1572872 | tf_op jit(solution)/shard_map/ppermute | solution.py:79
  169.8 13.4 %collective-permute-start.17 = (bf16[2,2,64,1024]{3,2,0,1:T(8,128)(2,1)S(1)}, bf16[2,2,64,1024]{3,2,0,1:T(8,128)(2,1)S(1)}, u32[]{:S(2)}, u32[]{:S(2)}) collective-permute-start(bf16[2,2,64,1024]{3,2,0,1:T(8,128)(2,1)S(1)} %dynamic-slice_bitcast_fusion.1), channel_id=1, source_target_pairs={{0,4},{2,6},{4,0},{6,2},{8,12},{10,14},{12,8},{14,10},{16,20},{18,... | collective-permute-start | bytes 1572872 | tf_op jit(solution)/shard_map/ppermute | solution.py:79
  175.2 11.2 %collective-permute-start.14 = (bf16[2,64,1024]{2,1,0:T(8,128)(2,1)S(1)}, bf16[2,64,1024]{2,1,0:T(8,128)(2,1)S(1)}, u32[]{:S(2)}, u32[]{:S(2)}) collective-permute-start(bf16[2,64,1024]{2,1,0:T(8,128)(2,1)S(1)} %dynamic-slice_bitcast_fusion.6), channel_id=1, source_target_pairs={{0,8},{2,10},{4,12},{6,14},{8,0},{10,2},{12,4},{14,6},{16,24},{18,... | collective-permute-start | bytes 786440 | tf_op jit(solution)/shard_map/ppermute | solution.py:79
  180.9 8.4 %collective-permute-start.22 = (bf16[2,64,1024]{2,1,0:T(8,128)(2,1)S(1)}, bf16[2,64,1024]{2,1,0:T(8,128)(2,1)S(1)}, u32[]{:S(2)}, u32[]{:S(2)}) collective-permute-start(bf16[2,64,1024]{2,1,0:T(8,128)(2,1)S(1)} %dynamic-slice_bitcast_fusion.4), channel_id=1, source_target_pairs={{0,8},{2,10},{4,12},{6,14},{8,0},{10,2},{12,4},{14,6},{16,24},{18,... | collective-permute-start | bytes 786440 | tf_op jit(solution)/shard_map/ppermute | solution.py:79
  182.3 12.0 %collective-permute-start.10 = (bf16[2,64,1024]{2,1,0:T(8,128)(2,1)S(1)}, bf16[2,64,1024]{2,1,0:T(8,128)(2,1)S(1)}, u32[]{:S(2)}, u32[]{:S(2)}) collective-permute-start(bf16[2,64,1024]{2,1,0:T(8,128)(2,1)S(1)} %dynamic-slice_bitcast_fusion.7), channel_id=1, source_target_pairs={{0,8},{2,10},{4,12},{6,14},{8,0},{10,2},{12,4},{14,6},{16,24},{18,... | collective-permute-start | bytes 786440 | tf_op jit(solution)/shard_map/ppermute | solution.py:79
  183.5 15.6 %collective-permute-start.18 = (bf16[2,64,1024]{2,1,0:T(8,128)(2,1)S(1)}, bf16[2,64,1024]{2,1,0:T(8,128)(2,1)S(1)}, u32[]{:S(2)}, u32[]{:S(2)}) collective-permute-start(bf16[2,64,1024]{2,1,0:T(8,128)(2,1)S(1)} %dynamic-slice_bitcast_fusion.5), channel_id=1, source_target_pairs={{0,8},{2,10},{4,12},{6,14},{8,0},{10,2},{12,4},{14,6},{16,24},{18,... | collective-permute-start | bytes 786440 | tf_op jit(solution)/shard_map/ppermute | solution.py:79
  186.5 13.8 %collective-permute-start.15 = (bf16[64,1024]{1,0:T(8,128)(2,1)S(1)}, bf16[64,1024]{1,0:T(8,128)(2,1)S(1)}, u32[]{:S(2)}, u32[]{:S(2)}) collective-permute-start(bf16[64,1024]{1,0:T(8,128)(2,1)S(1)} %dynamic-slice_bitcast_fusion.10), channel_id=1, source_target_pairs={{0,16},{2,18},{4,20},{6,22},{8,24},{10,26},{12,28},{14,30},{16,0},... | collective-permute-start | bytes 393224 | tf_op jit(solution)/shard_map/ppermute | solution.py:79
  189.3 16.7 %collective-permute-start.23 = (bf16[64,1024]{1,0:T(8,128)(2,1)S(1)}, bf16[64,1024]{1,0:T(8,128)(2,1)S(1)}, u32[]{:S(2)}, u32[]{:S(2)}) collective-permute-start(bf16[64,1024]{1,0:T(8,128)(2,1)S(1)} %dynamic-slice_bitcast_fusion.8), channel_id=1, source_target_pairs={{0,16},{2,18},{4,20},{6,22},{8,24},{10,26},{12,28},{14,30},{16,0},... | collective-permute-start | bytes 393224 | tf_op jit(solution)/shard_map/ppermute | solution.py:79
  194.3 11.6 %collective-permute-start.11 = (bf16[64,1024]{1,0:T(8,128)(2,1)S(1)}, bf16[64,1024]{1,0:T(8,128)(2,1)S(1)}, u32[]{:S(2)}, u32[]{:S(2)}) collective-permute-start(bf16[64,1024]{1,0:T(8,128)(2,1)S(1)} %dynamic-slice_bitcast_fusion.11), channel_id=1, source_target_pairs={{0,16},{2,18},{4,20},{6,22},{8,24},{10,26},{12,28},{14,30},{16,0},... | collective-permute-start | bytes 393224 | tf_op jit(solution)/shard_map/ppermute | solution.py:79
  199.2 8.2 %collective-permute-start.19 = (bf16[64,1024]{1,0:T(8,128)(2,1)S(1)}, bf16[64,1024]{1,0:T(8,128)(2,1)S(1)}, u32[]{:S(2)}, u32[]{:S(2)}) collective-permute-start(bf16[64,1024]{1,0:T(8,128)(2,1)S(1)} %dynamic-slice_bitcast_fusion.9), channel_id=1, source_target_pairs={{0,16},{2,18},{4,20},{6,22},{8,24},{10,26},{12,28},{14,30},{16,0},... | collective-permute-start | bytes 393224 | tf_op jit(solution)/shard_map/ppermute | solution.py:79
  (2 other events, 3.5 us)
Sparse Core Ops, SparseCore 0:
  11.9 13.2 all-gather.2
  49.8 15.8 all-gather.4

commit v2 on v0

--- a/solution.py
+++ b/solution.py
@@ -30,6 +30,21 @@
     return cells
 
 
+def padded_together(arrays, widths):
+    count = lax.axis_size("seq")
+    ends = count - 1
+    heads = jnp.concatenate([cells[:width] for cells, width in zip(arrays, widths)])
+    tails = jnp.concatenate([cells[-width:] for cells, width in zip(arrays, widths)])
+    before = lax.ppermute(tails, "seq", [(i, (i + 1) % count) for i in range(ends)])
+    after = lax.ppermute(heads, "seq", [((i + 1) % count, i) for i in range(ends)])
+    padded, first = [], 0
+    for cells, width in zip(arrays, widths):
+        rows = slice(first, first + width)
+        padded.append(jnp.concatenate([before[rows], cells, after[rows]]))
+        first += width
+    return padded
+
+
 def gelu_pair(pre_act):
     inner_arg = gelu_scale * (pre_act + gelu_cubic * pre_act * pre_act * pre_act)
     tangent = jnp.tanh(inner_arg)
@@ -72,6 +87,53 @@
     return jnp.einsum("vt,vc->tc", hot_rows, table_rows, preferred_element_type=jnp.float32).astype(
         jnp.bfloat16
     )
+
+
+def exchanged(cells, axis, bit):
+    count = lax.axis_size(axis)
+    return lax.ppermute(cells, axis, [(i, i ^ (1 << bit)) for i in range(count)])
+
+
+def split_rows(part, bits):
+    return part.reshape((2,) * bits + (part.shape[0] >> bits, part.shape[1]))
+
+
+def halving_step(part, order, step):
+    bit = order[step]
+    dim = sorted(order[step:], reverse=True).index(bit)
+    mine = (lax.axis_index("seq") >> bit) & 1
+    send = lax.dynamic_index_in_dim(part, 1 - mine, dim, keepdims=False)
+    keep = lax.dynamic_index_in_dim(part, mine, dim, keepdims=False)
+    return (keep, exchanged(send, "seq", bit))
+
+
+def added(keep, arrived, last):
+    total = keep.astype(jnp.float32) + arrived.astype(jnp.float32)
+    return total if last else total.astype(jnp.bfloat16)
+
+
+def halving_steps(parts, orders, steps):
+    pairs = None
+    for step in steps:
+        if pairs is not None:
+            parts = [added(keep, arrived, False) for keep, arrived in pairs]
+        pairs = [halving_step(part, order, step) for part, order in zip(parts, orders)]
+    return pairs
+
+
+def finished(pairs, scale):
+    return jnp.concatenate([added(keep, arrived, True) for keep, arrived in pairs], axis=1) * scale
+
+
+def tied(value, pairs):
+    value, pairs = lax.optimization_barrier((value, pairs))
+    return (value, pairs)
+
+
+def doubled_sum(part, order):
+    for bit in order:
+        part = part + exchanged(part, "seq", bit)
+    return part
 
 
 def on_device(
@@ -90,48 +152,75 @@
     masked_ids = jnp.where(covered, mask_token, base_ids)
     vocab_ids = jnp.arange(vocab_rows, dtype=jnp.int32)
     one_hot = (vocab_ids[:, None] == masked_ids[None, :]).astype(jnp.bfloat16)
-    initial_reach = taps_per_side * BASE_DILATION
+    bits = (lax.axis_size("seq") - 1).bit_length()
+    orders = (tuple(range(bits)), (1, 0) + tuple(range(2, bits)))
     first_input = lookup(one_hot, embedding)
-    first_padded = extended(first_input, (("seq", 0),), initial_reach)
+    steps = len(orders[0])
+    halo_rows = [taps_per_side * BASE_DILATION * 2**number for number in range(block_count)]
+    padded_inputs = padded_together((first_input, saved_input), halo_rows)
     upstream = jnp.where(covered[:, None], cotangent, jnp.zeros_like(cotangent))
     weight_parts = [None] * block_count
     kernel_parts = [None] * block_count
+    earlier = None
     for block_number in range(block_count - 1, -1, -1):
         tap_spacing = BASE_DILATION * 2**block_number
-        reach_rows = taps_per_side * tap_spacing
-        if block_number == 0:
-            padded_in = first_padded
-        else:
-            padded_in = extended(saved_input, (("seq", 0),), reach_rows)
+        padded_in = padded_inputs[block_number]
         kernel = conv_kernel[block_number]
-        weight_rows = mix_weight[block_number]
+        column_piece = lax.all_gather(upstream, "blk", axis=1, tiled=True)
         pre_act = tap_sum(padded_in, kernel, tap_spacing, row_count, False)
         activation, derivative = gelu_pair(pre_act)
         act_half = activation.astype(jnp.bfloat16)
-        column_piece = lax.all_gather(upstream, "blk", axis=1, tiled=True)
+        if earlier is not None:
+            parts = [added(keep, arrived, False) for keep, arrived in earlier]
+            pairs = halving_steps(parts, orders, range(1, 2))
+            column_piece, earlier = tied(column_piece, pairs)
+        width = column_piece.shape[1] // len(orders)
+        parts = [
+            lax.dot_general(
+                act_half,
+                lax.slice_in_dim(column_piece, chunk * width, (chunk + 1) * width, axis=1),
+                (((0,), (0,)), ((), ())),
+                preferred_element_type=jnp.float32,
+            ).astype(jnp.bfloat16)
+            for chunk in range(len(orders))
+        ]
+        column_piece, parts = lax.optimization_barrier((column_piece, parts))
+        parts = [split_rows(part, steps) for part in parts]
+        pairs = halving_steps(parts, orders, range(0, 1))
+        if earlier is not None:
+            parts = [added(keep, arrived, False) for keep, arrived in earlier]
+            earlier = halving_steps(parts, orders, range(2, 3))
         grad_held = lax.dot_general(
-            column_piece, weight_rows, (((1,), (1,)), ((), ())), preferred_element_type=jnp.float32
-        )
-        block_part = lax.dot_general(
-            act_half, column_piece, (((0,), (0,)), ((), ())), preferred_element_type=jnp.float32
-        )
-        weight_part = block_part
+            column_piece,
+            mix_weight[block_number],
+            (((1,), (1,)), ((), ())),
+            preferred_element_type=jnp.float32,
+        )
         grad_pre = (grad_held * derivative).astype(jnp.bfloat16)
+        if earlier is not None:
+            grad_pre, earlier = tied(grad_pre, earlier)
+            parts = [added(keep, arrived, False) for keep, arrived in earlier]
+            earlier = halving_steps(parts, orders, range(3, steps))
         kernel_parts[block_number] = (
             tap_products(grad_pre, padded_in, tap_spacing, tap_count) * grad_scale
         )
-        padded_grad = extended(grad_pre, (("seq", 0),), reach_rows)
+        padded_grad = extended(grad_pre, (("seq", 0),), halo_rows[block_number])
         upstream = (
             upstream.astype(jnp.float32)
             + tap_sum(padded_grad, kernel, tap_spacing, row_count, True)
         ).astype(jnp.bfloat16)
-        weight_part = weight_part * grad_scale
-        weight_parts[block_number] = lax.psum_scatter(
-            weight_part, "seq", scatter_dimension=0, tiled=True
-        )
+        if block_number > 0:
+            upstream, earlier = tied(upstream, pairs)
+        else:
+            upstream, (earlier, pairs) = tied(upstream, (earlier, pairs))
+            weight_parts[1] = finished(earlier, grad_scale)
+            parts = [added(keep, arrived, False) for keep, arrived in pairs]
+            weight_parts[0] = finished(halving_steps(parts, orders, range(1, steps)), grad_scale)
     weight_grad = jnp.stack(weight_parts)
     embed_part = jnp.dot(one_hot, upstream, preferred_element_type=jnp.float32) * grad_scale
-    kernel_grad, embed_grad = lax.psum((jnp.stack(kernel_parts), embed_part), "seq")
+    sums = doubled_sum(jnp.concatenate(kernel_parts + [embed_part]), orders[0])
+    kernel_grad = sums[: block_count * tap_count].reshape(block_count, tap_count, -1)
+    embed_grad = sums[block_count * tap_count :]
     return (upstream, weight_grad, kernel_grad, embed_grad)
 
 

time: 552 us -> 192 us (0.35)
  waiting for transfers between devices: 378 us -> 54.8 us
  blocking collectives: 77.2 us -> 0 us
  starting transfers between devices: 24 us -> 47 us
  other arithmetic: 20.3 us -> 38.9 us
  matrix products: 35 us -> 19.4 us
  local copies, waits for them, and re-layouts: 2.65 us -> 15.5 us
    reduce_scatter x2 -> x0, waiting for transfers between devices: 253 us -> none  [on_device(): lax.psum_scatter(weight_part, 'seq', scatter_dimension=0, tiled=True)]
    psum x1 -> x0, waiting for transfers between devices: 109 us -> none  [on_device(): lax.psum((jnp.stack(kernel_parts), embed_part), 'seq')]
    psum x1 -> x0, blocking collectives: 77.2 us -> none  [on_device(): lax.psum((jnp.stack(kernel_parts), embed_part), 'seq')]
    ppermute x0 -> x22, waiting for transfers between devices: none -> 40.8 us  [the longest x20 36.3 us: exchanged(): return lax.ppermute(cells, axis, [(i, i ^ 1 << bit) for i in range(count)])]
    ppermute x0 -> x22, starting transfers between devices: none -> 36 us  [the longest x20 29.9 us: exchanged(): return lax.ppermute(cells, axis, [(i, i ^ 1 << bit) for i in range(count)])]
    dot_general x4 -> x6, matrix products: 34.2 us -> 18.6 us  [the longest x2 9.94 us: on_device(): lax.dot_general(column_piece, mix_weight[block_number], (((1,), (1,)), ((...]
    convert_element_type x0 -> x11, other arithmetic: none -> 12 us  [added(): return total if last else total.astype(jnp.bfloat16)]
    ppermute x4 -> x2, starting transfers between devices: 18.4 us -> 8.08 us  [extended(): lax.ppermute(tail, axis, [(i, (i + 1) % count) for i in range(ends)])]
  transfers between devices with their start and end apart: 13 -> 28, of which waited for: 10 -> 14; matrix products, arithmetic and copies ran while one was open for 7% -> 29% of each run, Pallas kernels for 0% -> 0%
where the time goes in v2:
time: 192 us; the launch traced here: 191 us
  waiting for transfers between devices  54.8 us (29%)
  starting transfers between devices  47 us (24%)
  other arithmetic  38.9 us (20%)
  matrix products  19.4 us (10%)
  local copies, waits for them, and re-layouts  15.5 us (8%)
  between operations  15.2 us (8%)
    ppermute x20, waiting for transfers between devices, exchanged(): return lax.ppermute(cells, axis, [(i, i ^ 1 << bit) for i in range(count)])  36.3 us
    ppermute x20, starting transfers between devices, exchanged(): return lax.ppermute(cells, axis, [(i, i ^ 1 << bit) for i in range(count)])  29.9 us
    ppermute x2, waiting for transfers between devices, extended(): lax.ppermute(head, axis, [((i + 1) % count, i) for i in range(ends)])  12.1 us
    convert_element_type x11, other arithmetic, added(): return total if last else total.astype(jnp.bfloat16)  12 us
    dot_general x2, matrix products, on_device(): lax.dot_general(column_piece, mix_weight[block_number], (((1,), (1,)), ((...  9.94 us
    convert_element_type x2, other arithmetic, on_device(): upstream = (upstream.astype(jnp.float32) + tap_sum(padded_grad, kernel, t...  8.99 us
    dot_general x4, matrix products, on_device(): lax.dot_general(act_half, lax.slice_in_dim(column_piece, chunk * width, (...  8.68 us
    add x2, other arithmetic, tap_sum(): running = running + kernel[tap_index].astype(jnp.float32) * window  8.43 us
  transfers between devices with their start and end apart: 28, of which 14 were waited for; matrix products, arithmetic and copies ran while one was open for 29% of the time, Pallas kernels for 0%

profile of v2, /device:TPU:0, one launch (start us, length us, event | category | flops | bytes accessed | tf_op | source)
XLA Modules:
  0.0 190.7 jit_solution(15688562948301172749)
XLA Ops:
  8.0 1.3 and_reduce_fusion
  9.3 2.4 %broadcast_select_fusion = bf16[512,1024]{1,0:T(8,128)(2,1)} fusion(bf16[512,1024]{1,0:T(8,128)(2,1)} %param.15, pred[512]{0:T(512)(128)(4,1)S(1)} %and_reduce_fusion), kind=kLoop, calls=%fused_computation.186 | loop fusion | flops 524288 | bytes 2097664 | tf_op jit(solution)/shard_map/jit(_where)/select_n | solution.py:161
  13.2 4.8 %collective-permute-start = (bf16[48,1024]{1,0:T(8,128)(2,1)S(1)}, bf16[48,1024]{1,0:T(8,128)(2,1)S(1)}, u32[]{:S(2)}, u32[]{:S(2)}) collective-permute-start(bf16[48,1024]{1,0:T(8,128)(2,1)S(1)} %pad_maximum_fusion.7), channel_id=1, source_target_pairs={{0,2},{2,4},{4,6},{6,8},{8,10},{10,12},{12,14},{14,16},{16,18},{18... | collective-permute-start | bytes 294920 | tf_op jit(solution)/shard_map/ppermute | solution.py:38
  18.1 1.3 collective-permute-start.1
  20.3 4.3 %collective-permute-done.1 = bf16[48,1024]{1,0:T(8,128)(2,1)S(1)} collective-permute-done((bf16[48,1024]{1,0:T(8,128)(2,1)S(1)}, bf16[48,1024]{1,0:T(8,128)(2,1)S(1)}, u32[]{:S(2)}, u32[]{:S(2)}) %collective-permute-start.1) | collective-permute-done | bytes 98336 | tf_op jit(solution)/shard_map/ppermute | solution.py:39
  24.6 6.1 %fusion.13 = f32[512,1024]{1,0:T(8,128)S(1)} fusion(bf16[512,1024]{1,0:T(8,128)(2,1)} %param.14, bf16[32,1024]{1,0:T(8,128)(2,1)S(1)} %slice.393, bf16[32,1024]{1,0:T(8,128)(2,1)S(1)} %slice.385, f32[1024]{0:T(1024)S(1)} %bitcast.172, f32[1024]{0:T(1024)S(1)} %bitcast.174, f32[1024]{0:T(1024)S(1)} %bitcast.176, f32[1024]{0:T(1024)S(1)} %bitcast.178, ...), kind=kLoop, calls=%fused_computation.55 | loop fusion | flops 26214400 | bytes 3313664 | tf_op jit(solution)/shard_map/add | solution.py:64
  30.8 2.9 %convolution_convert_fusion.2 = bf16[1024,1024]{1,0:T(8,128)(2,1)S(1)} fusion(bf16[512,2048]{1,0:T(8,128)(2,1)} %all-gather.3.cloned.1.call-done, f32[512,1024]{1,0:T(8,128)S(1)} %fusion.13), kind=kOutput, calls=%fused_computation.131 | convolution fusion | flops 1079508992 | bytes 5242880 | tf_op jit(solution)/shard_map/dot_general | solution.py:179
  33.7 1.5 convolution_convert_fusion.3
  36.5 2.4 %collective-permute-start.4 = (bf16[2,2,2,64,1024]{4,3,1,0,2:T(8,128)(2,1)}, bf16[2,2,2,64,1024]{4,3,1,0,2:T(8,128)(2,1)}, u32[]{:S(2)}, u32[]{:S(2)}) collective-permute-start(bf16[2,2,2,64,1024]{4,3,1,0,2:T(8,128)(2,1)} %bitcast.140), channel_id=1, source_target_pairs={{0,2},{2,0},{4,6},{6,4},{8,10},{10,8},{12,14},{14,12},{16,18},{18,... | collective-permute-start | bytes 3145736 | tf_op jit(solution)/shard_map/ppermute | solution.py:94
  40.1 2.4 %collective-permute-start.5 = (bf16[2,2,2,64,1024]{4,3,1,0,2:T(8,128)(2,1)}, bf16[2,2,2,64,1024]{4,3,1,0,2:T(8,128)(2,1)}, u32[]{:S(2)}, u32[]{:S(2)}) collective-permute-start(bf16[2,2,2,64,1024]{4,3,1,0,2:T(8,128)(2,1)} %bitcast.138), channel_id=1, source_target_pairs={{0,4},{2,6},{4,0},{6,2},{8,12},{10,14},{12,8},{14,10},{16,20},{18,... | collective-permute-start | bytes 3145736 | tf_op jit(solution)/shard_map/ppermute | solution.py:94
  42.6 6.4 %fusion.51 = (f32[1024]{0:T(1024)}, f32[1024]{0:T(1024)}, f32[1024]{0:T(1024)}, f32[1024]{0:T(1024)}, f32[1024]{0:T(1024)}, /*index=5*/f32[1024]{0:T(1024)}, f32...) fusion(bf16[32,1024]{1,0:T(8,128)(2,1)S(1)} %slice.393, bf16[512,1024]{1,0:T(8,128)(2,1)S(1)} %copy-done.10, ...), kind=kOutput, calls=%fused_computation.93 | convolution fusion | flops 2184698880 | bytes 10653696 | tf_op jit(solution)/shard_map/dot_general | solution.py:193
  49.0 1.3 collective-permute-start.2
  50.3 4.7 %collective-permute-start.3 = (bf16[32,1024]{1,0:T(8,128)(2,1)S(1)}, bf16[32,1024]{1,0:T(8,128)(2,1)S(1)}, u32[]{:S(2)}, u32[]{:S(2)}) collective-permute-start(bf16[32,1024]{1,0:T(8,128)(2,1)S(1)} %get-tuple-element.115), channel_id=1, source_target_pairs={{0,2},{2,4},{4,6},{6,8},{8,10},{10,12},{12,14},{14,16},{16,18},{18... | collective-permute-start | bytes 196616 | tf_op jit(solution)/shard_map/ppermute | solution.py:24
  55.2 7.7 %collective-permute-done.2 = bf16[32,1024]{1,0:T(8,128)(2,1)S(1)} collective-permute-done((bf16[32,1024]{1,0:T(8,128)(2,1)S(1)}, bf16[32,1024]{1,0:T(8,128)(2,1)S(1)}, u32[]{:S(2)}, u32[]{:S(2)}) %collective-permute-start.2) | collective-permute-done | bytes 65568 | tf_op jit(solution)/shard_map/ppermute | solution.py:26
  62.9 6.6 %fusion.42 = bf16[512,1024]{1,0:T(8,128)(2,1)} fusion(bf16[512,1024]{1,0:T(8,128)(2,1)S(1)} %get-tuple-element.146, bf16[32,1024]{1,0:T(8,128)(2,1)S(1)} %collective-permute-done.3, bf16[32,1024]{1,0:T(8,128)(2,1)S(1)} %collective-permute-done.2, f32[1024]{0:T(1024)S(1)} %bitcast.173, f32[1024]{0:T(1024)S(1)} %bitcast.175, f32[1024]{0:T(1024)S(1)} %bitcast.177, ...), kind=kLoop, calls=%fused_computation.84 | loop fusion | flops 28311552 | bytes 3314176 | tf_op jit(solution)/shard_map/convert_element_type | solution.py:211
  69.6 2.5 %add_convert_fusion.2 = (bf16[2,2,2,64,1024]{4,3,1,0,2:T(8,128)(2,1)S(1)}, bf16[2,2,2,64,1024]{4,3,1,0,2:T(8,128)(2,1)S(1)}) fusion(bf16[2,2,2,64,1024]{4,3,1,0,2:T(8,128)(2,1)} %collective-permute-done.5, bf16[2,2,2,64,1024]{4,3,1,0,2:T(8,128)(2,1)S(1)} %bitcast.145, bf16[2,2,2,64,1024]{4,3,1,0,2:T(8,128)(2,1)} %collective-permute-done.4, ...), kind=kLoop, calls=%fused_computation.113 | loop fusion | flops 4194304 | bytes 6291456 | tf_op jit(solution)/shard_map/convert_element_type | solution.py:112
  73.2 3.6 %collective-permute-start.7 = (bf16[2,2,64,1024]{3,2,1,0:T(8,128)(2,1)}, bf16[2,2,64,1024]{3,2,1,0:T(8,128)(2,1)}, u32[]{:S(2)}, u32[]{:S(2)}) collective-permute-start(bf16[2,2,64,1024]{3,2,1,0:T(8,128)(2,1)} %get-tuple-element.110), channel_id=1, source_target_pairs={{0,2},{2,0},{4,6},{6,4},{8,10},{10,8},{12,14},{14,12},{16,18},{18,... | collective-permute-start | bytes 1572872 | tf_op jit(solution)/shard_map/ppermute | solution.py:94
  78.0 1.3 collective-permute-start.6
  79.4 2.3 %fusion.21 = f32[512,1024]{1,0:T(8,128)S(1)} fusion(bf16[512,1024]{1,0:T(8,128)(2,1)S(1)} %convolution_convert_fusion.4, bf16[16,1024]{1,0:T(8,128)(2,1)S(1)} %slice.423, bf16[16,1024]{1,0:T(8,128)(2,1)S(1)} %slice.416, f32[1024]{0:T(1024)S(1)} %bitcast.166, f32[1024]{0:T(1024)S(1)} %bitcast.168, f32[1024]{0:T(1024)S(1)} %bitcast.152, ...), kind=kLoop, calls=%fused_computation.63 | loop fusion | flops 26214400 | bytes 3248128 | tf_op jit(solution)/shard_map/add | solution.py:64
  81.9 3.8 %collective-permute-done.7 = bf16[2,2,64,1024]{3,2,1,0:T(8,128)(2,1)} collective-permute-done((bf16[2,2,64,1024]{3,2,1,0:T(8,128)(2,1)}, bf16[2,2,64,1024]{3,2,1,0:T(8,128)(2,1)}, u32[]{:S(2)}, u32[]{:S(2)}) %collective-permute-start.7) | collective-permute-done | bytes 524320 | tf_op jit(solution)/shard_map/ppermute | solution.py:94
  85.7 3.3 %collective-permute-done.6 = bf16[2,2,64,1024]{3,2,1,0:T(8,128)(2,1)} collective-permute-done((bf16[2,2,64,1024]{3,2,1,0:T(8,128)(2,1)}, bf16[2,2,64,1024]{3,2,1,0:T(8,128)(2,1)}, u32[]{:S(2)}, u32[]{:S(2)}) %collective-permute-start.6) | collective-permute-done | bytes 524320 | tf_op jit(solution)/shard_map/ppermute | solution.py:94
  89.0 2.9 %convolution_convert_fusion = bf16[1024,1024]{1,0:T(8,128)(2,1)S(1)} fusion(bf16[512,2048]{1,0:T(8,128)(2,1)} %all-gather.5.cloned.1.call-done, f32[512,1024]{1,0:T(8,128)S(1)} %fusion.21), kind=kOutput, calls=%fused_computation.129 | convolution fusion | flops 1079508992 | bytes 5242880 | tf_op jit(solution)/shard_map/dot_general | solution.py:179
  91.9 1.5 convolution_convert_fusion.1
  93.4 1.3 add_convert_fusion.4
  95.5 1.6 collective-permute-start.9
  98.9 3.5 %fusion.35 = bf16[512,1024]{1,0:T(8,128)(2,1)S(1)} fusion(f32[512,1024]{1,0:T(8,128)S(1)} %copy-done.7, bf16[512,2048]{1,0:T(8,128)(2,1)S(1)} %copy-done.45, bf16[2,1024,2048]{2,1,0:T(8,128)(2,1)S(1)} %bitcast.209), kind=kOutput, calls=%fused_computation.77 | convolution fusion | flops 2157445120 | bytes 9437184 | tf_op jit(solution)/shard_map/dot_general | solution.py:193
  105.2 1.7 collective-permute-start.15
  108.1 3.1 %fusion.67 = (f32[1024]{0:T(1024)}, f32[1024]{0:T(1024)}, f32[1024]{0:T(1024)}, f32[1024]{0:T(1024)}, f32[1024]{0:T(1024)}, /*index=5*/f32[1024]{0:T(1024)}, f32[1024]{0:T(1024)}, f32[1024]{0:T(1024)}, f32[1024]{0:T(1024)}) fusion(bf16[512,1024]{1,0:T(8,128)(2,1)S(1)} %fusion.35, bf16[16,1024]{1,0:T(8,128)(2,1)S(1)} %slice.423, ...), kind=kLoop, calls=%fused_computation.109 | loop fusion | flops 27253760 | bytes 2199552 | tf_op jit(solution)/shard_map/reduce_sum | solution.py:76
  111.2 1.5 stack.75
  113.9 2.9 %collective-permute-start.13 = (bf16[64,1024]{1,0:T(8,128)(2,1)S(1)}, bf16[64,1024]{1,0:T(8,128)(2,1)S(1)}, u32[]{:S(2)}, u32[]{:S(2)}) collective-permute-start(bf16[64,1024]{1,0:T(8,128)(2,1)S(1)} %get-tuple-element.124), channel_id=1, source_target_pairs={{0,16},{2,18},{4,20},{6,22},{8,24},{10,26},{12,28},{14,30},{16,0},... | collective-permute-start | bytes 393224 | tf_op jit(solution)/shard_map/ppermute | solution.py:94
  116.8 3.3 %collective-permute-start.11 = (bf16[16,1024]{1,0:T(8,128)(2,1)S(1)}, bf16[16,1024]{1,0:T(8,128)(2,1)S(1)}, u32[]{:S(2)}, u32[]{:S(2)}) collective-permute-start(bf16[16,1024]{1,0:T(8,128)(2,1)S(1)} %get-tuple-element.107), channel_id=1, source_target_pairs={{0,2},{2,4},{4,6},{6,8},{8,10},{10,12},{12,14},{14,16},{16,18},{18... | collective-permute-start | bytes 98312 | tf_op jit(solution)/shard_map/ppermute | solution.py:24
  121.7 1.8 collective-permute-done.11
  123.5 1.5 collective-permute-start.10
  125.4 4.4 %collective-permute-done.10 = bf16[16,1024]{1,0:T(8,128)(2,1)S(1)} collective-permute-done((bf16[16,1024]{1,0:T(8,128)(2,1)S(1)}, bf16[16,1024]{1,0:T(8,128)(2,1)S(1)}, u32[]{:S(2)}, u32[]{:S(2)}) %collective-permute-start.10) | collective-permute-done | bytes 32800 | tf_op jit(solution)/shard_map/ppermute | solution.py:26
  129.9 2.4 %fusion.58 = bf16[512,1024]{1,0:T(8,128)(2,1)S(1)} fusion(bf16[512,1024]{1,0:T(8,128)(2,1)S(1)} %fusion.35, bf16[512,1024]{1,0:T(8,128)(2,1)S(1)} %copy-done.2, bf16[528,1024]{1,0:T(8,128)(2,1)S(1)} %get-tuple-element.109, bf16[528,1024]{1,0:T(8,128)(2,1)S(1)} %constant_dynamic-update-slice_fusion, f32[1024]{0:T(1024)S(1)} %bitcast.167, ...), kind=kLoop, calls=%fused_computation.100 | loop fusion | flops 15204352 | bytes 11571200 | tf_op jit(solution)/shard_map/convert_element_type | solution.py:211
  132.6 3.0 %collective-permute-start.22 = (f32[23,1024]{1,0:T(8,128)S(1)}, f32[23,1024]{1,0:T(8,128)S(1)}, u32[]{:S(2)}, u32[]{:S(2)}) collective-permute-start(f32[23,1024]{1,0:T(8,128)S(1)} %pad_maximum_fusion.9), channel_id=1, source_target_pairs={{0,2},{2,0},{4,6},{6,4},{8,10},{10,8},{12,14},{14,12},{16,18},{18,... | collective-permute-start | bytes 282632 | tf_op jit(solution)/shard_map/ppermute | solution.py:94
  135.6 1.6 add_convert_fusion.1
  138.1 3.2 %collective-permute-start.16 = (bf16[2,2,64,1024]{3,2,0,1:T(8,128)(2,1)}, bf16[2,2,64,1024]{3,2,0,1:T(8,128)(2,1)}, u32[]{:S(2)}, u32[]{:S(2)}) collective-permute-start(bf16[2,2,64,1024]{3,2,0,1:T(8,128)(2,1)} %dynamic-slice_bitcast_fusion.1), channel_id=1, source_target_pairs={{0,4},{2,6},{4,0},{6,2},{8,12},{10,14},{12,8},{14,10},{16,20},{18,... | collective-permute-start | bytes 1572872 | tf_op jit(solution)/shard_map/ppermute | solution.py:94
  141.3 1.6 add_convert_fusion
  144.0 6.6 %collective-permute-done.23 = f32[23,1024]{1,0:T(8,128)S(1)} collective-permute-done((f32[23,1024]{1,0:T(8,128)S(1)}, f32[23,1024]{1,0:T(8,128)S(1)}, u32[]{:S(2)}, u32[]{:S(2)}) %collective-permute-start.23) | collective-permute-done | bytes 94240 | tf_op jit(solution)/shard_map/ppermute | solution.py:94
  151.5 3.7 %collective-permute-done.24 = f32[23,1024]{1,0:T(8,128)S(1)} collective-permute-done((f32[23,1024]{1,0:T(8,128)S(1)}, f32[23,1024]{1,0:T(8,128)S(1)}, u32[]{:S(2)}, u32[]{:S(2)}) %collective-permute-start.24) | collective-permute-done | bytes 94240 | tf_op jit(solution)/shard_map/ppermute | solution.py:94
  155.3 1.9 %collective-permute-start.25 = (f32[23,1024]{1,0:T(8,128)S(1)}, f32[23,1024]{1,0:T(8,128)S(1)}, u32[]{:S(2)}, u32[]{:S(2)}) collective-permute-start(f32[23,1024]{1,0:T(8,128)S(1)} %add.329), channel_id=1, source_target_pairs={{0,16},{2,18},{4,20},{6,22},{8,24},{10,26},{12,28},{14,30},{16,0},... | collective-permute-start | bytes 282632 | tf_op jit(solution)/shard_map/ppermute | solution.py:94
  157.3 4.3 %collective-permute-done.25 = f32[23,1024]{1,0:T(8,128)S(1)} collective-permute-done((f32[23,1024]{1,0:T(8,128)S(1)}, f32[23,1024]{1,0:T(8,128)S(1)}, u32[]{:S(2)}, u32[]{:S(2)}) %collective-permute-start.25) | collective-permute-done | bytes 94240 | tf_op jit(solution)/shard_map/ppermute | solution.py:94
  164.2 1.4 collective-permute-start.17
  166.6 6.7 %collective-permute-done.17 = bf16[2,64,1024]{2,1,0:T(8,128)(2,1)S(1)} collective-permute-done((bf16[2,64,1024]{2,1,0:T(8,128)(2,1)S(1)}, bf16[2,64,1024]{2,1,0:T(8,128)(2,1)S(1)}, u32[]{:S(2)}, u32[]{:S(2)}) %collective-permute-start.17) | collective-permute-done | bytes 262176 | tf_op jit(solution)/shard_map/ppermute | solution.py:94
  174.1 2.0 %collective-permute-done.20 = bf16[2,64,1024]{2,1,0:T(8,128)(2,1)S(1)} collective-permute-done((bf16[2,64,1024]{2,1,0:T(8,128)(2,1)S(1)}, bf16[2,64,1024]{2,1,0:T(8,128)(2,1)S(1)}, u32[]{:S(2)}, u32[]{:S(2)}) %collective-permute-start.20) | collective-permute-done | bytes 262176 | tf_op jit(solution)/shard_map/ppermute | solution.py:94
  177.0 3.0 %collective-permute-done.18 = bf16[64,1024]{1,0:T(8,128)(2,1)S(1)} collective-permute-done((bf16[64,1024]{1,0:T(8,128)(2,1)S(1)}, bf16[64,1024]{1,0:T(8,128)(2,1)S(1)}, u32[]{:S(2)}, u32[]{:S(2)}) %collective-permute-start.18) | collective-permute-done | bytes 131104 | tf_op jit(solution)/shard_map/ppermute | solution.py:94
  180.0 2.8 %collective-permute-done.21 = bf16[64,1024]{1,0:T(8,128)(2,1)S(1)} collective-permute-done((bf16[64,1024]{1,0:T(8,128)(2,1)S(1)}, bf16[64,1024]{1,0:T(8,128)(2,1)S(1)}, u32[]{:S(2)}, u32[]{:S(2)}) %collective-permute-start.21) | collective-permute-done | bytes 131104 | tf_op jit(solution)/shard_map/ppermute | solution.py:94
  (198 shorter events, 27.3 us)
Async XLA Ops:
  7.2 23.6 %all-gather.3.cloned.1.call-start = ((), (), s32[]{:S(2)}) async-start(), calls=%async_computation | async-start | bytes 3145728 | tf_op jit(solution)/shard_map/all_gather | solution.py:169
  9.3 10.1 %copy-start.13 = (bf16[2,9,1024]{2,0,1:T(2,128)(2,1)S(1)}, bf16[2,9,1024]{2,0,1:T(2,128)(2,1)}, u32[]{:S(2)}) copy-start(bf16[2,9,1024]{2,0,1:T(2,128)(2,1)} %param.12) | copy-start | bytes 110596
  11.7 77.3 %all-gather.5.cloned.1.call-start = ((), (), s32[]{:S(2)}) async-start(), calls=%async_computation.1 | async-start | bytes 3145728 | tf_op jit(solution)/shard_map/all_gather | solution.py:169
  13.2 7.0 %collective-permute-start = (bf16[48,1024]{1,0:T(8,128)(2,1)S(1)}, bf16[48,1024]{1,0:T(8,128)(2,1)S(1)}, u32[]{:S(2)}, u32[]{:S(2)}) collective-permute-start(bf16[48,1024]{1,0:T(8,128)(2,1)S(1)} %pad_maximum_fusion.7), channel_id=1, source_target_pairs={{0,2},{2,4},{4,6},{6,8},{8,10},{10,12},{12,14},{14,16},{16,18},{18... | collective-permute-start | bytes 294920 | tf_op jit(solution)/shard_map/ppermute | solution.py:38
  18.1 6.5 %collective-permute-start.1 = (bf16[48,1024]{1,0:T(8,128)(2,1)S(1)}, bf16[48,1024]{1,0:T(8,128)(2,1)S(1)}, u32[]{:S(2)}, u32[]{:S(2)}) collective-permute-start(bf16[48,1024]{1,0:T(8,128)(2,1)S(1)} %pad_maximum_fusion.8), channel_id=1, source_target_pairs={{2,0},{4,2},{6,4},{8,6},{10,8},{12,10},{14,12},{16,14},{18,16},{20... | collective-permute-start | bytes 294920 | tf_op jit(solution)/shard_map/ppermute | solution.py:39
  20.1 59.2 %copy-start.14 = (f32[1,1,1024]{2,0,1:T(1,128)}, f32[1,1,1024]{2,0,1:T(1,128)S(1)}, u32[]{:S(2)}) copy-start(f32[1,1,1024]{2,0,1:T(1,128)S(1)} %get-tuple-element.129) | copy-start | bytes 12292
  20.1 59.2 %copy-start.16 = (f32[1,1,1024]{2,0,1:T(1,128)}, f32[1,1,1024]{2,0,1:T(1,128)S(1)}, u32[]{:S(2)}) copy-start(f32[1,1,1024]{2,0,1:T(1,128)S(1)} %get-tuple-element.130) | copy-start | bytes 12292
  20.1 59.2 %copy-start.18 = (f32[1,1,1024]{2,0,1:T(1,128)}, f32[1,1,1024]{2,0,1:T(1,128)S(1)}, u32[]{:S(2)}) copy-start(f32[1,1,1024]{2,0,1:T(1,128)S(1)} %get-tuple-element.131) | copy-start | bytes 12292
  20.1 59.2 %copy-start.20 = (f32[1,1,1024]{2,0,1:T(1,128)}, f32[1,1,1024]{2,0,1:T(1,128)S(1)}, u32[]{:S(2)}) copy-start(f32[1,1,1024]{2,0,1:T(1,128)S(1)} %get-tuple-element.132) | copy-start | bytes 12292
  30.8 11.8 %slice-start = ((s8[8388608]{0:T(1024)(128)(4,1)}), s8[4194304]{0:T(1024)(128)(4,1)S(1)}, s32[]{:S(2)}) async-start(s8[8388608]{0:T(1024)(128)(4,1)} %bitcast.206), calls=%async_computation.2 | async-start | bytes 8388608
  33.7 8.9 %slice-start.1 = ((s8[8388608]{0:T(1024)(128)(4,1)}), s8[4194304]{0:T(1024)(128)(4,1)S(1)}, s32[]{:S(2)}) async-start(s8[8388608]{0:T(1024)(128)(4,1)} %bitcast.206), calls=%async_computation.3 | async-start | bytes 8388608
  36.5 33.0 %collective-permute-start.4 = (bf16[2,2,2,64,1024]{4,3,1,0,2:T(8,128)(2,1)}, bf16[2,2,2,64,1024]{4,3,1,0,2:T(8,128)(2,1)}, u32[]{:S(2)}, u32[]{:S(2)}) collective-permute-start(bf16[2,2,2,64,1024]{4,3,1,0,2:T(8,128)(2,1)} %bitcast.140), channel_id=1, source_target_pairs={{0,2},{2,0},{4,6},{6,4},{8,10},{10,8},{12,14},{14,12},{16,18},{18,... | collective-permute-start | bytes 3145736 | tf_op jit(solution)/shard_map/ppermute | solution.py:94
  40.1 29.4 %collective-permute-start.5 = (bf16[2,2,2,64,1024]{4,3,1,0,2:T(8,128)(2,1)}, bf16[2,2,2,64,1024]{4,3,1,0,2:T(8,128)(2,1)}, u32[]{:S(2)}, u32[]{:S(2)}) collective-permute-start(bf16[2,2,2,64,1024]{4,3,1,0,2:T(8,128)(2,1)} %bitcast.138), channel_id=1, source_target_pairs={{0,4},{2,6},{4,0},{6,2},{8,12},{10,14},{12,8},{14,10},{16,20},{18,... | collective-permute-start | bytes 3145736 | tf_op jit(solution)/shard_map/ppermute | solution.py:94
  49.0 13.9 %collective-permute-start.2 = (bf16[32,1024]{1,0:T(8,128)(2,1)S(1)}, bf16[32,1024]{1,0:T(8,128)(2,1)S(1)}, u32[]{:S(2)}, u32[]{:S(2)}) collective-permute-start(bf16[32,1024]{1,0:T(8,128)(2,1)S(1)} %get-tuple-element.114), channel_id=1, source_target_pairs={{2,0},{4,2},{6,4},{8,6},{10,8},{12,10},{14,12},{16,14},{18,16},{20... | collective-permute-start | bytes 196616 | tf_op jit(solution)/shard_map/ppermute | solution.py:26
  50.3 12.6 %collective-permute-start.3 = (bf16[32,1024]{1,0:T(8,128)(2,1)S(1)}, bf16[32,1024]{1,0:T(8,128)(2,1)S(1)}, u32[]{:S(2)}, u32[]{:S(2)}) collective-permute-start(bf16[32,1024]{1,0:T(8,128)(2,1)S(1)} %get-tuple-element.115), channel_id=1, source_target_pairs={{0,2},{2,4},{4,6},{6,8},{8,10},{10,12},{12,14},{14,16},{16,18},{18... | collective-permute-start | bytes 196616 | tf_op jit(solution)/shard_map/ppermute | solution.py:24
  55.0 7.9 %copy-start.4 = (bf16[512,1024]{1,0:T(8,128)(2,1)S(1)}, bf16[512,1024]{1,0:T(8,128)(2,1)}, u32[]{:S(2)}) copy-start(bf16[512,1024]{1,0:T(8,128)(2,1)} %param.15) | copy-start | bytes 3145732
  73.2 12.5 %collective-permute-start.7 = (bf16[2,2,64,1024]{3,2,1,0:T(8,128)(2,1)}, bf16[2,2,64,1024]{3,2,1,0:T(8,128)(2,1)}, u32[]{:S(2)}, u32[]{:S(2)}) collective-permute-start(bf16[2,2,64,1024]{3,2,1,0:T(8,128)(2,1)} %get-tuple-element.110), channel_id=1, source_target_pairs={{0,2},{2,0},{4,6},{6,4},{8,10},{10,8},{12,14},{14,12},{16,18},{18,... | collective-permute-start | bytes 1572872 | tf_op jit(solution)/shard_map/ppermute | solution.py:94
  78.0 11.0 %collective-permute-start.6 = (bf16[2,2,64,1024]{3,2,1,0:T(8,128)(2,1)}, bf16[2,2,64,1024]{3,2,1,0:T(8,128)(2,1)}, u32[]{:S(2)}, u32[]{:S(2)}) collective-permute-start(bf16[2,2,64,1024]{3,2,1,0:T(8,128)(2,1)} %get-tuple-element.112), channel_id=1, source_target_pairs={{0,4},{2,6},{4,0},{6,2},{8,12},{10,14},{12,8},{14,10},{16,20},{18,... | collective-permute-start | bytes 1572872 | tf_op jit(solution)/shard_map/ppermute | solution.py:94
  81.7 10.2 %copy-start.6 = (f32[512,1024]{1,0:T(8,128)}, f32[512,1024]{1,0:T(8,128)S(1)}, u32[]{:S(2)}) copy-start(f32[512,1024]{1,0:T(8,128)S(1)} %fusion.21) | copy-start | bytes 6291460
  89.0 9.9 %slice-start.2 = ((s8[8388608]{0:T(1024)(128)(4,1)}), s8[4194304]{0:T(1024)(128)(4,1)S(1)}, s32[]{:S(2)}) async-start(s8[8388608]{0:T(1024)(128)(4,1)} %bitcast.208), calls=%async_computation.4 | async-start | bytes 8388608
  95.5 12.6 %collective-permute-start.9 = (bf16[2,64,1024]{2,1,0:T(8,128)(2,1)S(1)}, bf16[2,64,1024]{2,1,0:T(8,128)(2,1)S(1)}, u32[]{:S(2)}, u32[]{:S(2)}) collective-permute-start(bf16[2,64,1024]{2,1,0:T(8,128)(2,1)S(1)} %get-tuple-element.120), channel_id=1, source_target_pairs={{0,8},{2,10},{4,12},{6,14},{8,0},{10,2},{12,4},{14,6},{16,24},{18,... | collective-permute-start | bytes 786440 | tf_op jit(solution)/shard_map/ppermute | solution.py:94
  98.4 9.8 %collective-permute-start.8 = (bf16[2,64,1024]{2,1,0:T(8,128)(2,1)S(1)}, bf16[2,64,1024]{2,1,0:T(8,128)(2,1)S(1)}, u32[]{:S(2)}, u32[]{:S(2)}) collective-permute-start(bf16[2,64,1024]{2,1,0:T(8,128)(2,1)S(1)} %get-tuple-element.122), channel_id=1, source_target_pairs={{0,8},{2,10},{4,12},{6,14},{8,0},{10,2},{12,4},{14,6},{16,24},{18,... | collective-permute-start | bytes 786440 | tf_op jit(solution)/shard_map/ppermute | solution.py:94
  103.7 28.6 %collective-permute-start.14 = (bf16[2,2,2,64,1024]{4,3,0,1,2:T(8,128)(2,1)}, bf16[2,2,2,64,1024]{4,3,0,1,2:T(8,128)(2,1)}, u32[]{:S(2)}, u32[]{:S(2)}) collective-permute-start(bf16[2,2,2,64,1024]{4,3,0,1,2:T(8,128)(2,1)} %bitcast.136), channel_id=1, source_target_pairs={{0,2},{2,0},{4,6},{6,4},{8,10},{10,8},{12,14},{14,12},{16,18},{18,... | collective-permute-start | bytes 3145736 | tf_op jit(solution)/shard_map/ppermute | solution.py:94
  105.2 27.1 %collective-permute-start.15 = (bf16[2,2,2,64,1024]{4,3,0,1,2:T(8,128)(2,1)}, bf16[2,2,2,64,1024]{4,3,0,1,2:T(8,128)(2,1)}, u32[]{:S(2)}, u32[]{:S(2)}) collective-permute-start(bf16[2,2,2,64,1024]{4,3,0,1,2:T(8,128)(2,1)} %bitcast.134), channel_id=1, source_target_pairs={{0,4},{2,6},{4,0},{6,2},{8,12},{10,14},{12,8},{14,10},{16,20},{18,... | collective-permute-start | bytes 3145736 | tf_op jit(solution)/shard_map/ppermute | solution.py:94
  113.9 18.4 %collective-permute-start.13 = (bf16[64,1024]{1,0:T(8,128)(2,1)S(1)}, bf16[64,1024]{1,0:T(8,128)(2,1)S(1)}, u32[]{:S(2)}, u32[]{:S(2)}) collective-permute-start(bf16[64,1024]{1,0:T(8,128)(2,1)S(1)} %get-tuple-element.124), channel_id=1, source_target_pairs={{0,16},{2,18},{4,20},{6,22},{8,24},{10,26},{12,28},{14,30},{16,0},... | collective-permute-start | bytes 393224 | tf_op jit(solution)/shard_map/ppermute | solution.py:94
  116.8 6.7 %collective-permute-start.11 = (bf16[16,1024]{1,0:T(8,128)(2,1)S(1)}, bf16[16,1024]{1,0:T(8,128)(2,1)S(1)}, u32[]{:S(2)}, u32[]{:S(2)}) collective-permute-start(bf16[16,1024]{1,0:T(8,128)(2,1)S(1)} %get-tuple-element.107), channel_id=1, source_target_pairs={{0,2},{2,4},{4,6},{6,8},{8,10},{10,12},{12,14},{14,16},{16,18},{18... | collective-permute-start | bytes 98312 | tf_op jit(solution)/shard_map/ppermute | solution.py:24
  121.2 8.6 %copy-start.2 = (bf16[512,1024]{1,0:T(8,128)(2,1)S(1)}, bf16[512,1024]{1,0:T(8,128)(2,1)}, u32[]{:S(2)}) copy-start(bf16[512,1024]{1,0:T(8,128)(2,1)} %fusion.42) | copy-start | bytes 3145732
  121.2 8.6 %copy-start.15 = (f32[1,1,1024]{2,0,1:T(1,128)S(1)}, f32[1,1,1024]{2,0,1:T(1,128)}, u32[]{:S(2)}) copy-start(f32[1,1,1024]{2,0,1:T(1,128)} %copy-done.14) | copy-start | bytes 12292
  121.2 8.6 %copy-start.17 = (f32[1,1,1024]{2,0,1:T(1,128)S(1)}, f32[1,1,1024]{2,0,1:T(1,128)}, u32[]{:S(2)}) copy-start(f32[1,1,1024]{2,0,1:T(1,128)} %copy-done.16) | copy-start | bytes 12292
  121.2 8.6 %copy-start.19 = (f32[1,1,1024]{2,0,1:T(1,128)S(1)}, f32[1,1,1024]{2,0,1:T(1,128)}, u32[]{:S(2)}) copy-start(f32[1,1,1024]{2,0,1:T(1,128)} %copy-done.18) | copy-start | bytes 12292
  121.2 8.6 %copy-start.21 = (f32[1,1,1024]{2,0,1:T(1,128)S(1)}, f32[1,1,1024]{2,0,1:T(1,128)}, u32[]{:S(2)}) copy-start(f32[1,1,1024]{2,0,1:T(1,128)} %copy-done.20) | copy-start | bytes 12292
  121.2 8.6 %copy-start.23 = (f32[1,1,1024]{2,0,1:T(1,128)S(1)}, f32[1,1,1024]{2,0,1:T(1,128)}, u32[]{:S(2)}) copy-start(f32[1,1,1024]{2,0,1:T(1,128)} %get-tuple-element.133) | copy-start | bytes 12292
  121.2 8.6 %copy-start.25 = (f32[1,1,1024]{2,0,1:T(1,128)S(1)}, f32[1,1,1024]{2,0,1:T(1,128)}, u32[]{:S(2)}) copy-start(f32[1,1,1024]{2,0,1:T(1,128)} %get-tuple-element.134) | copy-start | bytes 12292
  121.3 8.6 %copy-start.27 = (f32[1,1,1024]{2,0,1:T(1,128)S(1)}, f32[1,1,1024]{2,0,1:T(1,128)}, u32[]{:S(2)}) copy-start(f32[1,1,1024]{2,0,1:T(1,128)} %get-tuple-element.135) | copy-start | bytes 12292
  121.3 8.6 %copy-start.29 = (f32[1,1,1024]{2,0,1:T(1,128)S(1)}, f32[1,1,1024]{2,0,1:T(1,128)}, u32[]{:S(2)}) copy-start(f32[1,1,1024]{2,0,1:T(1,128)} %get-tuple-element.144) | copy-start | bytes 12292
  121.3 8.6 %copy-start.31 = (f32[1,1,1024]{2,0,1:T(1,128)S(1)}, f32[1,1,1024]{2,0,1:T(1,128)}, u32[]{:S(2)}) copy-start(f32[1,1,1024]{2,0,1:T(1,128)} %get-tuple-element.145) | copy-start | bytes 12292
  121.3 11.0 %collective-permute-start.12 = (bf16[64,1024]{1,0:T(8,128)(2,1)S(1)}, bf16[64,1024]{1,0:T(8,128)(2,1)S(1)}, u32[]{:S(2)}, u32[]{:S(2)}) collective-permute-start(bf16[64,1024]{1,0:T(8,128)(2,1)S(1)} %get-tuple-element.126), channel_id=1, source_target_pairs={{0,16},{2,18},{4,20},{6,22},{8,24},{10,26},{12,28},{14,30},{16,0},... | collective-permute-start | bytes 393224 | tf_op jit(solution)/shard_map/ppermute | solution.py:94
  123.5 6.3 %collective-permute-start.10 = (bf16[16,1024]{1,0:T(8,128)(2,1)S(1)}, bf16[16,1024]{1,0:T(8,128)(2,1)S(1)}, u32[]{:S(2)}, u32[]{:S(2)}) collective-permute-start(bf16[16,1024]{1,0:T(8,128)(2,1)S(1)} %get-tuple-element.106), channel_id=1, source_target_pairs={{2,0},{4,2},{6,4},{8,6},{10,8},{12,10},{14,12},{16,14},{18,16},{20... | collective-permute-start | bytes 98312 | tf_op jit(solution)/shard_map/ppermute | solution.py:26
  132.6 11.2 %collective-permute-start.22 = (f32[23,1024]{1,0:T(8,128)S(1)}, f32[23,1024]{1,0:T(8,128)S(1)}, u32[]{:S(2)}, u32[]{:S(2)}) collective-permute-start(f32[23,1024]{1,0:T(8,128)S(1)} %pad_maximum_fusion.9), channel_id=1, source_target_pairs={{0,2},{2,0},{4,6},{6,4},{8,10},{10,8},{12,14},{14,12},{16,18},{18,... | collective-permute-start | bytes 282632 | tf_op jit(solution)/shard_map/ppermute | solution.py:94
  138.1 24.8 %collective-permute-start.16 = (bf16[2,2,64,1024]{3,2,0,1:T(8,128)(2,1)}, bf16[2,2,64,1024]{3,2,0,1:T(8,128)(2,1)}, u32[]{:S(2)}, u32[]{:S(2)}) collective-permute-start(bf16[2,2,64,1024]{3,2,0,1:T(8,128)(2,1)} %dynamic-slice_bitcast_fusion.1), channel_id=1, source_target_pairs={{0,4},{2,6},{4,0},{6,2},{8,12},{10,14},{12,8},{14,10},{16,20},{18,... | collective-permute-start | bytes 1572872 | tf_op jit(solution)/shard_map/ppermute | solution.py:94
  143.8 21.7 %collective-permute-start.19 = (bf16[2,2,64,1024]{3,2,0,1:T(8,128)(2,1)}, bf16[2,2,64,1024]{3,2,0,1:T(8,128)(2,1)S(1)}, u32[]{:S(2)}, u32[]{:S(2)}) collective-permute-start(bf16[2,2,64,1024]{3,2,0,1:T(8,128)(2,1)} %dynamic-slice_bitcast_fusion), channel_id=1, source_target_pairs={{0,2},{2,0},{4,6},{6,4},{8,10},{10,8},{12,14},{14,12},{16,18},{18,... | collective-permute-start | bytes 1572872 | tf_op jit(solution)/shard_map/ppermute | solution.py:94
  143.8 6.7 %collective-permute-start.23 = (f32[23,1024]{1,0:T(8,128)S(1)}, f32[23,1024]{1,0:T(8,128)S(1)}, u32[]{:S(2)}, u32[]{:S(2)}) collective-permute-start(f32[23,1024]{1,0:T(8,128)S(1)} %fusion.110), channel_id=1, source_target_pairs={{0,4},{2,6},{4,0},{6,2},{8,12},{10,14},{12,8},{14,10},{16,20},{18,... | collective-permute-start | bytes 282632 | tf_op jit(solution)/shard_map/ppermute | solution.py:94
  150.6 4.7 %collective-permute-start.24 = (f32[23,1024]{1,0:T(8,128)S(1)}, f32[23,1024]{1,0:T(8,128)S(1)}, u32[]{:S(2)}, u32[]{:S(2)}) collective-permute-start(f32[23,1024]{1,0:T(8,128)S(1)} %add.328), channel_id=1, source_target_pairs={{0,8},{2,10},{4,12},{6,14},{8,0},{10,2},{12,4},{14,6},{16,24},{18,... | collective-permute-start | bytes 282632 | tf_op jit(solution)/shard_map/ppermute | solution.py:94
  155.3 6.3 %collective-permute-start.25 = (f32[23,1024]{1,0:T(8,128)S(1)}, f32[23,1024]{1,0:T(8,128)S(1)}, u32[]{:S(2)}, u32[]{:S(2)}) collective-permute-start(f32[23,1024]{1,0:T(8,128)S(1)} %add.329), channel_id=1, source_target_pairs={{0,16},{2,18},{4,20},{6,22},{8,24},{10,26},{12,28},{14,30},{16,0},... | collective-permute-start | bytes 282632 | tf_op jit(solution)/shard_map/ppermute | solution.py:94
  164.2 9.1 %collective-permute-start.17 = (bf16[2,64,1024]{2,1,0:T(8,128)(2,1)S(1)}, bf16[2,64,1024]{2,1,0:T(8,128)(2,1)S(1)}, u32[]{:S(2)}, u32[]{:S(2)}) collective-permute-start(bf16[2,64,1024]{2,1,0:T(8,128)(2,1)S(1)} %dynamic-slice_bitcast_fusion.7), channel_id=1, source_target_pairs={{0,8},{2,10},{4,12},{6,14},{8,0},{10,2},{12,4},{14,6},{16,24},{18,... | collective-permute-start | bytes 786440 | tf_op jit(solution)/shard_map/ppermute | solution.py:94
  165.8 10.4 %collective-permute-start.20 = (bf16[2,64,1024]{2,1,0:T(8,128)(2,1)S(1)}, bf16[2,64,1024]{2,1,0:T(8,128)(2,1)S(1)}, u32[]{:S(2)}, u32[]{:S(2)}) collective-permute-start(bf16[2,64,1024]{2,1,0:T(8,128)(2,1)S(1)} %dynamic-slice_bitcast_fusion.6), channel_id=1, source_target_pairs={{0,8},{2,10},{4,12},{6,14},{8,0},{10,2},{12,4},{14,6},{16,24},{18,... | collective-permute-start | bytes 786440 | tf_op jit(solution)/shard_map/ppermute | solution.py:94
  173.4 6.5 %collective-permute-start.18 = (bf16[64,1024]{1,0:T(8,128)(2,1)S(1)}, bf16[64,1024]{1,0:T(8,128)(2,1)S(1)}, u32[]{:S(2)}, u32[]{:S(2)}) collective-permute-start(bf16[64,1024]{1,0:T(8,128)(2,1)S(1)} %dynamic-slice_bitcast_fusion.13), channel_id=1, source_target_pairs={{0,16},{2,18},{4,20},{6,22},{8,24},{10,26},{12,28},{14,30},{16,0},... | collective-permute-start | bytes 393224 | tf_op jit(solution)/shard_map/ppermute | solution.py:94
  176.2 6.5 %collective-permute-start.21 = (bf16[64,1024]{1,0:T(8,128)(2,1)S(1)}, bf16[64,1024]{1,0:T(8,128)(2,1)S(1)}, u32[]{:S(2)}, u32[]{:S(2)}) collective-permute-start(bf16[64,1024]{1,0:T(8,128)(2,1)S(1)} %dynamic-slice_bitcast_fusion.12), channel_id=1, source_target_pairs={{0,16},{2,18},{4,20},{6,22},{8,24},{10,26},{12,28},{14,30},{16,0},... | collective-permute-start | bytes 393224 | tf_op jit(solution)/shard_map/ppermute | solution.py:94
  (30 other events, 139.7 us)
Sparse Core Ops, SparseCore 0:
  11.8 13.2 all-gather.2
  69.7 12.6 all-gather.4

commit v3 on v2

--- a/solution.py
+++ b/solution.py
@@ -13,21 +13,13 @@
 gelu_cubic = 0.044715
 
 
-def extended(cells, sides, width):
-    for axis, dim in sides:
-        count = lax.axis_size(axis)
-        ends = count - 1
-        head = lax.slice_in_dim(cells, 0, width, axis=dim)
-        tail = lax.slice_in_dim(cells, cells.shape[dim] - width, cells.shape[dim], axis=dim)
-        cells = jnp.concatenate(
-            [
-                lax.ppermute(tail, axis, [(i, (i + 1) % count) for i in range(ends)]),
-                cells,
-                lax.ppermute(head, axis, [((i + 1) % count, i) for i in range(ends)]),
-            ],
-            axis=dim,
-        )
-    return cells
+def edge_rows(cells, width):
+    count = lax.axis_size("seq")
+    ends = count - 1
+    return (
+        lax.ppermute(cells[-width:], "seq", [(i, (i + 1) % count) for i in range(ends)]),
+        lax.ppermute(cells[:width], "seq", [((i + 1) % count, i) for i in range(ends)]),
+    )
 
 
 def padded_together(arrays, widths):
@@ -98,13 +90,22 @@
     return part.reshape((2,) * bits + (part.shape[0] >> bits, part.shape[1]))
 
 
-def halving_step(part, order, step):
-    bit = order[step]
-    dim = sorted(order[step:], reverse=True).index(bit)
-    mine = (lax.axis_index("seq") >> bit) & 1
-    send = lax.dynamic_index_in_dim(part, 1 - mine, dim, keepdims=False)
-    keep = lax.dynamic_index_in_dim(part, mine, dim, keepdims=False)
-    return (keep, exchanged(send, "seq", bit))
+def halves_of(parts, orders, step):
+    halves = []
+    for part, order in zip(parts, orders):
+        bit = order[step]
+        dim = sorted(order[step:], reverse=True).index(bit)
+        mine = (lax.axis_index("seq") >> bit) & 1
+        send = lax.dynamic_index_in_dim(part, 1 - mine, dim, keepdims=False)
+        keep = lax.dynamic_index_in_dim(part, mine, dim, keepdims=False)
+        halves.append((keep, send))
+    return halves
+
+
+def swapped(halves, orders, step):
+    return [
+        (keep, exchanged(send, "seq", order[step])) for (keep, send), order in zip(halves, orders)
+    ]
 
 
 def added(keep, arrived, last):
@@ -112,28 +113,24 @@
     return total if last else total.astype(jnp.bfloat16)
 
 
-def halving_steps(parts, orders, steps):
-    pairs = None
+def next_halves(pairs, orders, step):
+    return halves_of([added(keep, arrived, False) for keep, arrived in pairs], orders, step)
+
+
+def kept_with(value, pairs):
+    kept = [keep for keep, arrived in pairs]
+    value, kept = lax.optimization_barrier((value, kept))
+    return (value, [(keep, arrived) for keep, (_, arrived) in zip(kept, pairs)])
+
+
+def later_steps(pairs, orders, steps):
     for step in steps:
-        if pairs is not None:
-            parts = [added(keep, arrived, False) for keep, arrived in pairs]
-        pairs = [halving_step(part, order, step) for part, order in zip(parts, orders)]
+        pairs = swapped(next_halves(pairs, orders, step), orders, step)
     return pairs
 
 
 def finished(pairs, scale):
     return jnp.concatenate([added(keep, arrived, True) for keep, arrived in pairs], axis=1) * scale
-
-
-def tied(value, pairs):
-    value, pairs = lax.optimization_barrier((value, pairs))
-    return (value, pairs)
-
-
-def doubled_sum(part, order):
-    for bit in order:
-        part = part + exchanged(part, "seq", bit)
-    return part
 
 
 def on_device(
@@ -159,37 +156,23 @@
     halo_rows = [taps_per_side * BASE_DILATION * 2**number for number in range(block_count)]
     padded_inputs = padded_together((first_input, saved_input), halo_rows)
     upstream = jnp.where(covered[:, None], cotangent, jnp.zeros_like(cotangent))
-    weight_parts = [None] * block_count
     kernel_parts = [None] * block_count
     earlier = None
     for block_number in range(block_count - 1, -1, -1):
         tap_spacing = BASE_DILATION * 2**block_number
+        reach_rows = halo_rows[block_number]
         padded_in = padded_inputs[block_number]
         kernel = conv_kernel[block_number]
         column_piece = lax.all_gather(upstream, "blk", axis=1, tiled=True)
+        if earlier is not None:
+            padded_in, earlier = lax.optimization_barrier((padded_in, earlier))
         pre_act = tap_sum(padded_in, kernel, tap_spacing, row_count, False)
         activation, derivative = gelu_pair(pre_act)
         act_half = activation.astype(jnp.bfloat16)
         if earlier is not None:
-            parts = [added(keep, arrived, False) for keep, arrived in earlier]
-            pairs = halving_steps(parts, orders, range(1, 2))
-            column_piece, earlier = tied(column_piece, pairs)
-        width = column_piece.shape[1] // len(orders)
-        parts = [
-            lax.dot_general(
-                act_half,
-                lax.slice_in_dim(column_piece, chunk * width, (chunk + 1) * width, axis=1),
-                (((0,), (0,)), ((), ())),
-                preferred_element_type=jnp.float32,
-            ).astype(jnp.bfloat16)
-            for chunk in range(len(orders))
-        ]
-        column_piece, parts = lax.optimization_barrier((column_piece, parts))
-        parts = [split_rows(part, steps) for part in parts]
-        pairs = halving_steps(parts, orders, range(0, 1))
-        if earlier is not None:
-            parts = [added(keep, arrived, False) for keep, arrived in earlier]
-            earlier = halving_steps(parts, orders, range(2, 3))
+            halves = next_halves(earlier, orders, 1)
+            earlier = swapped(halves, orders, 1)
+            column_piece, earlier = kept_with(column_piece, earlier)
         grad_held = lax.dot_general(
             column_piece,
             mix_weight[block_number],
@@ -197,28 +180,50 @@
             preferred_element_type=jnp.float32,
         )
         grad_pre = (grad_held * derivative).astype(jnp.bfloat16)
-        if earlier is not None:
-            grad_pre, earlier = tied(grad_pre, earlier)
-            parts = [added(keep, arrived, False) for keep, arrived in earlier]
-            earlier = halving_steps(parts, orders, range(3, steps))
+        edges = edge_rows(grad_pre, reach_rows)
+        act_half, grad_pre = lax.optimization_barrier((act_half, grad_pre))
+        width = column_piece.shape[1] // len(orders)
+        parts = [
+            split_rows(
+                lax.dot_general(
+                    act_half,
+                    lax.slice_in_dim(column_piece, chunk * width, (chunk + 1) * width, axis=1),
+                    (((0,), (0,)), ((), ())),
+                    preferred_element_type=jnp.float32,
+                ).astype(jnp.bfloat16),
+                steps,
+            )
+            for chunk in range(len(orders))
+        ]
+        halves = halves_of(parts, orders, 0)
+        pairs = swapped(halves, orders, 0)
+        edges, pairs = kept_with(edges, pairs)
+        if earlier is not None:
+            edges, earlier = lax.optimization_barrier((edges, earlier))
+        if earlier is not None:
+            earlier = later_steps(earlier, orders, range(2, 3))
         kernel_parts[block_number] = (
             tap_products(grad_pre, padded_in, tap_spacing, tap_count) * grad_scale
         )
-        padded_grad = extended(grad_pre, (("seq", 0),), halo_rows[block_number])
+        padded_grad = jnp.concatenate([edges[0], grad_pre, edges[1]])
         upstream = (
             upstream.astype(jnp.float32)
             + tap_sum(padded_grad, kernel, tap_spacing, row_count, True)
         ).astype(jnp.bfloat16)
         if block_number > 0:
-            upstream, earlier = tied(upstream, pairs)
-        else:
-            upstream, (earlier, pairs) = tied(upstream, (earlier, pairs))
-            weight_parts[1] = finished(earlier, grad_scale)
-            parts = [added(keep, arrived, False) for keep, arrived in pairs]
-            weight_parts[0] = finished(halving_steps(parts, orders, range(1, steps)), grad_scale)
+            earlier = pairs
+    embed_part = jnp.dot(one_hot, upstream, preferred_element_type=jnp.float32) * grad_scale
+    sums = jnp.concatenate(kernel_parts + [embed_part])
+    for step in range(steps):
+        sums = sums + exchanged(sums, "seq", steps - 1 - step)
+        if step == 0:
+            sums, earlier = lax.optimization_barrier((sums, earlier))
+            earlier = later_steps(earlier, orders, range(3, steps))
+        elif step < 4:
+            sums, pairs, earlier = lax.optimization_barrier((sums, pairs, earlier))
+            pairs = later_steps(pairs, orders, range(step, step + 1 if step < 3 else steps))
+    weight_parts = [finished(pairs, grad_scale), finished(earlier, grad_scale)]
     weight_grad = jnp.stack(weight_parts)
-    embed_part = jnp.dot(one_hot, upstream, preferred_element_type=jnp.float32) * grad_scale
-    sums = doubled_sum(jnp.concatenate(kernel_parts + [embed_part]), orders[0])
     kernel_grad = sums[: block_count * tap_count].reshape(block_count, tap_count, -1)
     embed_grad = sums[block_count * tap_count :]
     return (upstream, weight_grad, kernel_grad, embed_grad)

time: 192 us -> 193 us (level)
  waiting for transfers between devices: 54.8 us -> 59.2 us
  other arithmetic: 38.9 us -> 35.6 us
    ppermute x20, waiting for transfers between devices: 36.3 us -> 55.2 us  [exchanged(): return lax.ppermute(cells, axis, [(i, i ^ 1 << bit) for i in range(count)])]
    ppermute x4, waiting for transfers between devices: 13.9 us -> 0.01 us  [the longest x2 0.01 us: edge_rows(): lax.ppermute(cells[:width], 'seq', [((i + 1) % count, i) for i in range(e...]
    convert_element_type x0 -> x2, other arithmetic: none -> 7.73 us  [on_device(): act_half = activation.astype(jnp.bfloat16)]
    add x6 -> x4, other arithmetic: 8.5 us -> 0.95 us  [on_device(): sums = sums + exchanged(sums, 'seq', steps - 1 - step)]
    dot_general x2, matrix products: 9.94 us -> 13.7 us  [on_device(): lax.dot_general(column_piece, mix_weight[block_number], (((1,), (1,)), ((...]
    ppermute x1, waiting for transfers between devices: 4.33 us -> 0.69 us  [padded_together(): lax.ppermute(heads, 'seq', [((i + 1) % count, i) for i in range(ends)])]
    ppermute x20, starting transfers between devices: 29.9 us -> 26.5 us  [exchanged(): return lax.ppermute(cells, axis, [(i, i ^ 1 << bit) for i in range(count)])]
    ppermute x1, waiting for transfers between devices: 0.17 us -> 3.2 us  [padded_together(): lax.ppermute(tails, 'seq', [(i, (i + 1) % count) for i in range(ends)])]
  transfers between devices with their start and end apart: 28 -> 28, of which waited for: 14 -> 15; matrix products, arithmetic and copies ran while one was open for 29% -> 28% of each run, Pallas kernels for 0% -> 0%
where the time goes in v3:
time: 193 us
  waiting for transfers between devices  59.2 us (31%)
  starting transfers between devices  45.7 us (24%)
  other arithmetic  35.6 us (18%)
  matrix products  21.1 us (11%)
  local copies, waits for them, and re-layouts  16.2 us (8%)
  between operations  14.9 us (8%)
    ppermute x20, waiting for transfers between devices, exchanged(): return lax.ppermute(cells, axis, [(i, i ^ 1 << bit) for i in range(count)])  55.2 us
    ppermute x20, starting transfers between devices, exchanged(): return lax.ppermute(cells, axis, [(i, i ^ 1 << bit) for i in range(count)])  26.5 us
    dot_general x2, matrix products, on_device(): lax.dot_general(column_piece, mix_weight[block_number], (((1,), (1,)), ((...  13.7 us
    ppermute x2, starting transfers between devices, edge_rows(): lax.ppermute(cells[-width:], 'seq', [(i, (i + 1) % count) for i in range(...  9.79 us
    convert_element_type x11, other arithmetic, added(): return total if last else total.astype(jnp.bfloat16)  9.04 us
    convert_element_type x2, other arithmetic, on_device(): act_half = activation.astype(jnp.bfloat16)  7.73 us
    dot_general x4, matrix products, on_device(): lax.dot_general(act_half, lax.slice_in_dim(column_piece, chunk * width, (...  6.72 us
    squeeze x12, local copies, waits for them, and re-layouts, halves_of(): send = lax.dynamic_index_in_dim(part, 1 - mine, dim, keepdims=False)  6.34 us
  transfers between devices with their start and end apart: 28, of which 15 were waited for; matrix products, arithmetic and copies ran while one was open for 28% of the time, Pallas kernels for 0%

profile of v3, /device:TPU:0, one launch (start us, length us, event | category | flops | bytes accessed | tf_op | source)
XLA Modules:
  0.0 192.8 jit_solution(8333689761018775168)
XLA Ops:
  8.0 1.3 and_reduce_fusion
  9.3 2.4 %broadcast_select_fusion = bf16[512,1024]{1,0:T(8,128)(2,1)} fusion(bf16[512,1024]{1,0:T(8,128)(2,1)} %param.15, pred[512]{0:T(512)(128)(4,1)S(1)} %and_reduce_fusion), kind=kLoop, calls=%fused_computation.155 | loop fusion | flops 524288 | bytes 2097664 | tf_op jit(solution)/shard_map/jit(_where)/select_n | solution.py:158
  13.0 1.3 collective-permute-start.1
  14.3 5.5 %collective-permute-start = (bf16[48,1024]{1,0:T(8,128)(2,1)S(1)}, bf16[48,1024]{1,0:T(8,128)(2,1)S(1)}, u32[]{:S(2)}, u32[]{:S(2)}) collective-permute-start(bf16[48,1024]{1,0:T(8,128)(2,1)S(1)} %pad_maximum_fusion.4), channel_id=1, source_target_pairs={{0,2},{2,4},{4,6},{6,8},{8,10},{10,12},{12,14},{14,16},{16,18},{18... | collective-permute-start | bytes 294920 | tf_op jit(solution)/shard_map/ppermute | solution.py:30
  20.6 3.2 %collective-permute-done = bf16[48,1024]{1,0:T(8,128)(2,1)S(1)} collective-permute-done((bf16[48,1024]{1,0:T(8,128)(2,1)S(1)}, bf16[48,1024]{1,0:T(8,128)(2,1)S(1)}, u32[]{:S(2)}, u32[]{:S(2)}) %collective-permute-start) | collective-permute-done | bytes 98336 | tf_op jit(solution)/shard_map/ppermute | solution.py:30
  23.9 3.8 %multiply_convert_fusion.1 = (bf16[512,1024]{1,0:T(8,128)(2,1)}, f32[512,1024]{1,0:T(8,128)}) fusion(bf16[32,1024]{1,0:T(8,128)(2,1)S(1)} %slice.390, bf16[512,1024]{1,0:T(8,128)(2,1)S(1)} %copy-done.3, f32[1024]{0:T(1024)S(1)} %bitcast.170, f32[1024]{0:T(1024)S(1)} %bitcast.172, f32[1024]{0:T(1024)S(1)} %bitcast.174, f32[1024]{0:T(1024)S(1)} %bitcast.176, ...), kind=kLoop, calls=%fused_computation.115 | loop fusion | flops 30932992 | bytes 4362240 | tf_op jit(solution)/shard_map/convert_element_type | solution.py:171
  27.8 6.9 %fusion.28 = bf16[512,1024]{1,0:T(8,128)(2,1)S(1)} fusion(f32[512,1024]{1,0:T(8,128)} %get-tuple-element.153, bf16[512,2048]{1,0:T(8,128)(2,1)} %all-gather.3.cloned.1.call-done, bf16[2,1024,2048]{2,1,0:T(8,128)(2,1)} %param.13), kind=kOutput, calls=%fused_computation.70 | convolution fusion | flops 2157445120 | bytes 9437184 | tf_op jit(solution)/shard_map/dot_general | solution.py:176
  34.7 1.3 collective-permute-start.3
  36.0 5.0 %collective-permute-start.2 = (bf16[32,1024]{1,0:T(8,128)(2,1)S(1)}, bf16[32,1024]{1,0:T(8,128)(2,1)S(1)}, u32[]{:S(2)}, u32[]{:S(2)}) collective-permute-start(bf16[32,1024]{1,0:T(8,128)(2,1)S(1)} %get-tuple-element.177), channel_id=1, source_target_pairs={{0,2},{2,4},{4,6},{6,8},{8,10},{10,12},{12,14},{14,16},{16,18},{18... | collective-permute-start | bytes 196616 | tf_op jit(solution)/shard_map/ppermute | solution.py:20
  41.1 1.3 convolution_convert_fusion.2
  42.6 1.3 convolution_convert_fusion.3
  48.3 2.9 %collective-permute-start.4 = (bf16[2,2,2,64,1024]{4,3,1,0,2:T(8,128)(2,1)}, bf16[2,2,2,64,1024]{4,3,1,0,2:T(8,128)(2,1)}, u32[]{:S(2)}, u32[]{:S(2)}) collective-permute-start(bf16[2,2,2,64,1024]{4,3,1,0,2:T(8,128)(2,1)} %bitcast.133), channel_id=1, source_target_pairs={{0,2},{2,0},{4,6},{6,4},{8,10},{10,8},{12,14},{14,12},{16,18},{18,... | collective-permute-start | bytes 3145736 | tf_op jit(solution)/shard_map/ppermute | solution.py:86
  51.3 2.3 %collective-permute-start.5 = (bf16[2,2,2,64,1024]{4,3,1,0,2:T(8,128)(2,1)}, bf16[2,2,2,64,1024]{4,3,1,0,2:T(8,128)(2,1)}, u32[]{:S(2)}, u32[]{:S(2)}) collective-permute-start(bf16[2,2,2,64,1024]{4,3,1,0,2:T(8,128)(2,1)} %bitcast.132), channel_id=1, source_target_pairs={{0,4},{2,6},{4,0},{6,2},{8,12},{10,14},{12,8},{14,10},{16,20},{18,... | collective-permute-start | bytes 3145736 | tf_op jit(solution)/shard_map/ppermute | solution.py:86
  53.9 3.9 %fusion.42 = bf16[512,1024]{1,0:T(8,128)(2,1)} fusion(bf16[512,1024]{1,0:T(8,128)(2,1)S(1)} %fusion.28, bf16[544,1024]{1,0:T(8,128)(2,1)S(1)} %get-tuple-element.175, bf16[544,1024]{1,0:T(8,128)(2,1)S(1)} %constant_dynamic-update-slice_fusion, f32[1024]{0:T(1024)S(1)} %bitcast.171, f32[1024]{0:T(1024)S(1)} %bitcast.173, f32[1024]{0:T(1024)S(1)} %bitcast.175, ...), kind=kLoop, calls=%fused_computation.84 | loop fusion | flops 15728640 | bytes 11571712 | tf_op jit(solution)/shard_map/convert_element_type | solution.py:212
  57.7 2.8 %fusion.51 = (f32[1024]{0:T(1024)S(1)}, f32[1024]{0:T(1024)S(1)}, f32[1024]{0:T(1024)S(1)}, f32[1024]{0:T(1024)S(1)}, f32[1024]{0:T(1024)S(1)}, /*index=5*/f32[1...) fusion(bf16[512,1024]{1,0:T(8,128)(2,1)S(1)} %fusion.28, bf16[32,1024]{1,0:T(8,128)(2,1)S(1)} %slice.390, ...), kind=kLoop, calls=%fused_computation.93 | loop fusion | flops 27253760 | bytes 2265088 | tf_op jit(solution)/shard_map/reduce_sum | solution.py:68
  60.6 13.7 %collective-permute-done.4 = bf16[2,2,2,64,1024]{4,3,1,0,2:T(8,128)(2,1)} collective-permute-done((bf16[2,2,2,64,1024]{4,3,1,0,2:T(8,128)(2,1)}, bf16[2,2,2,64,1024]{4,3,1,0,2:T(8,128)(2,1)}, u32[]{:S(2)}, u32[]{:S(2)}) %collective-permute-start.4) | collective-permute-done | bytes 1048608 | tf_op jit(solution)/shard_map/ppermute | solution.py:86
  74.3 1.5 collective-permute-done.5
  75.8 3.1 %add_convert_fusion.2 = (bf16[2,2,2,64,1024]{4,3,1,0,2:T(8,128)(2,1)S(1)}, bf16[2,2,2,64,1024]{4,3,1,0,2:T(8,128)(2,1)S(1)}) fusion(bf16[2,2,2,64,1024]{4,3,1,0,2:T(8,128)(2,1)} %collective-permute-done.5, bf16[2,2,2,64,1024]{4,3,1,0,2:T(8,128)(2,1)} %bitcast.142, bf16[2,2,2,64,1024]{4,3,1,0,2:T(8,128)(2,1)} %collective-permute-done.4, ...), kind=kLoop, calls=%fused_computation.112 | loop fusion | flops 4194304 | bytes 6291456 | tf_op jit(solution)/shard_map/convert_element_type | solution.py:113
  79.0 1.1 dynamic-slice_bitcast_fusion.4
  82.4 3.9 %multiply_convert_fusion = (bf16[512,1024]{1,0:T(8,128)(2,1)}, f32[512,1024]{1,0:T(8,128)}) fusion(bf16[544,1024]{1,0:T(8,128)(2,1)S(1)} %pad_maximum_fusion, f32[1024]{0:T(1024)S(1)} %bitcast.166, f32[1024]{0:T(1024)S(1)} %bitcast.168, f32[1024]{0:T(1024)S(1)} %bitcast.154, f32[1024]{0:T(1024)S(1)} %bitcast.156, f32[1024]{0:T(1024)S(1)} %bitcast.158, ...), kind=kLoop, calls=%fused_computation.114 | loop fusion | flops 18350080 | bytes 12619776 | tf_op jit(solution)/shard_map/convert_element_type | solution.py:171
  86.3 6.8 %fusion.35 = bf16[512,1024]{1,0:T(8,128)(2,1)S(1)} fusion(f32[512,1024]{1,0:T(8,128)} %get-tuple-element.151, bf16[512,2048]{1,0:T(8,128)(2,1)} %all-gather.5.cloned.1.call-done, bf16[2,1024,2048]{2,1,0:T(8,128)(2,1)} %param.13), kind=kOutput, calls=%fused_computation.77 | convolution fusion | flops 2157445120 | bytes 9437184 | tf_op jit(solution)/shard_map/dot_general | solution.py:176
  93.1 2.3 %fusion.67 = (f32[1024]{0:T(1024)S(1)}, f32[1024]{0:T(1024)S(1)}, f32[1024]{0:T(1024)S(1)}, f32[1024]{0:T(1024)S(1)}, f32[1024]{0:T(1024)S(1)}, /*index=5*/f32[1...) fusion(bf16[512,1024]{1,0:T(8,128)(2,1)S(1)} %fusion.35, bf16[544,1024]{1,0:T(8,128)(2,1)S(1)} %pad_maximum_fusion), kind=kLoop, calls=%fused_computation.109 | loop fusion | flops 14670848 | bytes 10522624 | tf_op jit(solution)/shard_map/reduce_sum | solution.py:68
  95.5 1.3 collective-permute-start.7
  96.8 4.8 %collective-permute-start.6 = (bf16[16,1024]{1,0:T(8,128)(2,1)S(1)}, bf16[16,1024]{1,0:T(8,128)(2,1)S(1)}, u32[]{:S(2)}, u32[]{:S(2)}) collective-permute-start(bf16[16,1024]{1,0:T(8,128)(2,1)S(1)} %get-tuple-element.173), channel_id=1, source_target_pairs={{0,2},{2,4},{4,6},{6,8},{8,10},{10,12},{12,14},{14,16},{16,18},{18... | collective-permute-start | bytes 98312 | tf_op jit(solution)/shard_map/ppermute | solution.py:20
  101.6 2.8 %convolution_convert_fusion = bf16[1024,1024]{1,0:T(8,128)(2,1)S(1)} fusion(bf16[512,1024]{1,0:T(8,128)(2,1)} %get-tuple-element.75, bf16[512,2048]{1,0:T(8,128)(2,1)} %all-gather.5.cloned.1.call-done), kind=kOutput, calls=%fused_computation.123 | convolution fusion | flops 1074790400 | bytes 4194304 | tf_op jit(solution)/shard_map/dot_general | solution.py:188
  104.4 1.2 dynamic-slice_bitcast_fusion
  106.7 1.3 convolution_convert_fusion.1
  108.0 1.1 dynamic-slice_bitcast_fusion.1
  109.2 1.2 add_convert_fusion.7
  111.2 1.7 collective-permute-start.11
  113.3 2.4 %fusion.58 = bf16[512,1024]{1,0:T(8,128)(2,1)S(1)} fusion(bf16[512,1024]{1,0:T(8,128)(2,1)S(1)} %fusion.35, bf16[512,1024]{1,0:T(8,128)(2,1)S(1)} %copy-done.2, bf16[528,1024]{1,0:T(8,128)(2,1)S(1)} %get-tuple-element.167, bf16[528,1024]{1,0:T(8,128)(2,1)S(1)} %constant_dynamic-update-slice_fusion.4, f32[1024]{0:T(1024)S(1)} %bitcast.167, ...), kind=kLoop, calls=%fused_computation.100 | loop fusion | flops 15204352 | bytes 11571200 | tf_op jit(solution)/shard_map/convert_element_type | solution.py:212
  117.6 2.6 %collective-permute-start.10 = (f32[23,1024]{1,0:T(8,128)}, f32[23,1024]{1,0:T(8,128)}, u32[]{:S(2)}, u32[]{:S(2)}) collective-permute-start(f32[23,1024]{1,0:T(8,128)} %pad_maximum_fusion.6), channel_id=1, source_target_pairs={{0,16},{2,18},{4,20},{6,22},{8,24},{10,26},{12,28},{14,30},{16,0},... | collective-permute-start | bytes 282632 | tf_op jit(solution)/shard_map/ppermute | solution.py:86
  120.2 1.2 add_convert_fusion.6
  122.8 2.6 %collective-permute-start.14 = (bf16[2,2,2,64,1024]{4,3,2,1,0:T(8,128)(2,1)}, bf16[2,2,2,64,1024]{4,3,2,1,0:T(8,128)(2,1)S(1)}, u32[]{:S(2)}, u32[]{:S(2)}) collective-permute-start(bf16[2,2,2,64,1024]{4,3,2,1,0:T(8,128)(2,1)} %get-tuple-element.156), channel_id=1, source_target_pairs={{0,2},{2,0},{4,6},{6,4},{8,10},{10,8},{12,14},{14,12},{16,18},{18,... | collective-permute-start | bytes 3145736 | tf_op jit(solution)/shard_map/ppermute | solution.py:86
  125.3 1.9 %collective-permute-start.15 = (bf16[2,2,2,64,1024]{4,3,2,1,0:T(8,128)(2,1)S(1)}, bf16[2,2,2,64,1024]{4,3,2,1,0:T(8,128)(2,1)S(1)}, u32[]{:S(2)}, u32[]{:S(2)}) collective-permute-start(bf16[2,2,2,64,1024]{4,3,2,1,0:T(8,128)(2,1)S(1)} %copy-done.8), channel_id=1, source_target_pairs={{0,4},{2,6},{4,0},{6,2},{8,12},{10,14},{12,8},{14,10},{16,20},{18,... | collective-permute-start | bytes 3145736 | tf_op jit(solution)/shard_map/ppermute | solution.py:86
  131.6 2.6 %collective-permute-start.17 = (bf16[64,1024]{1,0:T(8,128)(2,1)S(1)}, bf16[64,1024]{1,0:T(8,128)(2,1)S(1)}, u32[]{:S(2)}, u32[]{:S(2)}) collective-permute-start(bf16[64,1024]{1,0:T(8,128)(2,1)S(1)} %get-tuple-element.190), channel_id=1, source_target_pairs={{0,16},{2,18},{4,20},{6,22},{8,24},{10,26},{12,28},{14,30},{16,0},... | collective-permute-start | bytes 393224 | tf_op jit(solution)/shard_map/ppermute | solution.py:86
  134.7 7.4 %collective-permute-done.13 = f32[23,1024]{1,0:T(8,128)S(1)} collective-permute-done((f32[23,1024]{1,0:T(8,128)S(1)}, f32[23,1024]{1,0:T(8,128)S(1)}, u32[]{:S(2)}, u32[]{:S(2)}) %collective-permute-start.13) | collective-permute-done | bytes 94240 | tf_op jit(solution)/shard_map/ppermute | solution.py:86
  142.1 2.2 %collective-permute-done.14 = bf16[2,2,2,64,1024]{4,3,2,1,0:T(8,128)(2,1)S(1)} collective-permute-done((bf16[2,2,2,64,1024]{4,3,2,1,0:T(8,128)(2,1)}, bf16[2,2,2,64,1024]{4,3,2,1,0:T(8,128)(2,1)S(1)}, u32[]{:S(2)}, u32[]{:S(2)}) %collective-permute-start.14) | collective-permute-done | bytes 1048608 | tf_op jit(solution)/shard_map/ppermute | solution.py:86
  144.3 3.7 %collective-permute-done.15 = bf16[2,2,2,64,1024]{4,3,2,1,0:T(8,128)(2,1)S(1)} collective-permute-done((bf16[2,2,2,64,1024]{4,3,2,1,0:T(8,128)(2,1)S(1)}, bf16[2,2,2,64,1024]{4,3,2,1,0:T(8,128)(2,1)S(1)}, u32[]{:S(2)}, u32[]{:S(2)}) %collective-permute-start.15) | collective-permute-done | bytes 1048608 | tf_op jit(solution)/shard_map/ppermute | solution.py:86
  148.6 2.0 %collective-permute-start.19 = (bf16[2,2,64,1024]{3,2,0,1:T(8,128)(2,1)S(1)}, bf16[2,2,64,1024]{3,2,0,1:T(8,128)(2,1)S(1)}, u32[]{:S(2)}, u32[]{:S(2)}) collective-permute-start(bf16[2,2,64,1024]{3,2,0,1:T(8,128)(2,1)S(1)} %bitcast.150), channel_id=1, source_target_pairs={{0,4},{2,6},{4,0},{6,2},{8,12},{10,14},{12,8},{14,10},{16,20},{18,... | collective-permute-start | bytes 1572872 | tf_op jit(solution)/shard_map/ppermute | solution.py:86
  151.4 8.2 %collective-permute-done.18 = f32[23,1024]{1,0:T(8,128)S(1)} collective-permute-done((f32[23,1024]{1,0:T(8,128)S(1)}, f32[23,1024]{1,0:T(8,128)S(1)}, u32[]{:S(2)}, u32[]{:S(2)}) %collective-permute-start.18) | collective-permute-done | bytes 94240 | tf_op jit(solution)/shard_map/ppermute | solution.py:86
  159.7 1.8 collective-permute-done.20
  162.1 1.9 %collective-permute-start.23 = (bf16[2,64,1024]{2,1,0:T(8,128)(2,1)S(1)}, bf16[2,64,1024]{2,1,0:T(8,128)(2,1)S(1)}, u32[]{:S(2)}, u32[]{:S(2)}) collective-permute-start(bf16[2,64,1024]{2,1,0:T(8,128)(2,1)S(1)} %get-tuple-element.182), channel_id=1, source_target_pairs={{0,8},{2,10},{4,12},{6,14},{8,0},{10,2},{12,4},{14,6},{16,24},{18,... | collective-permute-start | bytes 786440 | tf_op jit(solution)/shard_map/ppermute | solution.py:86
  164.1 4.6 %collective-permute-done.21 = f32[23,1024]{1,0:T(8,128)S(1)} collective-permute-done((f32[23,1024]{1,0:T(8,128)S(1)}, f32[23,1024]{1,0:T(8,128)S(1)}, u32[]{:S(2)}, u32[]{:S(2)}) %collective-permute-start.21) | collective-permute-done | bytes 94240 | tf_op jit(solution)/shard_map/ppermute | solution.py:86
  169.3 4.4 %collective-permute-done.23 = bf16[2,64,1024]{2,1,0:T(8,128)(2,1)S(1)} collective-permute-done((bf16[2,64,1024]{2,1,0:T(8,128)(2,1)S(1)}, bf16[2,64,1024]{2,1,0:T(8,128)(2,1)S(1)}, u32[]{:S(2)}, u32[]{:S(2)}) %collective-permute-start.23) | collective-permute-done | bytes 262176 | tf_op jit(solution)/shard_map/ppermute | solution.py:86
  175.6 2.6 %collective-permute-start.25 = (bf16[64,1024]{1,0:T(8,128)(2,1)S(1)}, bf16[64,1024]{1,0:T(8,128)(2,1)S(1)}, u32[]{:S(2)}, u32[]{:S(2)}) collective-permute-start(bf16[64,1024]{1,0:T(8,128)(2,1)S(1)} %dynamic-slice_bitcast_fusion.16), channel_id=1, source_target_pairs={{0,16},{2,18},{4,20},{6,22},{8,24},{10,26},{12,28},{14,30},{16,0},... | collective-permute-start | bytes 393224 | tf_op jit(solution)/shard_map/ppermute | solution.py:86
  178.4 5.0 %collective-permute-done.24 = bf16[64,1024]{1,0:T(8,128)(2,1)S(1)} collective-permute-done((bf16[64,1024]{1,0:T(8,128)(2,1)S(1)}, bf16[64,1024]{1,0:T(8,128)(2,1)S(1)}, u32[]{:S(2)}, u32[]{:S(2)}) %collective-permute-start.24) | collective-permute-done | bytes 131104 | tf_op jit(solution)/shard_map/ppermute | solution.py:86
  183.4 1.4 collective-permute-done.25
  (161 shorter events, 26.4 us)
Async XLA Ops:
  7.2 5.3 %copy-start = (bf16[5,1024]{1,0:T(8,128)(2,1)S(1)}, bf16[5,1024]{1,0:T(8,128)(2,1)}, u32[]{:S(2)}) copy-start(bf16[5,1024]{1,0:T(8,128)(2,1)} %param.11) | copy-start | bytes 30724
  7.2 4.6 %copy-start.27 = (s32[512]{0:T(512)S(1)}, s32[512]{0:T(512)}, u32[]{:S(2)}) copy-start(s32[512]{0:T(512)} %param.8) | copy-start | bytes 6148
  7.2 20.6 %all-gather.3.cloned.1.call-start = ((), (), s32[]{:S(2)}) async-start(), calls=%async_computation | async-start | bytes 3145728 | tf_op jit(solution)/shard_map/all_gather | solution.py:166
  9.3 3.7 %copy-start.3 = (bf16[512,1024]{1,0:T(8,128)(2,1)S(1)}, bf16[512,1024]{1,0:T(8,128)(2,1)}, u32[]{:S(2)}) copy-start(bf16[512,1024]{1,0:T(8,128)(2,1)} %param.14) | copy-start | bytes 3145732
  9.3 10.5 %copy-start.12 = (bf16[2,9,1024]{2,0,1:T(2,128)(2,1)S(1)}, bf16[2,9,1024]{2,0,1:T(2,128)(2,1)}, u32[]{:S(2)}) copy-start(bf16[2,9,1024]{2,0,1:T(2,128)(2,1)} %param.12) | copy-start | bytes 110596
  11.8 74.5 %all-gather.5.cloned.1.call-start = ((), (), s32[]{:S(2)}) async-start(), calls=%async_computation.1 | async-start | bytes 3145728 | tf_op jit(solution)/shard_map/all_gather | solution.py:166
  13.0 7.6 %collective-permute-start.1 = (bf16[48,1024]{1,0:T(8,128)(2,1)S(1)}, bf16[48,1024]{1,0:T(8,128)(2,1)S(1)}, u32[]{:S(2)}, u32[]{:S(2)}) collective-permute-start(bf16[48,1024]{1,0:T(8,128)(2,1)S(1)} %pad_maximum_fusion.5), channel_id=1, source_target_pairs={{2,0},{4,2},{6,4},{8,6},{10,8},{12,10},{14,12},{16,14},{18,16},{20... | collective-permute-start | bytes 294920 | tf_op jit(solution)/shard_map/ppermute | solution.py:31
  14.3 9.5 %collective-permute-start = (bf16[48,1024]{1,0:T(8,128)(2,1)S(1)}, bf16[48,1024]{1,0:T(8,128)(2,1)S(1)}, u32[]{:S(2)}, u32[]{:S(2)}) collective-permute-start(bf16[48,1024]{1,0:T(8,128)(2,1)S(1)} %pad_maximum_fusion.4), channel_id=1, source_target_pairs={{0,2},{2,4},{4,6},{6,8},{8,10},{10,12},{12,14},{14,16},{16,18},{18... | collective-permute-start | bytes 294920 | tf_op jit(solution)/shard_map/ppermute | solution.py:30
  19.9 62.5 %copy-start.15 = (f32[1,1,1024]{2,0,1:T(1,128)}, f32[1,1,1024]{2,0,1:T(1,128)S(1)}, u32[]{:S(2)}) copy-start(f32[1,1,1024]{2,0,1:T(1,128)S(1)} %get-tuple-element.198) | copy-start | bytes 12292
  19.9 62.5 %copy-start.17 = (f32[1,1,1024]{2,0,1:T(1,128)}, f32[1,1,1024]{2,0,1:T(1,128)S(1)}, u32[]{:S(2)}) copy-start(f32[1,1,1024]{2,0,1:T(1,128)S(1)} %get-tuple-element.199) | copy-start | bytes 12292
  19.9 62.5 %copy-start.19 = (f32[1,1,1024]{2,0,1:T(1,128)}, f32[1,1,1024]{2,0,1:T(1,128)S(1)}, u32[]{:S(2)}) copy-start(f32[1,1,1024]{2,0,1:T(1,128)S(1)} %get-tuple-element.200) | copy-start | bytes 12292
  19.9 62.5 %copy-start.21 = (f32[1,1,1024]{2,0,1:T(1,128)}, f32[1,1,1024]{2,0,1:T(1,128)S(1)}, u32[]{:S(2)}) copy-start(f32[1,1,1024]{2,0,1:T(1,128)S(1)} %get-tuple-element.210) | copy-start | bytes 12292
  19.9 62.5 %copy-start.23 = (f32[1,1,1024]{2,0,1:T(1,128)}, f32[1,1,1024]{2,0,1:T(1,128)S(1)}, u32[]{:S(2)}) copy-start(f32[1,1,1024]{2,0,1:T(1,128)S(1)} %get-tuple-element.211) | copy-start | bytes 12292
  27.8 13.3 %copy-start.10 = (bf16[512,1024]{1,0:T(8,128)(2,1)S(1)}, bf16[512,1024]{1,0:T(8,128)(2,1)}, u32[]{:S(2)}) copy-start(bf16[512,1024]{1,0:T(8,128)(2,1)} %get-tuple-element.63) | copy-start | bytes 3145732
  27.8 13.3 %copy-start.28 = (bf16[512,2048]{1,0:T(8,128)(2,1)S(1)}, bf16[512,2048]{1,0:T(8,128)(2,1)}, u32[]{:S(2)}) copy-start(bf16[512,2048]{1,0:T(8,128)(2,1)} %all-gather.3.cloned.1.call-done) | copy-start | bytes 6291460
  34.7 18.8 %collective-permute-start.3 = (bf16[32,1024]{1,0:T(8,128)(2,1)S(1)}, bf16[32,1024]{1,0:T(8,128)(2,1)S(1)}, u32[]{:S(2)}, u32[]{:S(2)}) collective-permute-start(bf16[32,1024]{1,0:T(8,128)(2,1)S(1)} %get-tuple-element.176), channel_id=1, source_target_pairs={{2,0},{4,2},{6,4},{8,6},{10,8},{12,10},{14,12},{16,14},{18,16},{20... | collective-permute-start | bytes 196616 | tf_op jit(solution)/shard_map/ppermute | solution.py:21
  36.0 17.5 %collective-permute-start.2 = (bf16[32,1024]{1,0:T(8,128)(2,1)S(1)}, bf16[32,1024]{1,0:T(8,128)(2,1)S(1)}, u32[]{:S(2)}, u32[]{:S(2)}) collective-permute-start(bf16[32,1024]{1,0:T(8,128)(2,1)S(1)} %get-tuple-element.177), channel_id=1, source_target_pairs={{0,2},{2,4},{4,6},{6,8},{8,10},{10,12},{12,14},{14,16},{16,18},{18... | collective-permute-start | bytes 196616 | tf_op jit(solution)/shard_map/ppermute | solution.py:20
  48.3 5.5 %copy-start.4 = (bf16[512,1024]{1,0:T(8,128)(2,1)S(1)}, bf16[512,1024]{1,0:T(8,128)(2,1)}, u32[]{:S(2)}) copy-start(bf16[512,1024]{1,0:T(8,128)(2,1)} %param.15) | copy-start | bytes 3145732
  48.3 26.0 %collective-permute-start.4 = (bf16[2,2,2,64,1024]{4,3,1,0,2:T(8,128)(2,1)}, bf16[2,2,2,64,1024]{4,3,1,0,2:T(8,128)(2,1)}, u32[]{:S(2)}, u32[]{:S(2)}) collective-permute-start(bf16[2,2,2,64,1024]{4,3,1,0,2:T(8,128)(2,1)} %bitcast.133), channel_id=1, source_target_pairs={{0,2},{2,0},{4,6},{6,4},{8,10},{10,8},{12,14},{14,12},{16,18},{18,... | collective-permute-start | bytes 3145736 | tf_op jit(solution)/shard_map/ppermute | solution.py:86
  51.3 24.6 %collective-permute-start.5 = (bf16[2,2,2,64,1024]{4,3,1,0,2:T(8,128)(2,1)}, bf16[2,2,2,64,1024]{4,3,1,0,2:T(8,128)(2,1)}, u32[]{:S(2)}, u32[]{:S(2)}) collective-permute-start(bf16[2,2,2,64,1024]{4,3,1,0,2:T(8,128)(2,1)} %bitcast.132), channel_id=1, source_target_pairs={{0,4},{2,6},{4,0},{6,2},{8,12},{10,14},{12,8},{14,10},{16,20},{18,... | collective-permute-start | bytes 3145736 | tf_op jit(solution)/shard_map/ppermute | solution.py:86
  80.1 29.1 %collective-permute-start.9 = (bf16[2,2,64,1024]{3,2,1,0:T(8,128)(2,1)}, bf16[2,2,64,1024]{3,2,1,0:T(8,128)(2,1)}, u32[]{:S(2)}, u32[]{:S(2)}) collective-permute-start(bf16[2,2,64,1024]{3,2,1,0:T(8,128)(2,1)} %get-tuple-element.168), channel_id=1, source_target_pairs={{0,2},{2,0},{4,6},{6,4},{8,10},{10,8},{12,14},{14,12},{16,18},{18,... | collective-permute-start | bytes 1572872 | tf_op jit(solution)/shard_map/ppermute | solution.py:86
  81.4 27.7 %collective-permute-start.8 = (bf16[2,2,64,1024]{3,2,1,0:T(8,128)(2,1)}, bf16[2,2,64,1024]{3,2,1,0:T(8,128)(2,1)}, u32[]{:S(2)}, u32[]{:S(2)}) collective-permute-start(bf16[2,2,64,1024]{3,2,1,0:T(8,128)(2,1)} %get-tuple-element.170), channel_id=1, source_target_pairs={{0,4},{2,6},{4,0},{6,2},{8,12},{10,14},{12,8},{14,10},{16,20},{18,... | collective-permute-start | bytes 1572872 | tf_op jit(solution)/shard_map/ppermute | solution.py:86
  95.5 13.7 %collective-permute-start.7 = (bf16[16,1024]{1,0:T(8,128)(2,1)S(1)}, bf16[16,1024]{1,0:T(8,128)(2,1)S(1)}, u32[]{:S(2)}, u32[]{:S(2)}) collective-permute-start(bf16[16,1024]{1,0:T(8,128)(2,1)S(1)} %get-tuple-element.172), channel_id=1, source_target_pairs={{2,0},{4,2},{6,4},{8,6},{10,8},{12,10},{14,12},{16,14},{18,16},{20... | collective-permute-start | bytes 98312 | tf_op jit(solution)/shard_map/ppermute | solution.py:21
  96.8 12.4 %collective-permute-start.6 = (bf16[16,1024]{1,0:T(8,128)(2,1)S(1)}, bf16[16,1024]{1,0:T(8,128)(2,1)S(1)}, u32[]{:S(2)}, u32[]{:S(2)}) collective-permute-start(bf16[16,1024]{1,0:T(8,128)(2,1)S(1)} %get-tuple-element.173), channel_id=1, source_target_pairs={{0,2},{2,4},{4,6},{6,8},{8,10},{10,12},{12,14},{14,16},{16,18},{18... | collective-permute-start | bytes 98312 | tf_op jit(solution)/shard_map/ppermute | solution.py:20
  110.4 2.8 %copy-start.2 = (bf16[512,1024]{1,0:T(8,128)(2,1)S(1)}, bf16[512,1024]{1,0:T(8,128)(2,1)}, u32[]{:S(2)}) copy-start(bf16[512,1024]{1,0:T(8,128)(2,1)} %fusion.42) | copy-start | bytes 3145732
  110.4 2.8 %copy-start.16 = (f32[1,1,1024]{2,0,1:T(1,128)S(1)}, f32[1,1,1024]{2,0,1:T(1,128)}, u32[]{:S(2)}) copy-start(f32[1,1,1024]{2,0,1:T(1,128)} %copy-done.15) | copy-start | bytes 12292
  111.2 16.9 %collective-permute-start.11 = (bf16[2,64,1024]{2,1,0:T(8,128)(2,1)}, bf16[2,64,1024]{2,1,0:T(8,128)(2,1)}, u32[]{:S(2)}, u32[]{:S(2)}) collective-permute-start(bf16[2,64,1024]{2,1,0:T(8,128)(2,1)} %get-tuple-element.188), channel_id=1, source_target_pairs={{0,8},{2,10},{4,12},{6,14},{8,0},{10,2},{12,4},{14,6},{16,24},{18,... | collective-permute-start | bytes 786440 | tf_op jit(solution)/shard_map/ppermute | solution.py:86
  113.3 3.4 %copy-start.26 = (s32[512]{0:T(512)S(1)}, s32[512]{0:T(512)}, u32[]{:S(2)}) copy-start(s32[512]{0:T(512)} %copy-done.25) | copy-start | bytes 6148
  113.3 6.9 %copy-start.6 = (bf16[2,2,64,1024]{3,2,1,0:T(8,128)(2,1)S(1)}, bf16[2,2,64,1024]{3,2,1,0:T(8,128)(2,1)}, u32[]{:S(2)}) copy-start(bf16[2,2,64,1024]{3,2,1,0:T(8,128)(2,1)} %get-tuple-element.84) | copy-start | bytes 1572868
  116.7 8.6 %copy-start.8 = (bf16[2,2,2,64,1024]{4,3,2,1,0:T(8,128)(2,1)S(1)}, bf16[2,2,2,64,1024]{4,3,2,1,0:T(8,128)(2,1)}, u32[]{:S(2)}) copy-start(bf16[2,2,2,64,1024]{4,3,2,1,0:T(8,128)(2,1)} %get-tuple-element.154) | copy-start | bytes 3145732
  117.6 9.6 %collective-permute-start.10 = (f32[23,1024]{1,0:T(8,128)}, f32[23,1024]{1,0:T(8,128)}, u32[]{:S(2)}, u32[]{:S(2)}) collective-permute-start(f32[23,1024]{1,0:T(8,128)} %pad_maximum_fusion.6), channel_id=1, source_target_pairs={{0,16},{2,18},{4,20},{6,22},{8,24},{10,26},{12,28},{14,30},{16,0},... | collective-permute-start | bytes 282632 | tf_op jit(solution)/shard_map/ppermute | solution.py:86
  122.3 6.7 %collective-permute-start.12 = (bf16[2,64,1024]{2,1,0:T(8,128)(2,1)}, bf16[2,64,1024]{2,1,0:T(8,128)(2,1)}, u32[]{:S(2)}, u32[]{:S(2)}) collective-permute-start(bf16[2,64,1024]{2,1,0:T(8,128)(2,1)} %get-tuple-element.186), channel_id=1, source_target_pairs={{0,8},{2,10},{4,12},{6,14},{8,0},{10,2},{12,4},{14,6},{16,24},{18,... | collective-permute-start | bytes 786440 | tf_op jit(solution)/shard_map/ppermute | solution.py:86
  122.8 21.5 %collective-permute-start.14 = (bf16[2,2,2,64,1024]{4,3,2,1,0:T(8,128)(2,1)}, bf16[2,2,2,64,1024]{4,3,2,1,0:T(8,128)(2,1)S(1)}, u32[]{:S(2)}, u32[]{:S(2)}) collective-permute-start(bf16[2,2,2,64,1024]{4,3,2,1,0:T(8,128)(2,1)} %get-tuple-element.156), channel_id=1, source_target_pairs={{0,2},{2,0},{4,6},{6,4},{8,10},{10,8},{12,14},{14,12},{16,18},{18,... | collective-permute-start | bytes 3145736 | tf_op jit(solution)/shard_map/ppermute | solution.py:86
  125.3 22.7 %collective-permute-start.15 = (bf16[2,2,2,64,1024]{4,3,2,1,0:T(8,128)(2,1)S(1)}, bf16[2,2,2,64,1024]{4,3,2,1,0:T(8,128)(2,1)S(1)}, u32[]{:S(2)}, u32[]{:S(2)}) collective-permute-start(bf16[2,2,2,64,1024]{4,3,2,1,0:T(8,128)(2,1)S(1)} %copy-done.8), channel_id=1, source_target_pairs={{0,4},{2,6},{4,0},{6,2},{8,12},{10,14},{12,8},{14,10},{16,20},{18,... | collective-permute-start | bytes 3145736 | tf_op jit(solution)/shard_map/ppermute | solution.py:86
  130.1 12.0 %collective-permute-start.16 = (bf16[64,1024]{1,0:T(8,128)(2,1)S(1)}, bf16[64,1024]{1,0:T(8,128)(2,1)S(1)}, u32[]{:S(2)}, u32[]{:S(2)}) collective-permute-start(bf16[64,1024]{1,0:T(8,128)(2,1)S(1)} %get-tuple-element.192), channel_id=1, source_target_pairs={{0,16},{2,18},{4,20},{6,22},{8,24},{10,26},{12,28},{14,30},{16,0},... | collective-permute-start | bytes 393224 | tf_op jit(solution)/shard_map/ppermute | solution.py:86
  131.6 10.5 %collective-permute-start.17 = (bf16[64,1024]{1,0:T(8,128)(2,1)S(1)}, bf16[64,1024]{1,0:T(8,128)(2,1)S(1)}, u32[]{:S(2)}, u32[]{:S(2)}) collective-permute-start(bf16[64,1024]{1,0:T(8,128)(2,1)S(1)} %get-tuple-element.190), channel_id=1, source_target_pairs={{0,16},{2,18},{4,20},{6,22},{8,24},{10,26},{12,28},{14,30},{16,0},... | collective-permute-start | bytes 393224 | tf_op jit(solution)/shard_map/ppermute | solution.py:86
  134.2 7.8 %collective-permute-start.13 = (f32[23,1024]{1,0:T(8,128)S(1)}, f32[23,1024]{1,0:T(8,128)S(1)}, u32[]{:S(2)}, u32[]{:S(2)}) collective-permute-start(f32[23,1024]{1,0:T(8,128)S(1)} %fusion.100), channel_id=1, source_target_pairs={{0,8},{2,10},{4,12},{6,14},{8,0},{10,2},{12,4},{14,6},{16,24},{18,... | collective-permute-start | bytes 282632 | tf_op jit(solution)/shard_map/ppermute | solution.py:86
  142.1 5.9 %copy-start.13 = (bf16[64,1024]{1,0:T(8,128)(2,1)}, bf16[64,1024]{1,0:T(8,128)(2,1)S(1)}, u32[]{:S(2)}) copy-start(bf16[64,1024]{1,0:T(8,128)(2,1)S(1)} %collective-permute-done.17) | copy-start | bytes 393220
  148.6 11.1 %collective-permute-start.19 = (bf16[2,2,64,1024]{3,2,0,1:T(8,128)(2,1)S(1)}, bf16[2,2,64,1024]{3,2,0,1:T(8,128)(2,1)S(1)}, u32[]{:S(2)}, u32[]{:S(2)}) collective-permute-start(bf16[2,2,64,1024]{3,2,0,1:T(8,128)(2,1)S(1)} %bitcast.150), channel_id=1, source_target_pairs={{0,4},{2,6},{4,0},{6,2},{8,12},{10,14},{12,8},{14,10},{16,20},{18,... | collective-permute-start | bytes 1572872 | tf_op jit(solution)/shard_map/ppermute | solution.py:86
  151.1 10.3 %collective-permute-start.20 = (bf16[2,2,64,1024]{3,2,0,1:T(8,128)(2,1)S(1)}, bf16[2,2,64,1024]{3,2,0,1:T(8,128)(2,1)S(1)}, u32[]{:S(2)}, u32[]{:S(2)}) collective-permute-start(bf16[2,2,64,1024]{3,2,0,1:T(8,128)(2,1)S(1)} %bitcast.151), channel_id=1, source_target_pairs={{0,2},{2,0},{4,6},{6,4},{8,10},{10,8},{12,14},{14,12},{16,18},{18,... | collective-permute-start | bytes 1572872 | tf_op jit(solution)/shard_map/ppermute | solution.py:86
  151.2 8.4 %collective-permute-start.18 = (f32[23,1024]{1,0:T(8,128)S(1)}, f32[23,1024]{1,0:T(8,128)S(1)}, u32[]{:S(2)}, u32[]{:S(2)}) collective-permute-start(f32[23,1024]{1,0:T(8,128)S(1)} %add.314), channel_id=1, source_target_pairs={{0,4},{2,6},{4,0},{6,2},{8,12},{10,14},{12,8},{14,10},{16,20},{18,... | collective-permute-start | bytes 282632 | tf_op jit(solution)/shard_map/ppermute | solution.py:86
  161.7 7.7 %collective-permute-start.22 = (bf16[2,64,1024]{2,1,0:T(8,128)(2,1)S(1)}, bf16[2,64,1024]{2,1,0:T(8,128)(2,1)S(1)}, u32[]{:S(2)}, u32[]{:S(2)}) collective-permute-start(bf16[2,64,1024]{2,1,0:T(8,128)(2,1)S(1)} %get-tuple-element.184), channel_id=1, source_target_pairs={{0,8},{2,10},{4,12},{6,14},{8,0},{10,2},{12,4},{14,6},{16,24},{18,... | collective-permute-start | bytes 786440 | tf_op jit(solution)/shard_map/ppermute | solution.py:86
  162.1 16.2 %copy-start.14 = (bf16[64,1024]{1,0:T(8,128)(2,1)S(1)}, bf16[64,1024]{1,0:T(8,128)(2,1)}, u32[]{:S(2)}) copy-start(bf16[64,1024]{1,0:T(8,128)(2,1)} %copy-done.13) | copy-start | bytes 393220
  162.1 11.6 %collective-permute-start.23 = (bf16[2,64,1024]{2,1,0:T(8,128)(2,1)S(1)}, bf16[2,64,1024]{2,1,0:T(8,128)(2,1)S(1)}, u32[]{:S(2)}, u32[]{:S(2)}) collective-permute-start(bf16[2,64,1024]{2,1,0:T(8,128)(2,1)S(1)} %get-tuple-element.182), channel_id=1, source_target_pairs={{0,8},{2,10},{4,12},{6,14},{8,0},{10,2},{12,4},{14,6},{16,24},{18,... | collective-permute-start | bytes 786440 | tf_op jit(solution)/shard_map/ppermute | solution.py:86
  164.1 4.6 %collective-permute-start.21 = (f32[23,1024]{1,0:T(8,128)S(1)}, f32[23,1024]{1,0:T(8,128)S(1)}, u32[]{:S(2)}, u32[]{:S(2)}) collective-permute-start(f32[23,1024]{1,0:T(8,128)S(1)} %add.319), channel_id=1, source_target_pairs={{0,2},{2,0},{4,6},{6,4},{8,10},{10,8},{12,14},{14,12},{16,18},{18,... | collective-permute-start | bytes 282632 | tf_op jit(solution)/shard_map/ppermute | solution.py:86
  175.1 8.3 %collective-permute-start.24 = (bf16[64,1024]{1,0:T(8,128)(2,1)S(1)}, bf16[64,1024]{1,0:T(8,128)(2,1)S(1)}, u32[]{:S(2)}, u32[]{:S(2)}) collective-permute-start(bf16[64,1024]{1,0:T(8,128)(2,1)S(1)} %dynamic-slice_bitcast_fusion.17), channel_id=1, source_target_pairs={{0,16},{2,18},{4,20},{6,22},{8,24},{10,26},{12,28},{14,30},{16,0},... | collective-permute-start | bytes 393224 | tf_op jit(solution)/shard_map/ppermute | solution.py:86
  175.6 9.2 %collective-permute-start.25 = (bf16[64,1024]{1,0:T(8,128)(2,1)S(1)}, bf16[64,1024]{1,0:T(8,128)(2,1)S(1)}, u32[]{:S(2)}, u32[]{:S(2)}) collective-permute-start(bf16[64,1024]{1,0:T(8,128)(2,1)S(1)} %dynamic-slice_bitcast_fusion.16), channel_id=1, source_target_pairs={{0,16},{2,18},{4,20},{6,22},{8,24},{10,26},{12,28},{14,30},{16,0},... | collective-permute-start | bytes 393224 | tf_op jit(solution)/shard_map/ppermute | solution.py:86
  178.3 7.7 %copy-start.1 = (bf16[5,1024]{1,0:T(8,128)(2,1)S(1)}, bf16[5,1024]{1,0:T(8,128)(2,1)}, u32[]{:S(2)}) copy-start(bf16[5,1024]{1,0:T(8,128)(2,1)} %param.11) | copy-start | bytes 30724
  (10 other events, 18.5 us)
Sparse Core Ops, SparseCore 0:
  11.9 13.2 all-gather.2
  57.9 10.3 all-gather.4

commit v4 on v3

--- a/solution.py
+++ b/solution.py
@@ -90,16 +90,15 @@
     return part.reshape((2,) * bits + (part.shape[0] >> bits, part.shape[1]))
 
 
-def halves_of(parts, orders, step):
+def halves_of(arrays, order, step):
+    bit = order[step]
+    dim = sorted(order[step:], reverse=True).index(bit)
+    mine = (lax.axis_index("seq") >> bit) & 1
     halves = []
-    for part, order in zip(parts, orders):
-        bit = order[step]
-        dim = sorted(order[step:], reverse=True).index(bit)
-        mine = (lax.axis_index("seq") >> bit) & 1
-        send = lax.dynamic_index_in_dim(part, 1 - mine, dim, keepdims=False)
-        keep = lax.dynamic_index_in_dim(part, mine, dim, keepdims=False)
-        halves.append((keep, send))
-    return halves
+    for index in (mine, 1 - mine):
+        cut = [lax.dynamic_index_in_dim(cells, index, dim, keepdims=False) for cells in arrays]
+        halves.append(cut[0] if len(cut) == 1 else added(*cut, False))
+    return tuple(halves)
 
 
 def swapped(halves, orders, step):
@@ -113,19 +112,10 @@
     return total if last else total.astype(jnp.bfloat16)
 
 
-def next_halves(pairs, orders, step):
-    return halves_of([added(keep, arrived, False) for keep, arrived in pairs], orders, step)
-
-
-def kept_with(value, pairs):
-    kept = [keep for keep, arrived in pairs]
-    value, kept = lax.optimization_barrier((value, kept))
-    return (value, [(keep, arrived) for keep, (_, arrived) in zip(kept, pairs)])
-
-
 def later_steps(pairs, orders, steps):
     for step in steps:
-        pairs = swapped(next_halves(pairs, orders, step), orders, step)
+        halves = [halves_of(pair, order, step) for pair, order in zip(pairs, orders)]
+        pairs = swapped(halves, orders, step)
     return pairs
 
 
@@ -164,15 +154,11 @@
         padded_in = padded_inputs[block_number]
         kernel = conv_kernel[block_number]
         column_piece = lax.all_gather(upstream, "blk", axis=1, tiled=True)
-        if earlier is not None:
-            padded_in, earlier = lax.optimization_barrier((padded_in, earlier))
         pre_act = tap_sum(padded_in, kernel, tap_spacing, row_count, False)
         activation, derivative = gelu_pair(pre_act)
         act_half = activation.astype(jnp.bfloat16)
         if earlier is not None:
-            halves = next_halves(earlier, orders, 1)
-            earlier = swapped(halves, orders, 1)
-            column_piece, earlier = kept_with(column_piece, earlier)
+            column_piece, earlier = lax.optimization_barrier((column_piece, earlier))
         grad_held = lax.dot_general(
             column_piece,
             mix_weight[block_number],
@@ -181,7 +167,11 @@
         )
         grad_pre = (grad_held * derivative).astype(jnp.bfloat16)
         edges = edge_rows(grad_pre, reach_rows)
-        act_half, grad_pre = lax.optimization_barrier((act_half, grad_pre))
+        if earlier is None:
+            act_half, grad_pre = lax.optimization_barrier((act_half, grad_pre))
+        else:
+            act_half, grad_pre, earlier = lax.optimization_barrier((act_half, grad_pre, earlier))
+            earlier = later_steps(earlier, orders, range(1, 2))
         width = column_piece.shape[1] // len(orders)
         parts = [
             split_rows(
@@ -195,13 +185,10 @@
             )
             for chunk in range(len(orders))
         ]
-        halves = halves_of(parts, orders, 0)
-        pairs = swapped(halves, orders, 0)
-        edges, pairs = kept_with(edges, pairs)
-        if earlier is not None:
-            edges, earlier = lax.optimization_barrier((edges, earlier))
-        if earlier is not None:
-            earlier = later_steps(earlier, orders, range(2, 3))
+        edges, parts = lax.optimization_barrier((edges, parts))
+        pairs = swapped([halves_of([part], order, 0) for part, order in zip(parts, orders)], orders, 0)
+        kept, edges = lax.optimization_barrier(([keep for keep, _ in pairs], edges))
+        pairs = [(keep, arrived) for keep, (_, arrived) in zip(kept, pairs)]
         kernel_parts[block_number] = (
             tap_products(grad_pre, padded_in, tap_spacing, tap_count) * grad_scale
         )
@@ -214,14 +201,15 @@
             earlier = pairs
     embed_part = jnp.dot(one_hot, upstream, preferred_element_type=jnp.float32) * grad_scale
     sums = jnp.concatenate(kernel_parts + [embed_part])
+    sums, pairs, earlier = lax.optimization_barrier((sums, pairs, earlier))
+    earlier = later_steps(earlier, orders, range(2, 3))
+    pairs = later_steps(pairs, orders, range(1, 2))
     for step in range(steps):
         sums = sums + exchanged(sums, "seq", steps - 1 - step)
-        if step == 0:
-            sums, earlier = lax.optimization_barrier((sums, earlier))
-            earlier = later_steps(earlier, orders, range(3, steps))
-        elif step < 4:
+        if step < 2:
             sums, pairs, earlier = lax.optimization_barrier((sums, pairs, earlier))
-            pairs = later_steps(pairs, orders, range(step, step + 1 if step < 3 else steps))
+            pairs = later_steps(pairs, orders, range(2, 3) if step == 0 else range(3, steps))
+            earlier = later_steps(earlier, orders, range(3, steps) if step == 0 else ())
     weight_parts = [finished(pairs, grad_scale), finished(earlier, grad_scale)]
     weight_grad = jnp.stack(weight_parts)
     kernel_grad = sums[: block_count * tap_count].reshape(block_count, tap_count, -1)

time: 193 us -> 203 us (1.052)
  waiting for transfers between devices: 59.2 us -> 65.2 us
    squeeze x12 -> x0, local copies, waits for them, and re-layouts: 6.34 us -> none  [halves_of(): send = lax.dynamic_index_in_dim(part, 1 - mine, dim, keepdims=False)]
    ppermute x20, waiting for transfers between devices: 55.2 us -> 61.2 us  [exchanged(): return lax.ppermute(cells, axis, [(i, i ^ 1 << bit) for i in range(count)])]
    dynamic_slice x12, local copies, waits for them, and re-layouts: 4.97 us -> 10.3 us  [halves_of(): lax.dynamic_index_in_dim(cells, index, dim, keepdims=False)]
    convert_element_type x11 -> x12, other arithmetic: 9.04 us -> 12 us  [added(): return total if last else total.astype(jnp.bfloat16)]
    unnamed x65 -> x45, local copies, waits for them, and re-layouts: 4.06 us -> 4.43 us
  transfers between devices with their start and end apart: 28 -> 28, of which waited for: 15 -> 11; matrix products, arithmetic and copies ran while one was open for 28% -> 17% of each run, Pallas kernels for 0% -> 0%
where the time goes in v4:
time: 203 us; the launch traced here: 202 us
  waiting for transfers between devices  65.2 us (32%)
  starting transfers between devices  47.3 us (23%)
  other arithmetic  36.9 us (18%)
  matrix products  22.4 us (11%)
  local copies, waits for them, and re-layouts  15.5 us (8%)
  between operations  14.7 us (7%)
    ppermute x20, waiting for transfers between devices, exchanged(): return lax.ppermute(cells, axis, [(i, i ^ 1 << bit) for i in range(count)])  61.2 us
    ppermute x20, starting transfers between devices, exchanged(): return lax.ppermute(cells, axis, [(i, i ^ 1 << bit) for i in range(count)])  28.1 us
    dot_general x2, matrix products, on_device(): lax.dot_general(column_piece, mix_weight[block_number], (((1,), (1,)), ((...  13.8 us
    convert_element_type x12, other arithmetic, added(): return total if last else total.astype(jnp.bfloat16)  12 us
    dynamic_slice x12, local copies, waits for them, and re-layouts, halves_of(): lax.dynamic_index_in_dim(cells, index, dim, keepdims=False)  10.3 us
    ppermute x2, starting transfers between devices, edge_rows(): lax.ppermute(cells[-width:], 'seq', [(i, (i + 1) % count) for i in range(...  9.61 us
    dot_general x4, matrix products, on_device(): lax.dot_general(act_half, lax.slice_in_dim(column_piece, chunk * width, (...  7.82 us
    convert_element_type x2, other arithmetic, on_device(): act_half = activation.astype(jnp.bfloat16)  7.72 us
  transfers between devices with their start and end apart: 28, of which 11 were waited for; matrix products, arithmetic and copies ran while one was open for 17% of the time, Pallas kernels for 0%

profile of v4, /device:TPU:0, one launch (start us, length us, event | category | flops | bytes accessed | tf_op | source)
XLA Modules:
  0.0 202.0 jit_solution(17147752654613040620)
XLA Ops:
  8.0 1.3 and_reduce_fusion
  9.3 2.4 %broadcast_select_fusion = bf16[512,1024]{1,0:T(8,128)(2,1)} fusion(bf16[512,1024]{1,0:T(8,128)(2,1)} %param.15, pred[512]{0:T(512)(128)(4,1)S(1)} %and_reduce_fusion), kind=kLoop, calls=%fused_computation.168 | loop fusion | flops 524288 | bytes 2097664 | tf_op jit(solution)/shard_map/jit(_where)/select_n | solution.py:148
  12.4 1.3 collective-permute-start.1
  13.8 5.5 %collective-permute-start = (bf16[48,1024]{1,0:T(8,128)(2,1)S(1)}, bf16[48,1024]{1,0:T(8,128)(2,1)S(1)}, u32[]{:S(2)}, u32[]{:S(2)}) collective-permute-start(bf16[48,1024]{1,0:T(8,128)(2,1)S(1)} %pad_maximum_fusion.5), channel_id=1, source_target_pairs={{0,2},{2,4},{4,6},{6,8},{8,10},{10,12},{12,14},{14,16},{16,18},{18... | collective-permute-start | bytes 294920 | tf_op jit(solution)/shard_map/ppermute | solution.py:30
  20.1 3.2 %collective-permute-done = bf16[48,1024]{1,0:T(8,128)(2,1)S(1)} collective-permute-done((bf16[48,1024]{1,0:T(8,128)(2,1)S(1)}, bf16[48,1024]{1,0:T(8,128)(2,1)S(1)}, u32[]{:S(2)}, u32[]{:S(2)}) %collective-permute-start) | collective-permute-done | bytes 98336 | tf_op jit(solution)/shard_map/ppermute | solution.py:30
  23.3 3.8 %multiply_convert_fusion.1 = (bf16[512,1024]{1,0:T(8,128)(2,1)}, f32[512,1024]{1,0:T(8,128)}) fusion(bf16[32,1024]{1,0:T(8,128)(2,1)S(1)} %slice.393, bf16[512,1024]{1,0:T(8,128)(2,1)S(1)} %copy-done.3, f32[1024]{0:T(1024)S(1)} %bitcast.176, f32[1024]{0:T(1024)S(1)} %bitcast.178, f32[1024]{0:T(1024)S(1)} %bitcast.180, f32[1024]{0:T(1024)S(1)} %bitcast.182, ...), kind=kLoop, calls=%fused_computation.111 | loop fusion | flops 30932992 | bytes 4362240 | tf_op jit(solution)/shard_map/convert_element_type | solution.py:159
  27.1 6.9 %fusion.28 = bf16[512,1024]{1,0:T(8,128)(2,1)S(1)} fusion(f32[512,1024]{1,0:T(8,128)} %get-tuple-element.151, bf16[512,2048]{1,0:T(8,128)(2,1)} %all-gather.3.cloned.1.call-done, bf16[2,1024,2048]{2,1,0:T(8,128)(2,1)} %param.13), kind=kOutput, calls=%fused_computation.70 | convolution fusion | flops 2157445120 | bytes 9437184 | tf_op jit(solution)/shard_map/dot_general | solution.py:162
  34.0 1.3 collective-permute-start.3
  35.3 5.1 %collective-permute-start.2 = (bf16[32,1024]{1,0:T(8,128)(2,1)S(1)}, bf16[32,1024]{1,0:T(8,128)(2,1)S(1)}, u32[]{:S(2)}, u32[]{:S(2)}) collective-permute-start(bf16[32,1024]{1,0:T(8,128)(2,1)S(1)} %get-tuple-element.185), channel_id=1, source_target_pairs={{0,2},{2,4},{4,6},{6,8},{8,10},{10,12},{12,14},{14,16},{16,18},{18... | collective-permute-start | bytes 196616 | tf_op jit(solution)/shard_map/ppermute | solution.py:20
  40.4 1.3 convolution_convert_fusion.2
  41.7 1.3 convolution_convert_fusion.3
  48.7 3.6 %fusion.42 = bf16[512,1024]{1,0:T(8,128)(2,1)} fusion(bf16[512,1024]{1,0:T(8,128)(2,1)S(1)} %fusion.28, bf16[544,1024]{1,0:T(8,128)(2,1)S(1)} %get-tuple-element.183, bf16[544,1024]{1,0:T(8,128)(2,1)S(1)} %constant_dynamic-update-slice_fusion, f32[1024]{0:T(1024)S(1)} %bitcast.177, f32[1024]{0:T(1024)S(1)} %bitcast.179, f32[1024]{0:T(1024)S(1)} %bitcast.181, ...), kind=kLoop, calls=%fused_computation.84 | loop fusion | flops 15728640 | bytes 11571712 | tf_op jit(solution)/shard_map/convert_element_type | solution.py:199
  52.4 2.4 %copy.51 = bf16[2,2,2,1,64,1024]{5,4,0,1,2,3:T(8,128)(2,1)} copy(bf16[2,2,2,1,64,1024]{5,4,3,2,1,0:T(8,128)(2,1)} %get-tuple-element.168) | data formatting | bytes 2097152 | tf_op jit(solution)/shard_map/jit(dynamic_index_in_dim)/dynamic_slice | solution.py:99
  54.8 2.9 %collective-permute-start.4 = (bf16[2,2,2,64,1024]{4,3,0,1,2:T(8,128)(2,1)}, bf16[2,2,2,64,1024]{4,3,0,1,2:T(8,128)(2,1)}, u32[]{:S(2)}, u32[]{:S(2)}) collective-permute-start(bf16[2,2,2,64,1024]{4,3,0,1,2:T(8,128)(2,1)} %bitcast.141), channel_id=1, source_target_pairs={{0,2},{2,0},{4,6},{6,4},{8,10},{10,8},{12,14},{14,12},{16,18},{18,... | collective-permute-start | bytes 3145736 | tf_op jit(solution)/shard_map/ppermute | solution.py:86
  58.8 2.3 %collective-permute-start.5 = (bf16[2,2,2,64,1024]{4,3,0,1,2:T(8,128)(2,1)}, bf16[2,2,2,64,1024]{4,3,0,1,2:T(8,128)(2,1)}, u32[]{:S(2)}, u32[]{:S(2)}) collective-permute-start(bf16[2,2,2,64,1024]{4,3,0,1,2:T(8,128)(2,1)} %bitcast.140), channel_id=1, source_target_pairs={{0,4},{2,6},{4,0},{6,2},{8,12},{10,14},{12,8},{14,10},{16,20},{18,... | collective-permute-start | bytes 3145736 | tf_op jit(solution)/shard_map/ppermute | solution.py:86
  61.1 3.9 %multiply_convert_fusion = (bf16[512,1024]{1,0:T(8,128)(2,1)}, f32[512,1024]{1,0:T(8,128)}) fusion(bf16[16,1024]{1,0:T(8,128)(2,1)S(1)} %slice.419, bf16[512,1024]{1,0:T(8,128)(2,1)S(1)} %convolution_convert_fusion.4, f32[1024]{0:T(1024)S(1)} %bitcast.170, f32[1024]{0:T(1024)S(1)} %bitcast.172, f32[1024]{0:T(1024)S(1)} %bitcast.156, f32[1024]{0:T(1024)S(1)} %bitcast.158, ...), kind=kLoop, calls=%fused_computation.110 | loop fusion | flops 30932992 | bytes 4296704 | tf_op jit(solution)/shard_map/convert_element_type | solution.py:159
  65.0 2.8 %fusion.51 = (f32[1024]{0:T(1024)S(1)}, f32[1024]{0:T(1024)S(1)}, f32[1024]{0:T(1024)S(1)}, f32[1024]{0:T(1024)S(1)}, f32[1024]{0:T(1024)S(1)}, /*index=5*/f32[1...) fusion(bf16[512,1024]{1,0:T(8,128)(2,1)S(1)} %fusion.28, bf16[32,1024]{1,0:T(8,128)(2,1)S(1)} %slice.393, ...), kind=kLoop, calls=%fused_computation.93 | loop fusion | flops 27253760 | bytes 2265088 | tf_op jit(solution)/shard_map/reduce_sum | solution.py:68
  67.9 12.9 %collective-permute-done.4 = bf16[2,2,2,64,1024]{4,3,0,1,2:T(8,128)(2,1)} collective-permute-done((bf16[2,2,2,64,1024]{4,3,0,1,2:T(8,128)(2,1)}, bf16[2,2,2,64,1024]{4,3,0,1,2:T(8,128)(2,1)}, u32[]{:S(2)}, u32[]{:S(2)}) %collective-permute-start.4) | collective-permute-done | bytes 1048608 | tf_op jit(solution)/shard_map/ppermute | solution.py:86
  80.8 2.6 %collective-permute-done.5 = bf16[2,2,2,64,1024]{4,3,0,1,2:T(8,128)(2,1)} collective-permute-done((bf16[2,2,2,64,1024]{4,3,0,1,2:T(8,128)(2,1)}, bf16[2,2,2,64,1024]{4,3,0,1,2:T(8,128)(2,1)}, u32[]{:S(2)}, u32[]{:S(2)}) %collective-permute-start.5) | collective-permute-done | bytes 1048608 | tf_op jit(solution)/shard_map/ppermute | solution.py:86
  83.4 6.9 %fusion.35 = bf16[512,1024]{1,0:T(8,128)(2,1)S(1)} fusion(f32[512,1024]{1,0:T(8,128)} %get-tuple-element.153, bf16[512,2048]{1,0:T(8,128)(2,1)} %all-gather.5.cloned.1.call-done, bf16[2,1024,2048]{2,1,0:T(8,128)(2,1)} %param.13), kind=kOutput, calls=%fused_computation.77 | convolution fusion | flops 2157445120 | bytes 9437184 | tf_op jit(solution)/shard_map/dot_general | solution.py:162
  90.3 2.6 %convolution_convert_fusion = bf16[1024,1024]{1,0:T(8,128)(2,1)} fusion(bf16[512,1024]{1,0:T(8,128)(2,1)S(1)} %copy-done.10, bf16[512,2048]{1,0:T(8,128)(2,1)S(1)} %copy-done.19), kind=kOutput, calls=%fused_computation.119 | convolution fusion | flops 1074790400 | bytes 4194304 | tf_op jit(solution)/shard_map/dot_general | solution.py:178
  93.0 2.6 %convolution_convert_fusion.1 = bf16[1024,1024]{1,0:T(8,128)(2,1)} fusion(bf16[512,1024]{1,0:T(8,128)(2,1)S(1)} %copy-done.10, bf16[512,2048]{1,0:T(8,128)(2,1)S(1)} %copy-done.19), kind=kOutput, calls=%fused_computation.120 | convolution fusion | flops 1074790400 | bytes 4194304 | tf_op jit(solution)/shard_map/dot_general | solution.py:178
  95.6 2.4 %fusion.67 = (f32[1024]{0:T(1024)S(1)}, f32[1024]{0:T(1024)S(1)}, f32[1024]{0:T(1024)S(1)}, f32[1024]{0:T(1024)S(1)}, f32[1024]{0:T(1024)S(1)}, /*index=5*/f32[1...) fusion(bf16[512,1024]{1,0:T(8,128)(2,1)S(1)} %fusion.35, bf16[16,1024]{1,0:T(8,128)(2,1)S(1)} %slice.419, ...), kind=kLoop, calls=%fused_computation.109 | loop fusion | flops 27253760 | bytes 2199552 | tf_op jit(solution)/shard_map/reduce_sum | solution.py:68
  98.0 1.4 collective-permute-start.7
  99.5 4.5 %collective-permute-start.6 = (bf16[16,1024]{1,0:T(8,128)(2,1)S(1)}, bf16[16,1024]{1,0:T(8,128)(2,1)S(1)}, u32[]{:S(2)}, u32[]{:S(2)}) collective-permute-start(bf16[16,1024]{1,0:T(8,128)(2,1)S(1)} %get-tuple-element.181), channel_id=1, source_target_pairs={{0,2},{2,4},{4,6},{6,8},{8,10},{10,12},{12,14},{14,16},{16,18},{18... | collective-permute-start | bytes 98312 | tf_op jit(solution)/shard_map/ppermute | solution.py:20
  104.0 2.4 %fusion.89 = (bf16[2,2,64,1024]{3,2,0,1:T(8,128)(2,1)}, bf16[2,2,64,1024]{3,2,0,1:T(8,128)(2,1)S(1)}) fusion(bf16[2,2,2,64,1024]{4,3,0,1,2:T(8,128)(2,1)} %collective-permute-done.4, s32[]{:T(128)S(6)} %select_n.90, bf16[2,2,2,64,1024]{4,3,0,1,2:T(8,128)(2,1)S(1)} %bitcast.146, s32[]{:T(128)S(6)} %select_n.88), kind=kLoop, calls=%fused_computation.170 | loop fusion | flops 2097152 | bytes 3145736 | tf_op jit(solution)/shard_map/convert_element_type | solution.py:112
  107.4 2.4 %fusion.91 = (bf16[2,2,64,1024]{3,2,0,1:T(8,128)(2,1)}, bf16[2,2,64,1024]{3,2,0,1:T(8,128)(2,1)S(1)}) fusion(bf16[2,2,2,64,1024]{4,3,0,1,2:T(8,128)(2,1)} %collective-permute-done.5, s32[]{:T(128)S(6)} %select_n.89, bf16[2,2,2,64,1024]{4,3,0,1,2:T(8,128)(2,1)S(1)} %bitcast.145, s32[]{:T(128)S(6)} %select_n.87), kind=kLoop, calls=%fused_computation.172 | loop fusion | flops 2097152 | bytes 3145736 | tf_op jit(solution)/shard_map/convert_element_type | solution.py:112
  109.8 3.0 %collective-permute-start.11 = (bf16[2,2,64,1024]{3,2,0,1:T(8,128)(2,1)}, bf16[2,2,64,1024]{3,2,0,1:T(8,128)(2,1)}, u32[]{:S(2)}, u32[]{:S(2)}) collective-permute-start(bf16[2,2,64,1024]{3,2,0,1:T(8,128)(2,1)} %get-tuple-element.158), channel_id=1, source_target_pairs={{0,2},{2,0},{4,6},{6,4},{8,10},{10,8},{12,14},{14,12},{16,18},{18,... | collective-permute-start | bytes 1572872 | tf_op jit(solution)/shard_map/ppermute | solution.py:86
  112.9 1.8 constant_dynamic-slice_fusion.1
  115.0 1.3 copy-done.9
  118.0 2.3 %fusion.58 = bf16[512,1024]{1,0:T(8,128)(2,1)S(1)} fusion(bf16[512,1024]{1,0:T(8,128)(2,1)S(1)} %fusion.35, bf16[512,1024]{1,0:T(8,128)(2,1)S(1)} %copy-done.2, bf16[528,1024]{1,0:T(8,128)(2,1)S(1)} %get-tuple-element.179, bf16[528,1024]{1,0:T(8,128)(2,1)S(1)} %constant_dynamic-update-slice_fusion.4, f32[1024]{0:T(1024)S(1)} %bitcast.171, ...), kind=kLoop, calls=%fused_computation.100 | loop fusion | flops 15204352 | bytes 11571200 | tf_op jit(solution)/shard_map/convert_element_type | solution.py:199
  120.6 5.3 %collective-permute-done.11 = bf16[2,2,64,1024]{3,2,0,1:T(8,128)(2,1)} collective-permute-done((bf16[2,2,64,1024]{3,2,0,1:T(8,128)(2,1)}, bf16[2,2,64,1024]{3,2,0,1:T(8,128)(2,1)}, u32[]{:S(2)}, u32[]{:S(2)}) %collective-permute-start.11) | collective-permute-done | bytes 524320 | tf_op jit(solution)/shard_map/ppermute | solution.py:86
  126.0 18.1 %collective-permute-done.8 = bf16[2,2,2,64,1024]{4,3,0,1,2:T(8,128)(2,1)S(1)} collective-permute-done((bf16[2,2,2,64,1024]{4,3,0,1,2:T(8,128)(2,1)S(1)}, bf16[2,2,2,64,1024]{4,3,0,1,2:T(8,128)(2,1)S(1)}, u32[]{:S(2)}, u32[]{:S(2)}) %collective-permute-start.8) | collective-permute-done | bytes 1048608 | tf_op jit(solution)/shard_map/ppermute | solution.py:86
  146.9 1.6 collective-permute-start.14
  149.8 1.5 collective-permute-start.15
  151.2 1.9 fusion.99
  153.8 2.4 %collective-permute-start.12 = (f32[23,1024]{1,0:T(8,128)S(1)}, f32[23,1024]{1,0:T(8,128)S(1)}, u32[]{:S(2)}, u32[]{:S(2)}) collective-permute-start(f32[23,1024]{1,0:T(8,128)S(1)} %pad_maximum_fusion.7), channel_id=1, source_target_pairs={{0,16},{2,18},{4,20},{6,22},{8,24},{10,26},{12,28},{14,30},{16,0},... | collective-permute-start | bytes 282632 | tf_op jit(solution)/shard_map/ppermute | solution.py:86
  156.2 5.7 %collective-permute-done.12 = f32[23,1024]{1,0:T(8,128)S(1)} collective-permute-done((f32[23,1024]{1,0:T(8,128)S(1)}, f32[23,1024]{1,0:T(8,128)S(1)}, u32[]{:S(2)}, u32[]{:S(2)}) %collective-permute-start.12) | collective-permute-done | bytes 94240 | tf_op jit(solution)/shard_map/ppermute | solution.py:86
  161.9 2.2 %collective-permute-done.16 = bf16[2,64,1024]{2,1,0:T(8,128)(2,1)S(1)} collective-permute-done((bf16[2,64,1024]{2,1,0:T(8,128)(2,1)}, bf16[2,64,1024]{2,1,0:T(8,128)(2,1)S(1)}, u32[]{:S(2)}, u32[]{:S(2)}) %collective-permute-start.16) | collective-permute-done | bytes 262176 | tf_op jit(solution)/shard_map/ppermute | solution.py:86
  164.3 1.9 collective-permute-start.18
  167.8 1.3 collective-permute-start.20
  169.2 1.8 collective-permute-start.21
  170.9 1.8 collective-permute-start.17
  172.7 7.6 %collective-permute-done.17 = f32[23,1024]{1,0:T(8,128)S(1)} collective-permute-done((f32[23,1024]{1,0:T(8,128)S(1)}, f32[23,1024]{1,0:T(8,128)S(1)}, u32[]{:S(2)}, u32[]{:S(2)}) %collective-permute-start.17) | collective-permute-done | bytes 94240 | tf_op jit(solution)/shard_map/ppermute | solution.py:86
  180.4 1.5 collective-permute-start.24
  182.0 2.4 %collective-permute-start.23 = (bf16[64,1024]{1,0:T(8,128)(2,1)S(1)}, bf16[64,1024]{1,0:T(8,128)(2,1)S(1)}, u32[]{:S(2)}, u32[]{:S(2)}) collective-permute-start(bf16[64,1024]{1,0:T(8,128)(2,1)S(1)} %fusion.113), channel_id=1, source_target_pairs={{0,16},{2,18},{4,20},{6,22},{8,24},{10,26},{12,28},{14,30},{16,0},... | collective-permute-start | bytes 393224 | tf_op jit(solution)/shard_map/ppermute | solution.py:86
  185.9 5.3 %collective-permute-done.23 = bf16[64,1024]{1,0:T(8,128)(2,1)S(1)} collective-permute-done((bf16[64,1024]{1,0:T(8,128)(2,1)S(1)}, bf16[64,1024]{1,0:T(8,128)(2,1)S(1)}, u32[]{:S(2)}, u32[]{:S(2)}) %collective-permute-start.23) | collective-permute-done | bytes 131104 | tf_op jit(solution)/shard_map/ppermute | solution.py:86
  191.2 1.4 collective-permute-done.22
  (128 shorter events, 22.8 us)
Async XLA Ops:
  7.2 4.7 %copy-start = (bf16[5,1024]{1,0:T(8,128)(2,1)S(1)}, bf16[5,1024]{1,0:T(8,128)(2,1)}, u32[]{:S(2)}) copy-start(bf16[5,1024]{1,0:T(8,128)(2,1)} %param.11) | copy-start | bytes 30724
  7.2 4.6 %copy-start.17 = (s32[512]{0:T(512)S(1)}, s32[512]{0:T(512)}, u32[]{:S(2)}) copy-start(s32[512]{0:T(512)} %param.8) | copy-start | bytes 6148
  7.2 19.9 %all-gather.3.cloned.1.call-start = ((), (), s32[]{:S(2)}) async-start(), calls=%async_computation | async-start | bytes 3145728 | tf_op jit(solution)/shard_map/all_gather | solution.py:156
  9.3 3.1 %copy-start.3 = (bf16[512,1024]{1,0:T(8,128)(2,1)S(1)}, bf16[512,1024]{1,0:T(8,128)(2,1)}, u32[]{:S(2)}) copy-start(bf16[512,1024]{1,0:T(8,128)(2,1)} %param.14) | copy-start | bytes 3145732
  9.3 9.9 %copy-start.12 = (bf16[2,9,1024]{2,0,1:T(2,128)(2,1)S(1)}, bf16[2,9,1024]{2,0,1:T(2,128)(2,1)}, u32[]{:S(2)}) copy-start(bf16[2,9,1024]{2,0,1:T(2,128)(2,1)} %param.12) | copy-start | bytes 110596
  11.8 71.6 %all-gather.5.cloned.1.call-start = ((), (), s32[]{:S(2)}) async-start(), calls=%async_computation.1 | async-start | bytes 3145728 | tf_op jit(solution)/shard_map/all_gather | solution.py:156
  11.9 7.4 %copy-start.15 = (s32[512]{0:T(512)}, s32[512]{0:T(512)S(1)}, u32[]{:S(2)}) copy-start(s32[512]{0:T(512)S(1)} %broadcast_select_fusion.1) | copy-start | bytes 6148
  12.4 7.6 %collective-permute-start.1 = (bf16[48,1024]{1,0:T(8,128)(2,1)S(1)}, bf16[48,1024]{1,0:T(8,128)(2,1)S(1)}, u32[]{:S(2)}, u32[]{:S(2)}) collective-permute-start(bf16[48,1024]{1,0:T(8,128)(2,1)S(1)} %pad_maximum_fusion.6), channel_id=1, source_target_pairs={{2,0},{4,2},{6,4},{8,6},{10,8},{12,10},{14,12},{16,14},{18,16},{20... | collective-permute-start | bytes 294920 | tf_op jit(solution)/shard_map/ppermute | solution.py:31
  13.8 9.5 %collective-permute-start = (bf16[48,1024]{1,0:T(8,128)(2,1)S(1)}, bf16[48,1024]{1,0:T(8,128)(2,1)S(1)}, u32[]{:S(2)}, u32[]{:S(2)}) collective-permute-start(bf16[48,1024]{1,0:T(8,128)(2,1)S(1)} %pad_maximum_fusion.5), channel_id=1, source_target_pairs={{0,2},{2,4},{4,6},{6,8},{8,10},{10,12},{12,14},{14,16},{16,18},{18... | collective-permute-start | bytes 294920 | tf_op jit(solution)/shard_map/ppermute | solution.py:30
  19.3 41.8 %copy-start.13 = (f32[1,1,1024]{2,0,1:T(1,128)}, f32[1,1,1024]{2,0,1:T(1,128)S(1)}, u32[]{:S(2)}) copy-start(f32[1,1,1024]{2,0,1:T(1,128)S(1)} %get-tuple-element.211) | copy-start | bytes 12292
  27.1 13.3 %copy-start.11 = (bf16[512,1024]{1,0:T(8,128)(2,1)S(1)}, bf16[512,1024]{1,0:T(8,128)(2,1)}, u32[]{:S(2)}) copy-start(bf16[512,1024]{1,0:T(8,128)(2,1)} %get-tuple-element.61) | copy-start | bytes 3145732
  27.1 13.3 %copy-start.18 = (bf16[512,2048]{1,0:T(8,128)(2,1)S(1)}, bf16[512,2048]{1,0:T(8,128)(2,1)}, u32[]{:S(2)}) copy-start(bf16[512,2048]{1,0:T(8,128)(2,1)} %all-gather.3.cloned.1.call-done) | copy-start | bytes 6291460
  34.0 9.0 %collective-permute-start.3 = (bf16[32,1024]{1,0:T(8,128)(2,1)S(1)}, bf16[32,1024]{1,0:T(8,128)(2,1)S(1)}, u32[]{:S(2)}, u32[]{:S(2)}) collective-permute-start(bf16[32,1024]{1,0:T(8,128)(2,1)S(1)} %get-tuple-element.184), channel_id=1, source_target_pairs={{2,0},{4,2},{6,4},{8,6},{10,8},{12,10},{14,12},{16,14},{18,16},{20... | collective-permute-start | bytes 196616 | tf_op jit(solution)/shard_map/ppermute | solution.py:21
  35.3 7.7 %collective-permute-start.2 = (bf16[32,1024]{1,0:T(8,128)(2,1)S(1)}, bf16[32,1024]{1,0:T(8,128)(2,1)S(1)}, u32[]{:S(2)}, u32[]{:S(2)}) collective-permute-start(bf16[32,1024]{1,0:T(8,128)(2,1)S(1)} %get-tuple-element.185), channel_id=1, source_target_pairs={{0,2},{2,4},{4,6},{6,8},{8,10},{10,12},{12,14},{14,16},{16,18},{18... | collective-permute-start | bytes 196616 | tf_op jit(solution)/shard_map/ppermute | solution.py:20
  47.4 1.2 copy-start.7
  52.3 5.4 %copy-start.4 = (bf16[2,2,1,2,64,1024]{5,4,3,2,1,0:T(8,128)(2,1)S(1)}, bf16[2,2,1,2,64,1024]{5,4,3,2,1,0:T(8,128)(2,1)}, u32[]{:S(2)}) copy-start(bf16[2,2,1,2,64,1024]{5,4,3,2,1,0:T(8,128)(2,1)} %get-tuple-element.166) | copy-start | bytes 3145732
  54.8 26.0 %collective-permute-start.4 = (bf16[2,2,2,64,1024]{4,3,0,1,2:T(8,128)(2,1)}, bf16[2,2,2,64,1024]{4,3,0,1,2:T(8,128)(2,1)}, u32[]{:S(2)}, u32[]{:S(2)}) collective-permute-start(bf16[2,2,2,64,1024]{4,3,0,1,2:T(8,128)(2,1)} %bitcast.141), channel_id=1, source_target_pairs={{0,2},{2,0},{4,6},{6,4},{8,10},{10,8},{12,14},{14,12},{16,18},{18,... | collective-permute-start | bytes 3145736 | tf_op jit(solution)/shard_map/ppermute | solution.py:86
  58.8 24.5 %collective-permute-start.5 = (bf16[2,2,2,64,1024]{4,3,0,1,2:T(8,128)(2,1)}, bf16[2,2,2,64,1024]{4,3,0,1,2:T(8,128)(2,1)}, u32[]{:S(2)}, u32[]{:S(2)}) collective-permute-start(bf16[2,2,2,64,1024]{4,3,0,1,2:T(8,128)(2,1)} %bitcast.140), channel_id=1, source_target_pairs={{0,4},{2,6},{4,0},{6,2},{8,12},{10,14},{12,8},{14,10},{16,20},{18,... | collective-permute-start | bytes 3145736 | tf_op jit(solution)/shard_map/ppermute | solution.py:86
  83.4 6.9 %copy-start.10 = (bf16[512,1024]{1,0:T(8,128)(2,1)S(1)}, bf16[512,1024]{1,0:T(8,128)(2,1)}, u32[]{:S(2)}) copy-start(bf16[512,1024]{1,0:T(8,128)(2,1)} %get-tuple-element.76) | copy-start | bytes 3145732
  83.4 6.9 %copy-start.19 = (bf16[512,2048]{1,0:T(8,128)(2,1)S(1)}, bf16[512,2048]{1,0:T(8,128)(2,1)}, u32[]{:S(2)}) copy-start(bf16[512,2048]{1,0:T(8,128)(2,1)} %all-gather.5.cloned.1.call-done) | copy-start | bytes 6291460
  95.6 8.5 %copy-start.6 = (bf16[2,2,2,1,64,1024]{5,4,0,1,2,3:T(8,128)(2,1)S(1)}, bf16[2,2,2,1,64,1024]{5,4,0,1,2,3:T(8,128)(2,1)}, u32[]{:S(2)}) copy-start(bf16[2,2,2,1,64,1024]{5,4,0,1,2,3:T(8,128)(2,1)} %copy.53) | copy-start | bytes 3145732
  98.0 9.4 %copy-start.5 = (bf16[2,2,1,2,64,1024]{5,4,0,1,3,2:T(8,128)(2,1)S(1)}, bf16[2,2,1,2,64,1024]{5,4,0,1,3,2:T(8,128)(2,1)}, u32[]{:S(2)}) copy-start(bf16[2,2,1,2,64,1024]{5,4,0,1,3,2:T(8,128)(2,1)} %copy.52) | copy-start | bytes 3145732
  98.0 14.9 %collective-permute-start.7 = (bf16[16,1024]{1,0:T(8,128)(2,1)S(1)}, bf16[16,1024]{1,0:T(8,128)(2,1)S(1)}, u32[]{:S(2)}, u32[]{:S(2)}) collective-permute-start(bf16[16,1024]{1,0:T(8,128)(2,1)S(1)} %get-tuple-element.180), channel_id=1, source_target_pairs={{2,0},{4,2},{6,4},{8,6},{10,8},{12,10},{14,12},{16,14},{18,16},{20... | collective-permute-start | bytes 98312 | tf_op jit(solution)/shard_map/ppermute | solution.py:21
  99.5 13.5 %collective-permute-start.6 = (bf16[16,1024]{1,0:T(8,128)(2,1)S(1)}, bf16[16,1024]{1,0:T(8,128)(2,1)S(1)}, u32[]{:S(2)}, u32[]{:S(2)}) collective-permute-start(bf16[16,1024]{1,0:T(8,128)(2,1)S(1)} %get-tuple-element.181), channel_id=1, source_target_pairs={{0,2},{2,4},{4,6},{6,8},{8,10},{10,12},{12,14},{14,16},{16,18},{18... | collective-permute-start | bytes 98312 | tf_op jit(solution)/shard_map/ppermute | solution.py:20
  106.4 14.2 %collective-permute-start.10 = (bf16[2,2,64,1024]{3,2,0,1:T(8,128)(2,1)}, bf16[2,2,64,1024]{3,2,0,1:T(8,128)(2,1)}, u32[]{:S(2)}, u32[]{:S(2)}) collective-permute-start(bf16[2,2,64,1024]{3,2,0,1:T(8,128)(2,1)} %get-tuple-element.160), channel_id=1, source_target_pairs={{0,4},{2,6},{4,0},{6,2},{8,12},{10,14},{12,8},{14,10},{16,20},{18,... | collective-permute-start | bytes 1572872 | tf_op jit(solution)/shard_map/ppermute | solution.py:86
  109.8 16.2 %collective-permute-start.11 = (bf16[2,2,64,1024]{3,2,0,1:T(8,128)(2,1)}, bf16[2,2,64,1024]{3,2,0,1:T(8,128)(2,1)}, u32[]{:S(2)}, u32[]{:S(2)}) collective-permute-start(bf16[2,2,64,1024]{3,2,0,1:T(8,128)(2,1)} %get-tuple-element.158), channel_id=1, source_target_pairs={{0,2},{2,0},{4,6},{6,4},{8,10},{10,8},{12,14},{14,12},{16,18},{18,... | collective-permute-start | bytes 1572872 | tf_op jit(solution)/shard_map/ppermute | solution.py:86
  114.7 1.6 copy-start.9
  114.9 29.2 %collective-permute-start.8 = (bf16[2,2,2,64,1024]{4,3,0,1,2:T(8,128)(2,1)S(1)}, bf16[2,2,2,64,1024]{4,3,0,1,2:T(8,128)(2,1)S(1)}, u32[]{:S(2)}, u32[]{:S(2)}) collective-permute-start(bf16[2,2,2,64,1024]{4,3,0,1,2:T(8,128)(2,1)S(1)} %bitcast.153), channel_id=1, source_target_pairs={{0,2},{2,0},{4,6},{6,4},{8,10},{10,8},{12,14},{14,12},{16,18},{18,... | collective-permute-start | bytes 3145736 | tf_op jit(solution)/shard_map/ppermute | solution.py:86
  116.7 1.2 copy-start.2
  116.8 1.2 copy-start.14
  116.8 27.4 %collective-permute-start.9 = (bf16[2,2,2,64,1024]{4,3,0,1,2:T(8,128)(2,1)S(1)}, bf16[2,2,2,64,1024]{4,3,0,1,2:T(8,128)(2,1)S(1)}, u32[]{:S(2)}, u32[]{:S(2)}) collective-permute-start(bf16[2,2,2,64,1024]{4,3,0,1,2:T(8,128)(2,1)S(1)} %bitcast.154), channel_id=1, source_target_pairs={{0,4},{2,6},{4,0},{6,2},{8,12},{10,14},{12,8},{14,10},{16,20},{18,... | collective-permute-start | bytes 3145736 | tf_op jit(solution)/shard_map/ppermute | solution.py:86
  118.0 2.4 %copy-start.16 = (s32[512]{0:T(512)S(1)}, s32[512]{0:T(512)}, u32[]{:S(2)}) copy-start(s32[512]{0:T(512)} %copy-done.15) | copy-start | bytes 6148
  120.3 25.0 %copy-start.8 = (bf16[512,1024]{1,0:T(8,128)(2,1)}, bf16[512,1024]{1,0:T(8,128)(2,1)S(1)}, u32[]{:S(2)}) copy-start(bf16[512,1024]{1,0:T(8,128)(2,1)S(1)} %fusion.58) | copy-start | bytes 3145732
  145.3 18.8 %collective-permute-start.13 = (bf16[2,2,64,1024]{3,2,0,1:T(8,128)(2,1)}, bf16[2,2,64,1024]{3,2,0,1:T(8,128)(2,1)S(1)}, u32[]{:S(2)}, u32[]{:S(2)}) collective-permute-start(bf16[2,2,64,1024]{3,2,0,1:T(8,128)(2,1)} %get-tuple-element.156), channel_id=1, source_target_pairs={{0,4},{2,6},{4,0},{6,2},{8,12},{10,14},{12,8},{14,10},{16,20},{18,... | collective-permute-start | bytes 1572872 | tf_op jit(solution)/shard_map/ppermute | solution.py:86
  146.9 17.2 %collective-permute-start.14 = (bf16[2,2,64,1024]{3,2,0,1:T(8,128)(2,1)}, bf16[2,2,64,1024]{3,2,0,1:T(8,128)(2,1)}, u32[]{:S(2)}, u32[]{:S(2)}) collective-permute-start(bf16[2,2,64,1024]{3,2,0,1:T(8,128)(2,1)} %get-tuple-element.154), channel_id=1, source_target_pairs={{0,2},{2,0},{4,6},{6,4},{8,10},{10,8},{12,14},{14,12},{16,18},{18,... | collective-permute-start | bytes 1572872 | tf_op jit(solution)/shard_map/ppermute | solution.py:86
  149.8 12.1 %collective-permute-start.15 = (bf16[2,64,1024]{2,1,0:T(8,128)(2,1)S(1)}, bf16[2,64,1024]{2,1,0:T(8,128)(2,1)S(1)}, u32[]{:S(2)}, u32[]{:S(2)}) collective-permute-start(bf16[2,64,1024]{2,1,0:T(8,128)(2,1)S(1)} %get-tuple-element.176), channel_id=1, source_target_pairs={{0,8},{2,10},{4,12},{6,14},{8,0},{10,2},{12,4},{14,6},{16,24},{18,... | collective-permute-start | bytes 786440 | tf_op jit(solution)/shard_map/ppermute | solution.py:86
  153.2 10.9 %collective-permute-start.16 = (bf16[2,64,1024]{2,1,0:T(8,128)(2,1)}, bf16[2,64,1024]{2,1,0:T(8,128)(2,1)S(1)}, u32[]{:S(2)}, u32[]{:S(2)}) collective-permute-start(bf16[2,64,1024]{2,1,0:T(8,128)(2,1)} %get-tuple-element.174), channel_id=1, source_target_pairs={{0,8},{2,10},{4,12},{6,14},{8,0},{10,2},{12,4},{14,6},{16,24},{18,... | collective-permute-start | bytes 786440 | tf_op jit(solution)/shard_map/ppermute | solution.py:86
  153.8 8.1 %collective-permute-start.12 = (f32[23,1024]{1,0:T(8,128)S(1)}, f32[23,1024]{1,0:T(8,128)S(1)}, u32[]{:S(2)}, u32[]{:S(2)}) collective-permute-start(f32[23,1024]{1,0:T(8,128)S(1)} %pad_maximum_fusion.7), channel_id=1, source_target_pairs={{0,16},{2,18},{4,20},{6,22},{8,24},{10,26},{12,28},{14,30},{16,0},... | collective-permute-start | bytes 282632 | tf_op jit(solution)/shard_map/ppermute | solution.py:86
  164.3 16.1 %collective-permute-start.18 = (bf16[2,64,1024]{2,1,0:T(8,128)(2,1)S(1)}, bf16[2,64,1024]{2,1,0:T(8,128)(2,1)S(1)}, u32[]{:S(2)}, u32[]{:S(2)}) collective-permute-start(bf16[2,64,1024]{2,1,0:T(8,128)(2,1)S(1)} %get-tuple-element.172), channel_id=1, source_target_pairs={{0,8},{2,10},{4,12},{6,14},{8,0},{10,2},{12,4},{14,6},{16,24},{18,... | collective-permute-start | bytes 786440 | tf_op jit(solution)/shard_map/ppermute | solution.py:86
  167.4 13.0 %collective-permute-start.19 = (bf16[2,64,1024]{2,1,0:T(8,128)(2,1)S(1)}, bf16[2,64,1024]{2,1,0:T(8,128)(2,1)S(1)}, u32[]{:S(2)}, u32[]{:S(2)}) collective-permute-start(bf16[2,64,1024]{2,1,0:T(8,128)(2,1)S(1)} %get-tuple-element.170), channel_id=1, source_target_pairs={{0,8},{2,10},{4,12},{6,14},{8,0},{10,2},{12,4},{14,6},{16,24},{18,... | collective-permute-start | bytes 786440 | tf_op jit(solution)/shard_map/ppermute | solution.py:86
  167.8 12.6 %collective-permute-start.20 = (bf16[64,1024]{1,0:T(8,128)(2,1)S(1)}, bf16[64,1024]{1,0:T(8,128)(2,1)S(1)}, u32[]{:S(2)}, u32[]{:S(2)}) collective-permute-start(bf16[64,1024]{1,0:T(8,128)(2,1)S(1)} %get-tuple-element.192), channel_id=1, source_target_pairs={{0,16},{2,18},{4,20},{6,22},{8,24},{10,26},{12,28},{14,30},{16,0},... | collective-permute-start | bytes 393224 | tf_op jit(solution)/shard_map/ppermute | solution.py:86
  169.2 11.2 %collective-permute-start.21 = (bf16[64,1024]{1,0:T(8,128)(2,1)S(1)}, bf16[64,1024]{1,0:T(8,128)(2,1)S(1)}, u32[]{:S(2)}, u32[]{:S(2)}) collective-permute-start(bf16[64,1024]{1,0:T(8,128)(2,1)S(1)} %get-tuple-element.190), channel_id=1, source_target_pairs={{0,16},{2,18},{4,20},{6,22},{8,24},{10,26},{12,28},{14,30},{16,0},... | collective-permute-start | bytes 393224 | tf_op jit(solution)/shard_map/ppermute | solution.py:86
  170.9 9.4 %collective-permute-start.17 = (f32[23,1024]{1,0:T(8,128)S(1)}, f32[23,1024]{1,0:T(8,128)S(1)}, u32[]{:S(2)}, u32[]{:S(2)}) collective-permute-start(f32[23,1024]{1,0:T(8,128)S(1)} %add.395), channel_id=1, source_target_pairs={{0,8},{2,10},{4,12},{6,14},{8,0},{10,2},{12,4},{14,6},{16,24},{18,... | collective-permute-start | bytes 282632 | tf_op jit(solution)/shard_map/ppermute | solution.py:86
  180.4 4.8 %collective-permute-start.24 = (f32[23,1024]{1,0:T(8,128)S(1)}, f32[23,1024]{1,0:T(8,128)S(1)}, u32[]{:S(2)}, u32[]{:S(2)}) collective-permute-start(f32[23,1024]{1,0:T(8,128)S(1)} %add.406), channel_id=1, source_target_pairs={{0,4},{2,6},{4,0},{6,2},{8,12},{10,14},{12,8},{14,10},{16,20},{18,... | collective-permute-start | bytes 282632 | tf_op jit(solution)/shard_map/ppermute | solution.py:86
  182.0 9.2 %collective-permute-start.23 = (bf16[64,1024]{1,0:T(8,128)(2,1)S(1)}, bf16[64,1024]{1,0:T(8,128)(2,1)S(1)}, u32[]{:S(2)}, u32[]{:S(2)}) collective-permute-start(bf16[64,1024]{1,0:T(8,128)(2,1)S(1)} %fusion.113), channel_id=1, source_target_pairs={{0,16},{2,18},{4,20},{6,22},{8,24},{10,26},{12,28},{14,30},{16,0},... | collective-permute-start | bytes 393224 | tf_op jit(solution)/shard_map/ppermute | solution.py:86
  184.4 8.2 %collective-permute-start.22 = (bf16[64,1024]{1,0:T(8,128)(2,1)S(1)}, bf16[64,1024]{1,0:T(8,128)(2,1)S(1)}, u32[]{:S(2)}, u32[]{:S(2)}) collective-permute-start(bf16[64,1024]{1,0:T(8,128)(2,1)S(1)} %fusion.111), channel_id=1, source_target_pairs={{0,16},{2,18},{4,20},{6,22},{8,24},{10,26},{12,28},{14,30},{16,0},... | collective-permute-start | bytes 393224 | tf_op jit(solution)/shard_map/ppermute | solution.py:86
  185.2 8.6 %collective-permute-start.25 = (f32[23,1024]{1,0:T(8,128)S(1)}, f32[23,1024]{1,0:T(8,128)S(1)}, u32[]{:S(2)}, u32[]{:S(2)}) collective-permute-start(f32[23,1024]{1,0:T(8,128)S(1)} %add.425), channel_id=1, source_target_pairs={{0,2},{2,0},{4,6},{6,4},{8,10},{10,8},{12,14},{14,12},{16,18},{18,... | collective-permute-start | bytes 282632 | tf_op jit(solution)/shard_map/ppermute | solution.py:86
  192.6 2.5 %copy-start.1 = (bf16[5,1024]{1,0:T(8,128)(2,1)S(1)}, bf16[5,1024]{1,0:T(8,128)(2,1)}, u32[]{:S(2)}) copy-start(bf16[5,1024]{1,0:T(8,128)(2,1)} %param.11) | copy-start | bytes 30724
Sparse Core Ops, SparseCore 0:
  11.9 13.2 all-gather.2
  52.5 14.0 all-gather.4

commit v5 on v3

--- a/solution.py
+++ b/solution.py
@@ -216,12 +216,10 @@
     sums = jnp.concatenate(kernel_parts + [embed_part])
     for step in range(steps):
         sums = sums + exchanged(sums, "seq", steps - 1 - step)
-        if step == 0:
-            sums, earlier = lax.optimization_barrier((sums, earlier))
-            earlier = later_steps(earlier, orders, range(3, steps))
-        elif step < 4:
+        if step < 3:
             sums, pairs, earlier = lax.optimization_barrier((sums, pairs, earlier))
-            pairs = later_steps(pairs, orders, range(step, step + 1 if step < 3 else steps))
+            pairs = later_steps(pairs, orders, range(step + 1, step + 2 if step < 2 else steps))
+            earlier = later_steps(earlier, orders, range(3, steps) if step == 0 else ())
     weight_parts = [finished(pairs, grad_scale), finished(earlier, grad_scale)]
     weight_grad = jnp.stack(weight_parts)
     kernel_grad = sums[: block_count * tap_count].reshape(block_count, tap_count, -1)

time: 193 us -> 183 us (0.948)
  waiting for transfers between devices: 59.2 us -> 45.2 us
  starting transfers between devices: 45.7 us -> 50.4 us
    ppermute x20, waiting for transfers between devices: 55.2 us -> 41.3 us  [exchanged(): return lax.ppermute(cells, axis, [(i, i ^ 1 << bit) for i in range(count)])]
    ppermute x20, starting transfers between devices: 26.5 us -> 31.2 us  [exchanged(): return lax.ppermute(cells, axis, [(i, i ^ 1 << bit) for i in range(count)])]
  transfers between devices with their start and end apart: 28 -> 28, of which waited for: 15 -> 15; matrix products, arithmetic and copies ran while one was open for 28% -> 30% of each run, Pallas kernels for 0% -> 0%
where the time goes in v5:
time: 183 us
  starting transfers between devices  50.4 us (28%)
  waiting for transfers between devices  45.2 us (25%)
  other arithmetic  35.3 us (19%)
  matrix products  20.8 us (11%)
  local copies, waits for them, and re-layouts  15.8 us (9%)
  between operations  14.9 us (8%)
    ppermute x20, waiting for transfers between devices, exchanged(): return lax.ppermute(cells, axis, [(i, i ^ 1 << bit) for i in range(count)])  41.3 us
    ppermute x20, starting transfers between devices, exchanged(): return lax.ppermute(cells, axis, [(i, i ^ 1 << bit) for i in range(count)])  31.2 us
    dot_general x2, matrix products, on_device(): lax.dot_general(column_piece, mix_weight[block_number], (((1,), (1,)), ((...  13.7 us
    convert_element_type x11, other arithmetic, added(): return total if last else total.astype(jnp.bfloat16)  10.4 us
    ppermute x2, starting transfers between devices, edge_rows(): lax.ppermute(cells[-width:], 'seq', [(i, (i + 1) % count) for i in range(...  9.79 us
    convert_element_type x2, other arithmetic, on_device(): act_half = activation.astype(jnp.bfloat16)  7.6 us
    dot_general x4, matrix products, on_device(): lax.dot_general(act_half, lax.slice_in_dim(column_piece, chunk * width, (...  6.4 us
    squeeze x12, local copies, waits for them, and re-layouts, halves_of(): send = lax.dynamic_index_in_dim(part, 1 - mine, dim, keepdims=False)  6.26 us
  transfers between devices with their start and end apart: 28, of which 15 were waited for; matrix products, arithmetic and copies ran while one was open for 30% of the time, Pallas kernels for 0%

profile of v5, /device:TPU:0, one launch (start us, length us, event | category | flops | bytes accessed | tf_op | source)
XLA Modules:
  0.0 182.6 jit_solution(4984664949435685178)
XLA Ops:
  8.0 1.3 and_reduce_fusion
  9.3 2.4 %broadcast_select_fusion = bf16[512,1024]{1,0:T(8,128)(2,1)} fusion(bf16[512,1024]{1,0:T(8,128)(2,1)} %param.15, pred[512]{0:T(512)(128)(4,1)S(1)} %and_reduce_fusion), kind=kLoop, calls=%fused_computation.155 | loop fusion | flops 524288 | bytes 2097664 | tf_op jit(solution)/shard_map/jit(_where)/select_n | solution.py:158
  13.0 1.3 collective-permute-start.1
  14.3 5.5 %collective-permute-start = (bf16[48,1024]{1,0:T(8,128)(2,1)S(1)}, bf16[48,1024]{1,0:T(8,128)(2,1)S(1)}, u32[]{:S(2)}, u32[]{:S(2)}) collective-permute-start(bf16[48,1024]{1,0:T(8,128)(2,1)S(1)} %pad_maximum_fusion.4), channel_id=1, source_target_pairs={{0,2},{2,4},{4,6},{6,8},{8,10},{10,12},{12,14},{14,16},{16,18},{18... | collective-permute-start | bytes 294920 | tf_op jit(solution)/shard_map/ppermute | solution.py:30
  20.7 3.2 %collective-permute-done = bf16[48,1024]{1,0:T(8,128)(2,1)S(1)} collective-permute-done((bf16[48,1024]{1,0:T(8,128)(2,1)S(1)}, bf16[48,1024]{1,0:T(8,128)(2,1)S(1)}, u32[]{:S(2)}, u32[]{:S(2)}) %collective-permute-start) | collective-permute-done | bytes 98336 | tf_op jit(solution)/shard_map/ppermute | solution.py:30
  24.0 3.8 %multiply_convert_fusion.1 = (bf16[512,1024]{1,0:T(8,128)(2,1)}, f32[512,1024]{1,0:T(8,128)}) fusion(bf16[32,1024]{1,0:T(8,128)(2,1)S(1)} %slice.390, bf16[512,1024]{1,0:T(8,128)(2,1)S(1)} %copy-done.3, f32[1024]{0:T(1024)S(1)} %bitcast.170, f32[1024]{0:T(1024)S(1)} %bitcast.172, f32[1024]{0:T(1024)S(1)} %bitcast.174, f32[1024]{0:T(1024)S(1)} %bitcast.176, ...), kind=kLoop, calls=%fused_computation.115 | loop fusion | flops 30932992 | bytes 4362240 | tf_op jit(solution)/shard_map/convert_element_type | solution.py:171
  27.8 6.9 %fusion.28 = bf16[512,1024]{1,0:T(8,128)(2,1)S(1)} fusion(f32[512,1024]{1,0:T(8,128)} %get-tuple-element.143, bf16[512,2048]{1,0:T(8,128)(2,1)} %all-gather.3.cloned.1.call-done, bf16[2,1024,2048]{2,1,0:T(8,128)(2,1)} %param.13), kind=kOutput, calls=%fused_computation.70 | convolution fusion | flops 2157445120 | bytes 9437184 | tf_op jit(solution)/shard_map/dot_general | solution.py:176
  34.7 1.3 collective-permute-start.3
  36.0 5.0 %collective-permute-start.2 = (bf16[32,1024]{1,0:T(8,128)(2,1)S(1)}, bf16[32,1024]{1,0:T(8,128)(2,1)S(1)}, u32[]{:S(2)}, u32[]{:S(2)}) collective-permute-start(bf16[32,1024]{1,0:T(8,128)(2,1)S(1)} %get-tuple-element.167), channel_id=1, source_target_pairs={{0,2},{2,4},{4,6},{6,8},{8,10},{10,12},{12,14},{14,16},{16,18},{18... | collective-permute-start | bytes 196616 | tf_op jit(solution)/shard_map/ppermute | solution.py:20
  41.1 1.3 convolution_convert_fusion.2
  42.6 1.3 convolution_convert_fusion.3
  48.4 2.9 %collective-permute-start.4 = (bf16[2,2,2,64,1024]{4,3,1,0,2:T(8,128)(2,1)}, bf16[2,2,2,64,1024]{4,3,1,0,2:T(8,128)(2,1)}, u32[]{:S(2)}, u32[]{:S(2)}) collective-permute-start(bf16[2,2,2,64,1024]{4,3,1,0,2:T(8,128)(2,1)} %bitcast.133), channel_id=1, source_target_pairs={{0,2},{2,0},{4,6},{6,4},{8,10},{10,8},{12,14},{14,12},{16,18},{18,... | collective-permute-start | bytes 3145736 | tf_op jit(solution)/shard_map/ppermute | solution.py:86
  51.3 2.3 %collective-permute-start.5 = (bf16[2,2,2,64,1024]{4,3,1,0,2:T(8,128)(2,1)}, bf16[2,2,2,64,1024]{4,3,1,0,2:T(8,128)(2,1)}, u32[]{:S(2)}, u32[]{:S(2)}) collective-permute-start(bf16[2,2,2,64,1024]{4,3,1,0,2:T(8,128)(2,1)} %bitcast.132), channel_id=1, source_target_pairs={{0,4},{2,6},{4,0},{6,2},{8,12},{10,14},{12,8},{14,10},{16,20},{18,... | collective-permute-start | bytes 3145736 | tf_op jit(solution)/shard_map/ppermute | solution.py:86
  53.9 3.9 %fusion.42 = bf16[512,1024]{1,0:T(8,128)(2,1)} fusion(bf16[512,1024]{1,0:T(8,128)(2,1)S(1)} %fusion.28, bf16[544,1024]{1,0:T(8,128)(2,1)S(1)} %get-tuple-element.165, bf16[544,1024]{1,0:T(8,128)(2,1)S(1)} %constant_dynamic-update-slice_fusion, f32[1024]{0:T(1024)S(1)} %bitcast.171, f32[1024]{0:T(1024)S(1)} %bitcast.173, f32[1024]{0:T(1024)S(1)} %bitcast.175, ...), kind=kLoop, calls=%fused_computation.84 | loop fusion | flops 15728640 | bytes 11571712 | tf_op jit(solution)/shard_map/convert_element_type | solution.py:212
  57.8 2.8 %fusion.51 = (f32[1024]{0:T(1024)S(1)}, f32[1024]{0:T(1024)S(1)}, f32[1024]{0:T(1024)S(1)}, f32[1024]{0:T(1024)S(1)}, f32[1024]{0:T(1024)S(1)}, /*index=5*/f32[1...) fusion(bf16[512,1024]{1,0:T(8,128)(2,1)S(1)} %fusion.28, bf16[32,1024]{1,0:T(8,128)(2,1)S(1)} %slice.390, ...), kind=kLoop, calls=%fused_computation.93 | loop fusion | flops 27253760 | bytes 2265088 | tf_op jit(solution)/shard_map/reduce_sum | solution.py:68
  60.6 13.7 %collective-permute-done.4 = bf16[2,2,2,64,1024]{4,3,1,0,2:T(8,128)(2,1)} collective-permute-done((bf16[2,2,2,64,1024]{4,3,1,0,2:T(8,128)(2,1)}, bf16[2,2,2,64,1024]{4,3,1,0,2:T(8,128)(2,1)}, u32[]{:S(2)}, u32[]{:S(2)}) %collective-permute-start.4) | collective-permute-done | bytes 1048608 | tf_op jit(solution)/shard_map/ppermute | solution.py:86
  74.3 1.5 collective-permute-done.5
  75.8 3.1 %add_convert_fusion.2 = (bf16[2,2,2,64,1024]{4,3,1,0,2:T(8,128)(2,1)S(1)}, bf16[2,2,2,64,1024]{4,3,1,0,2:T(8,128)(2,1)S(1)}) fusion(bf16[2,2,2,64,1024]{4,3,1,0,2:T(8,128)(2,1)} %collective-permute-done.5, bf16[2,2,2,64,1024]{4,3,1,0,2:T(8,128)(2,1)} %bitcast.142, bf16[2,2,2,64,1024]{4,3,1,0,2:T(8,128)(2,1)} %collective-permute-done.4, ...), kind=kLoop, calls=%fused_computation.112 | loop fusion | flops 4194304 | bytes 6291456 | tf_op jit(solution)/shard_map/convert_element_type | solution.py:113
  82.4 3.8 %multiply_convert_fusion = (bf16[512,1024]{1,0:T(8,128)(2,1)S(1)}, f32[512,1024]{1,0:T(8,128)}) fusion(bf16[544,1024]{1,0:T(8,128)(2,1)S(1)} %pad_maximum_fusion, f32[1024]{0:T(1024)S(1)} %bitcast.166, f32[1024]{0:T(1024)S(1)} %bitcast.168, f32[1024]{0:T(1024)S(1)} %bitcast.154, f32[1024]{0:T(1024)S(1)} %bitcast.156, f32[1024]{0:T(1024)S(1)} %bitcast.158, ...), kind=kLoop, calls=%fused_computation.114 | loop fusion | flops 18350080 | bytes 12619776 | tf_op jit(solution)/shard_map/convert_element_type | solution.py:171
  86.2 6.8 %fusion.35 = bf16[512,1024]{1,0:T(8,128)(2,1)S(1)} fusion(f32[512,1024]{1,0:T(8,128)} %get-tuple-element.141, bf16[512,2048]{1,0:T(8,128)(2,1)} %all-gather.5.cloned.1.call-done, bf16[2,1024,2048]{2,1,0:T(8,128)(2,1)} %param.13), kind=kOutput, calls=%fused_computation.77 | convolution fusion | flops 2157445120 | bytes 9437184 | tf_op jit(solution)/shard_map/dot_general | solution.py:176
  92.9 2.3 %fusion.67 = (f32[1024]{0:T(1024)S(1)}, f32[1024]{0:T(1024)S(1)}, f32[1024]{0:T(1024)S(1)}, f32[1024]{0:T(1024)S(1)}, f32[1024]{0:T(1024)S(1)}, /*index=5*/f32[1...) fusion(bf16[512,1024]{1,0:T(8,128)(2,1)S(1)} %fusion.35, bf16[544,1024]{1,0:T(8,128)(2,1)S(1)} %pad_maximum_fusion), kind=kLoop, calls=%fused_computation.109 | loop fusion | flops 14670848 | bytes 10522624 | tf_op jit(solution)/shard_map/reduce_sum | solution.py:68
  95.3 1.3 collective-permute-start.7
  96.6 4.8 %collective-permute-start.6 = (bf16[16,1024]{1,0:T(8,128)(2,1)S(1)}, bf16[16,1024]{1,0:T(8,128)(2,1)S(1)}, u32[]{:S(2)}, u32[]{:S(2)}) collective-permute-start(bf16[16,1024]{1,0:T(8,128)(2,1)S(1)} %get-tuple-element.163), channel_id=1, source_target_pairs={{0,2},{2,4},{4,6},{6,8},{8,10},{10,12},{12,14},{14,16},{16,18},{18... | collective-permute-start | bytes 98312 | tf_op jit(solution)/shard_map/ppermute | solution.py:20
  101.4 2.5 %convolution_convert_fusion = bf16[1024,1024]{1,0:T(8,128)(2,1)S(1)} fusion(bf16[512,1024]{1,0:T(8,128)(2,1)S(1)} %get-tuple-element.70, bf16[512,2048]{1,0:T(8,128)(2,1)} %all-gather.5.cloned.1.call-done), kind=kOutput, calls=%fused_computation.123 | convolution fusion | flops 1074790400 | bytes 4194304 | tf_op jit(solution)/shard_map/dot_general | solution.py:188
  105.9 1.3 convolution_convert_fusion.1
  108.4 2.6 %collective-permute-start.11 = (bf16[2,2,2,64,1024]{4,3,2,1,0:T(8,128)(2,1)}, bf16[2,2,2,64,1024]{4,3,2,1,0:T(8,128)(2,1)}, u32[]{:S(2)}, u32[]{:S(2)}) collective-permute-start(bf16[2,2,2,64,1024]{4,3,2,1,0:T(8,128)(2,1)} %get-tuple-element.146), channel_id=1, source_target_pairs={{0,2},{2,0},{4,6},{6,4},{8,10},{10,8},{12,14},{14,12},{16,18},{18,... | collective-permute-start | bytes 3145736 | tf_op jit(solution)/shard_map/ppermute | solution.py:86
  111.0 2.0 %collective-permute-start.12 = (bf16[2,2,2,64,1024]{4,3,2,1,0:T(8,128)(2,1)}, bf16[2,2,2,64,1024]{4,3,2,1,0:T(8,128)(2,1)}, u32[]{:S(2)}, u32[]{:S(2)}) collective-permute-start(bf16[2,2,2,64,1024]{4,3,2,1,0:T(8,128)(2,1)} %get-tuple-element.144), channel_id=1, source_target_pairs={{0,4},{2,6},{4,0},{6,2},{8,12},{10,14},{12,8},{14,10},{16,20},{18,... | collective-permute-start | bytes 3145736 | tf_op jit(solution)/shard_map/ppermute | solution.py:86
  113.0 1.2 add_convert_fusion.7
  115.1 1.6 collective-permute-start.13
  117.0 2.4 %fusion.58 = bf16[512,1024]{1,0:T(8,128)(2,1)S(1)} fusion(bf16[512,1024]{1,0:T(8,128)(2,1)S(1)} %fusion.35, bf16[512,1024]{1,0:T(8,128)(2,1)S(1)} %copy-done.2, bf16[528,1024]{1,0:T(8,128)(2,1)S(1)} %get-tuple-element.157, bf16[528,1024]{1,0:T(8,128)(2,1)S(1)} %constant_dynamic-update-slice_fusion.4, f32[1024]{0:T(1024)S(1)} %bitcast.167, ...), kind=kLoop, calls=%fused_computation.100 | loop fusion | flops 15204352 | bytes 11571200 | tf_op jit(solution)/shard_map/convert_element_type | solution.py:212
  120.7 1.2 collective-permute-start.10
  124.0 1.9 %collective-permute-start.14 = (bf16[2,64,1024]{2,1,0:T(8,128)(2,1)}, bf16[2,64,1024]{2,1,0:T(8,128)(2,1)S(1)}, u32[]{:S(2)}, u32[]{:S(2)}) collective-permute-start(bf16[2,64,1024]{2,1,0:T(8,128)(2,1)} %get-tuple-element.176), channel_id=1, source_target_pairs={{0,8},{2,10},{4,12},{6,14},{8,0},{10,2},{12,4},{14,6},{16,24},{18,... | collective-permute-start | bytes 786440 | tf_op jit(solution)/shard_map/ppermute | solution.py:86
  125.8 1.4 collective-permute-done.10
  127.3 3.2 %collective-permute-done.14 = bf16[2,64,1024]{2,1,0:T(8,128)(2,1)S(1)} collective-permute-done((bf16[2,64,1024]{2,1,0:T(8,128)(2,1)}, bf16[2,64,1024]{2,1,0:T(8,128)(2,1)S(1)}, u32[]{:S(2)}, u32[]{:S(2)}) %collective-permute-start.14) | collective-permute-done | bytes 262176 | tf_op jit(solution)/shard_map/ppermute | solution.py:86
  130.8 2.4 %collective-permute-done.12 = bf16[2,2,2,64,1024]{4,3,2,1,0:T(8,128)(2,1)} collective-permute-done((bf16[2,2,2,64,1024]{4,3,2,1,0:T(8,128)(2,1)}, bf16[2,2,2,64,1024]{4,3,2,1,0:T(8,128)(2,1)}, u32[]{:S(2)}, u32[]{:S(2)}) %collective-permute-start.12) | collective-permute-done | bytes 1048608 | tf_op jit(solution)/shard_map/ppermute | solution.py:86
  133.2 1.6 add_convert_fusion.1
  135.0 1.8 collective-permute-start.16
  136.8 1.6 add_convert_fusion
  140.0 2.6 %collective-permute-start.18 = (bf16[64,1024]{1,0:T(8,128)(2,1)S(1)}, bf16[64,1024]{1,0:T(8,128)(2,1)S(1)}, u32[]{:S(2)}, u32[]{:S(2)}) collective-permute-start(bf16[64,1024]{1,0:T(8,128)(2,1)S(1)} %get-tuple-element.182), channel_id=1, source_target_pairs={{0,16},{2,18},{4,20},{6,22},{8,24},{10,26},{12,28},{14,30},{16,0},... | collective-permute-start | bytes 393224 | tf_op jit(solution)/shard_map/ppermute | solution.py:86
  143.1 1.5 collective-permute-start.15
  144.7 5.2 %collective-permute-done.15 = f32[23,1024]{1,0:T(8,128)S(1)} collective-permute-done((f32[23,1024]{1,0:T(8,128)S(1)}, f32[23,1024]{1,0:T(8,128)S(1)}, u32[]{:S(2)}, u32[]{:S(2)}) %collective-permute-start.15) | collective-permute-done | bytes 94240 | tf_op jit(solution)/shard_map/ppermute | solution.py:86
  150.5 2.3 %collective-permute-start.21 = (bf16[2,64,1024]{2,1,0:T(8,128)(2,1)S(1)}, bf16[2,64,1024]{2,1,0:T(8,128)(2,1)S(1)}, u32[]{:S(2)}, u32[]{:S(2)}) collective-permute-start(bf16[2,64,1024]{2,1,0:T(8,128)(2,1)S(1)} %get-tuple-element.174), channel_id=1, source_target_pairs={{0,8},{2,10},{4,12},{6,14},{8,0},{10,2},{12,4},{14,6},{16,24},{18,... | collective-permute-start | bytes 786440 | tf_op jit(solution)/shard_map/ppermute | solution.py:86
  153.4 4.4 %collective-permute-done.20 = f32[23,1024]{1,0:T(8,128)S(1)} collective-permute-done((f32[23,1024]{1,0:T(8,128)S(1)}, f32[23,1024]{1,0:T(8,128)S(1)}, u32[]{:S(2)}, u32[]{:S(2)}) %collective-permute-start.20) | collective-permute-done | bytes 94240 | tf_op jit(solution)/shard_map/ppermute | solution.py:86
  157.9 3.4 %collective-permute-done.22 = bf16[2,64,1024]{2,1,0:T(8,128)(2,1)S(1)} collective-permute-done((bf16[2,64,1024]{2,1,0:T(8,128)(2,1)S(1)}, bf16[2,64,1024]{2,1,0:T(8,128)(2,1)S(1)}, u32[]{:S(2)}, u32[]{:S(2)}) %collective-permute-start.22) | collective-permute-done | bytes 262176 | tf_op jit(solution)/shard_map/ppermute | solution.py:86
  161.3 3.1 %collective-permute-start.25 = (f32[23,1024]{1,0:T(8,128)S(1)}, f32[23,1024]{1,0:T(8,128)S(1)}, u32[]{:S(2)}, u32[]{:S(2)}) collective-permute-start(f32[23,1024]{1,0:T(8,128)S(1)} %add.321), channel_id=1, source_target_pairs={{0,2},{2,0},{4,6},{6,4},{8,10},{10,8},{12,14},{14,12},{16,18},{18,... | collective-permute-start | bytes 282632 | tf_op jit(solution)/shard_map/ppermute | solution.py:86
  164.9 2.7 %collective-permute-start.24 = (bf16[64,1024]{1,0:T(8,128)(2,1)S(1)}, bf16[64,1024]{1,0:T(8,128)(2,1)S(1)}, u32[]{:S(2)}, u32[]{:S(2)}) collective-permute-start(bf16[64,1024]{1,0:T(8,128)(2,1)S(1)} %dynamic-slice_bitcast_fusion.16), channel_id=1, source_target_pairs={{0,16},{2,18},{4,20},{6,22},{8,24},{10,26},{12,28},{14,30},{16,0},... | collective-permute-start | bytes 393224 | tf_op jit(solution)/shard_map/ppermute | solution.py:86
  169.1 1.3 collective-permute-done.23
  170.4 4.2 %collective-permute-done.24 = bf16[64,1024]{1,0:T(8,128)(2,1)S(1)} collective-permute-done((bf16[64,1024]{1,0:T(8,128)(2,1)S(1)}, bf16[64,1024]{1,0:T(8,128)(2,1)S(1)}, u32[]{:S(2)}, u32[]{:S(2)}) %collective-permute-start.24) | collective-permute-done | bytes 131104 | tf_op jit(solution)/shard_map/ppermute | solution.py:86
  (161 shorter events, 25.9 us)
Async XLA Ops:
  7.2 5.3 %copy-start = (bf16[5,1024]{1,0:T(8,128)(2,1)S(1)}, bf16[5,1024]{1,0:T(8,128)(2,1)}, u32[]{:S(2)}) copy-start(bf16[5,1024]{1,0:T(8,128)(2,1)} %param.11) | copy-start | bytes 30724
  7.2 4.6 %copy-start.27 = (s32[512]{0:T(512)S(1)}, s32[512]{0:T(512)}, u32[]{:S(2)}) copy-start(s32[512]{0:T(512)} %param.8) | copy-start | bytes 6148
  7.2 20.6 %all-gather.3.cloned.1.call-start = ((), (), s32[]{:S(2)}) async-start(), calls=%async_computation | async-start | bytes 3145728 | tf_op jit(solution)/shard_map/all_gather | solution.py:166
  9.3 3.7 %copy-start.3 = (bf16[512,1024]{1,0:T(8,128)(2,1)S(1)}, bf16[512,1024]{1,0:T(8,128)(2,1)}, u32[]{:S(2)}) copy-start(bf16[512,1024]{1,0:T(8,128)(2,1)} %param.14) | copy-start | bytes 3145732
  9.3 10.5 %copy-start.14 = (bf16[2,9,1024]{2,0,1:T(2,128)(2,1)S(1)}, bf16[2,9,1024]{2,0,1:T(2,128)(2,1)}, u32[]{:S(2)}) copy-start(bf16[2,9,1024]{2,0,1:T(2,128)(2,1)} %param.12) | copy-start | bytes 110596
  11.8 74.4 %all-gather.5.cloned.1.call-start = ((), (), s32[]{:S(2)}) async-start(), calls=%async_computation.1 | async-start | bytes 3145728 | tf_op jit(solution)/shard_map/all_gather | solution.py:166
  13.0 7.6 %collective-permute-start.1 = (bf16[48,1024]{1,0:T(8,128)(2,1)S(1)}, bf16[48,1024]{1,0:T(8,128)(2,1)S(1)}, u32[]{:S(2)}, u32[]{:S(2)}) collective-permute-start(bf16[48,1024]{1,0:T(8,128)(2,1)S(1)} %pad_maximum_fusion.5), channel_id=1, source_target_pairs={{2,0},{4,2},{6,4},{8,6},{10,8},{12,10},{14,12},{16,14},{18,16},{20... | collective-permute-start | bytes 294920 | tf_op jit(solution)/shard_map/ppermute | solution.py:31
  14.3 9.5 %collective-permute-start = (bf16[48,1024]{1,0:T(8,128)(2,1)S(1)}, bf16[48,1024]{1,0:T(8,128)(2,1)S(1)}, u32[]{:S(2)}, u32[]{:S(2)}) collective-permute-start(bf16[48,1024]{1,0:T(8,128)(2,1)S(1)} %pad_maximum_fusion.4), channel_id=1, source_target_pairs={{0,2},{2,4},{4,6},{6,8},{8,10},{10,12},{12,14},{14,16},{16,18},{18... | collective-permute-start | bytes 294920 | tf_op jit(solution)/shard_map/ppermute | solution.py:30
  19.9 62.5 %copy-start.15 = (f32[1,1,1024]{2,0,1:T(1,128)}, f32[1,1,1024]{2,0,1:T(1,128)S(1)}, u32[]{:S(2)}) copy-start(f32[1,1,1024]{2,0,1:T(1,128)S(1)} %get-tuple-element.188) | copy-start | bytes 12292
  19.9 62.5 %copy-start.17 = (f32[1,1,1024]{2,0,1:T(1,128)}, f32[1,1,1024]{2,0,1:T(1,128)S(1)}, u32[]{:S(2)}) copy-start(f32[1,1,1024]{2,0,1:T(1,128)S(1)} %get-tuple-element.189) | copy-start | bytes 12292
  19.9 62.5 %copy-start.19 = (f32[1,1,1024]{2,0,1:T(1,128)}, f32[1,1,1024]{2,0,1:T(1,128)S(1)}, u32[]{:S(2)}) copy-start(f32[1,1,1024]{2,0,1:T(1,128)S(1)} %get-tuple-element.190) | copy-start | bytes 12292
  19.9 62.5 %copy-start.21 = (f32[1,1,1024]{2,0,1:T(1,128)}, f32[1,1,1024]{2,0,1:T(1,128)S(1)}, u32[]{:S(2)}) copy-start(f32[1,1,1024]{2,0,1:T(1,128)S(1)} %get-tuple-element.200) | copy-start | bytes 12292
  19.9 62.5 %copy-start.23 = (f32[1,1,1024]{2,0,1:T(1,128)}, f32[1,1,1024]{2,0,1:T(1,128)S(1)}, u32[]{:S(2)}) copy-start(f32[1,1,1024]{2,0,1:T(1,128)S(1)} %get-tuple-element.201) | copy-start | bytes 12292
  27.8 13.3 %copy-start.8 = (bf16[512,1024]{1,0:T(8,128)(2,1)S(1)}, bf16[512,1024]{1,0:T(8,128)(2,1)}, u32[]{:S(2)}) copy-start(bf16[512,1024]{1,0:T(8,128)(2,1)} %get-tuple-element.58) | copy-start | bytes 3145732
  27.8 13.3 %copy-start.28 = (bf16[512,2048]{1,0:T(8,128)(2,1)S(1)}, bf16[512,2048]{1,0:T(8,128)(2,1)}, u32[]{:S(2)}) copy-start(bf16[512,2048]{1,0:T(8,128)(2,1)} %all-gather.3.cloned.1.call-done) | copy-start | bytes 6291460
  34.7 18.8 %collective-permute-start.3 = (bf16[32,1024]{1,0:T(8,128)(2,1)S(1)}, bf16[32,1024]{1,0:T(8,128)(2,1)S(1)}, u32[]{:S(2)}, u32[]{:S(2)}) collective-permute-start(bf16[32,1024]{1,0:T(8,128)(2,1)S(1)} %get-tuple-element.166), channel_id=1, source_target_pairs={{2,0},{4,2},{6,4},{8,6},{10,8},{12,10},{14,12},{16,14},{18,16},{20... | collective-permute-start | bytes 196616 | tf_op jit(solution)/shard_map/ppermute | solution.py:21
  36.0 17.5 %collective-permute-start.2 = (bf16[32,1024]{1,0:T(8,128)(2,1)S(1)}, bf16[32,1024]{1,0:T(8,128)(2,1)S(1)}, u32[]{:S(2)}, u32[]{:S(2)}) collective-permute-start(bf16[32,1024]{1,0:T(8,128)(2,1)S(1)} %get-tuple-element.167), channel_id=1, source_target_pairs={{0,2},{2,4},{4,6},{6,8},{8,10},{10,12},{12,14},{14,16},{16,18},{18... | collective-permute-start | bytes 196616 | tf_op jit(solution)/shard_map/ppermute | solution.py:20
  48.4 5.5 %copy-start.4 = (bf16[512,1024]{1,0:T(8,128)(2,1)S(1)}, bf16[512,1024]{1,0:T(8,128)(2,1)}, u32[]{:S(2)}) copy-start(bf16[512,1024]{1,0:T(8,128)(2,1)} %param.15) | copy-start | bytes 3145732
  48.4 26.0 %collective-permute-start.4 = (bf16[2,2,2,64,1024]{4,3,1,0,2:T(8,128)(2,1)}, bf16[2,2,2,64,1024]{4,3,1,0,2:T(8,128)(2,1)}, u32[]{:S(2)}, u32[]{:S(2)}) collective-permute-start(bf16[2,2,2,64,1024]{4,3,1,0,2:T(8,128)(2,1)} %bitcast.133), channel_id=1, source_target_pairs={{0,2},{2,0},{4,6},{6,4},{8,10},{10,8},{12,14},{14,12},{16,18},{18,... | collective-permute-start | bytes 3145736 | tf_op jit(solution)/shard_map/ppermute | solution.py:86
  51.3 24.5 %collective-permute-start.5 = (bf16[2,2,2,64,1024]{4,3,1,0,2:T(8,128)(2,1)}, bf16[2,2,2,64,1024]{4,3,1,0,2:T(8,128)(2,1)}, u32[]{:S(2)}, u32[]{:S(2)}) collective-permute-start(bf16[2,2,2,64,1024]{4,3,1,0,2:T(8,128)(2,1)} %bitcast.132), channel_id=1, source_target_pairs={{0,4},{2,6},{4,0},{6,2},{8,12},{10,14},{12,8},{14,10},{16,20},{18,... | collective-permute-start | bytes 3145736 | tf_op jit(solution)/shard_map/ppermute | solution.py:86
  80.1 32.9 %collective-permute-start.9 = (bf16[2,2,64,1024]{3,2,1,0:T(8,128)(2,1)}, bf16[2,2,64,1024]{3,2,1,0:T(8,128)(2,1)}, u32[]{:S(2)}, u32[]{:S(2)}) collective-permute-start(bf16[2,2,64,1024]{3,2,1,0:T(8,128)(2,1)} %get-tuple-element.158), channel_id=1, source_target_pairs={{0,2},{2,0},{4,6},{6,4},{8,10},{10,8},{12,14},{14,12},{16,18},{18,... | collective-permute-start | bytes 1572872 | tf_op jit(solution)/shard_map/ppermute | solution.py:86
  81.4 31.6 %collective-permute-start.8 = (bf16[2,2,64,1024]{3,2,1,0:T(8,128)(2,1)}, bf16[2,2,64,1024]{3,2,1,0:T(8,128)(2,1)}, u32[]{:S(2)}, u32[]{:S(2)}) collective-permute-start(bf16[2,2,64,1024]{3,2,1,0:T(8,128)(2,1)} %get-tuple-element.160), channel_id=1, source_target_pairs={{0,4},{2,6},{4,0},{6,2},{8,12},{10,14},{12,8},{14,10},{16,20},{18,... | collective-permute-start | bytes 1572872 | tf_op jit(solution)/shard_map/ppermute | solution.py:86
  95.3 25.3 %copy-start.10 = (f32[9,1024]{1,0:T(8,128)}, f32[9,1024]{1,0:T(8,128)S(1)}, u32[]{:S(2)}) copy-start(f32[9,1024]{1,0:T(8,128)S(1)} %broadcast_multiply_fusion.1) | copy-start | bytes 110596
  95.3 15.7 %collective-permute-start.7 = (bf16[16,1024]{1,0:T(8,128)(2,1)S(1)}, bf16[16,1024]{1,0:T(8,128)(2,1)S(1)}, u32[]{:S(2)}, u32[]{:S(2)}) collective-permute-start(bf16[16,1024]{1,0:T(8,128)(2,1)S(1)} %get-tuple-element.162), channel_id=1, source_target_pairs={{2,0},{4,2},{6,4},{8,6},{10,8},{12,10},{14,12},{16,14},{18,16},{20... | collective-permute-start | bytes 98312 | tf_op jit(solution)/shard_map/ppermute | solution.py:21
  96.6 16.3 %collective-permute-start.6 = (bf16[16,1024]{1,0:T(8,128)(2,1)S(1)}, bf16[16,1024]{1,0:T(8,128)(2,1)S(1)}, u32[]{:S(2)}, u32[]{:S(2)}) collective-permute-start(bf16[16,1024]{1,0:T(8,128)(2,1)S(1)} %get-tuple-element.163), channel_id=1, source_target_pairs={{0,2},{2,4},{4,6},{6,8},{8,10},{10,12},{12,14},{14,16},{16,18},{18... | collective-permute-start | bytes 98312 | tf_op jit(solution)/shard_map/ppermute | solution.py:20
  107.2 5.8 %copy-start.7 = (bf16[2,2,64,1024]{3,2,1,0:T(8,128)(2,1)S(1)}, bf16[2,2,64,1024]{3,2,1,0:T(8,128)(2,1)}, u32[]{:S(2)}) copy-start(bf16[2,2,64,1024]{3,2,1,0:T(8,128)(2,1)} %get-tuple-element.79) | copy-start | bytes 1572868
  108.4 22.5 %collective-permute-start.11 = (bf16[2,2,2,64,1024]{4,3,2,1,0:T(8,128)(2,1)}, bf16[2,2,2,64,1024]{4,3,2,1,0:T(8,128)(2,1)}, u32[]{:S(2)}, u32[]{:S(2)}) collective-permute-start(bf16[2,2,2,64,1024]{4,3,2,1,0:T(8,128)(2,1)} %get-tuple-element.146), channel_id=1, source_target_pairs={{0,2},{2,0},{4,6},{6,4},{8,10},{10,8},{12,14},{14,12},{16,18},{18,... | collective-permute-start | bytes 3145736 | tf_op jit(solution)/shard_map/ppermute | solution.py:86
  111.0 22.2 %collective-permute-start.12 = (bf16[2,2,2,64,1024]{4,3,2,1,0:T(8,128)(2,1)}, bf16[2,2,2,64,1024]{4,3,2,1,0:T(8,128)(2,1)}, u32[]{:S(2)}, u32[]{:S(2)}) collective-permute-start(bf16[2,2,2,64,1024]{4,3,2,1,0:T(8,128)(2,1)} %get-tuple-element.144), channel_id=1, source_target_pairs={{0,4},{2,6},{4,0},{6,2},{8,12},{10,14},{12,8},{14,10},{16,20},{18,... | collective-permute-start | bytes 3145736 | tf_op jit(solution)/shard_map/ppermute | solution.py:86
  115.1 12.2 %collective-permute-start.13 = (bf16[2,64,1024]{2,1,0:T(8,128)(2,1)}, bf16[2,64,1024]{2,1,0:T(8,128)(2,1)}, u32[]{:S(2)}, u32[]{:S(2)}) collective-permute-start(bf16[2,64,1024]{2,1,0:T(8,128)(2,1)} %get-tuple-element.178), channel_id=1, source_target_pairs={{0,8},{2,10},{4,12},{6,14},{8,0},{10,2},{12,4},{14,6},{16,24},{18,... | collective-permute-start | bytes 786440 | tf_op jit(solution)/shard_map/ppermute | solution.py:86
  117.0 3.4 %copy-start.26 = (s32[512]{0:T(512)S(1)}, s32[512]{0:T(512)}, u32[]{:S(2)}) copy-start(s32[512]{0:T(512)} %copy-done.25) | copy-start | bytes 6148
  117.0 4.9 %copy-start.6 = (bf16[2,2,64,1024]{3,2,1,0:T(8,128)(2,1)S(1)}, bf16[2,2,64,1024]{3,2,1,0:T(8,128)(2,1)}, u32[]{:S(2)}) copy-start(bf16[2,2,64,1024]{3,2,1,0:T(8,128)(2,1)} %get-tuple-element.81) | copy-start | bytes 1572868
  120.6 6.6 %copy-start.11 = (f32[9,1024]{1,0:T(8,128)S(1)}, f32[9,1024]{1,0:T(8,128)}, u32[]{:S(2)}) copy-start(f32[9,1024]{1,0:T(8,128)} %copy-done.10) | copy-start | bytes 110596
  120.7 6.6 %collective-permute-start.10 = (f32[23,1024]{1,0:T(8,128)S(1)}, f32[23,1024]{1,0:T(8,128)S(1)}, u32[]{:S(2)}, u32[]{:S(2)}) collective-permute-start(f32[23,1024]{1,0:T(8,128)S(1)} %pad_maximum_fusion.6), channel_id=1, source_target_pairs={{0,16},{2,18},{4,20},{6,22},{8,24},{10,26},{12,28},{14,30},{16,0},... | collective-permute-start | bytes 282632 | tf_op jit(solution)/shard_map/ppermute | solution.py:86
  124.0 6.6 %collective-permute-start.14 = (bf16[2,64,1024]{2,1,0:T(8,128)(2,1)}, bf16[2,64,1024]{2,1,0:T(8,128)(2,1)S(1)}, u32[]{:S(2)}, u32[]{:S(2)}) collective-permute-start(bf16[2,64,1024]{2,1,0:T(8,128)(2,1)} %get-tuple-element.176), channel_id=1, source_target_pairs={{0,8},{2,10},{4,12},{6,14},{8,0},{10,2},{12,4},{14,6},{16,24},{18,... | collective-permute-start | bytes 786440 | tf_op jit(solution)/shard_map/ppermute | solution.py:86
  135.0 15.3 %collective-permute-start.16 = (bf16[2,2,64,1024]{3,2,0,1:T(8,128)(2,1)S(1)}, bf16[2,2,64,1024]{3,2,0,1:T(8,128)(2,1)S(1)}, u32[]{:S(2)}, u32[]{:S(2)}) collective-permute-start(bf16[2,2,64,1024]{3,2,0,1:T(8,128)(2,1)S(1)} %bitcast.150), channel_id=1, source_target_pairs={{0,4},{2,6},{4,0},{6,2},{8,12},{10,14},{12,8},{14,10},{16,20},{18,... | collective-permute-start | bytes 1572872 | tf_op jit(solution)/shard_map/ppermute | solution.py:86
  138.4 4.2 %copy-start.9 = (bf16[2,64,1024]{2,1,0:T(8,128)(2,1)S(1)}, bf16[2,64,1024]{2,1,0:T(8,128)(2,1)}, u32[]{:S(2)}) copy-start(bf16[2,64,1024]{2,1,0:T(8,128)(2,1)} %get-tuple-element.90) | copy-start | bytes 786436
  138.4 4.2 %copy-start.13 = (bf16[2,64,1024]{2,1,0:T(8,128)(2,1)S(1)}, bf16[2,64,1024]{2,1,0:T(8,128)(2,1)}, u32[]{:S(2)}) copy-start(bf16[2,64,1024]{2,1,0:T(8,128)(2,1)} %copy-done.12) | copy-start | bytes 786436
  138.5 11.7 %collective-permute-start.17 = (bf16[2,2,64,1024]{3,2,0,1:T(8,128)(2,1)S(1)}, bf16[2,2,64,1024]{3,2,0,1:T(8,128)(2,1)S(1)}, u32[]{:S(2)}, u32[]{:S(2)}) collective-permute-start(bf16[2,2,64,1024]{3,2,0,1:T(8,128)(2,1)S(1)} %bitcast.151), channel_id=1, source_target_pairs={{0,2},{2,0},{4,6},{6,4},{8,10},{10,8},{12,14},{14,12},{16,18},{18,... | collective-permute-start | bytes 1572872 | tf_op jit(solution)/shard_map/ppermute | solution.py:86
  140.0 10.0 %collective-permute-start.18 = (bf16[64,1024]{1,0:T(8,128)(2,1)S(1)}, bf16[64,1024]{1,0:T(8,128)(2,1)S(1)}, u32[]{:S(2)}, u32[]{:S(2)}) collective-permute-start(bf16[64,1024]{1,0:T(8,128)(2,1)S(1)} %get-tuple-element.182), channel_id=1, source_target_pairs={{0,16},{2,18},{4,20},{6,22},{8,24},{10,26},{12,28},{14,30},{16,0},... | collective-permute-start | bytes 393224 | tf_op jit(solution)/shard_map/ppermute | solution.py:86
  142.7 7.5 %collective-permute-start.19 = (bf16[64,1024]{1,0:T(8,128)(2,1)S(1)}, bf16[64,1024]{1,0:T(8,128)(2,1)S(1)}, u32[]{:S(2)}, u32[]{:S(2)}) collective-permute-start(bf16[64,1024]{1,0:T(8,128)(2,1)S(1)} %get-tuple-element.180), channel_id=1, source_target_pairs={{0,16},{2,18},{4,20},{6,22},{8,24},{10,26},{12,28},{14,30},{16,0},... | collective-permute-start | bytes 393224 | tf_op jit(solution)/shard_map/ppermute | solution.py:86
  143.1 6.8 %collective-permute-start.15 = (f32[23,1024]{1,0:T(8,128)S(1)}, f32[23,1024]{1,0:T(8,128)S(1)}, u32[]{:S(2)}, u32[]{:S(2)}) collective-permute-start(f32[23,1024]{1,0:T(8,128)S(1)} %fusion.100), channel_id=1, source_target_pairs={{0,8},{2,10},{4,12},{6,14},{8,0},{10,2},{12,4},{14,6},{16,24},{18,... | collective-permute-start | bytes 282632 | tf_op jit(solution)/shard_map/ppermute | solution.py:86
  150.5 7.4 %collective-permute-start.21 = (bf16[2,64,1024]{2,1,0:T(8,128)(2,1)S(1)}, bf16[2,64,1024]{2,1,0:T(8,128)(2,1)S(1)}, u32[]{:S(2)}, u32[]{:S(2)}) collective-permute-start(bf16[2,64,1024]{2,1,0:T(8,128)(2,1)S(1)} %get-tuple-element.174), channel_id=1, source_target_pairs={{0,8},{2,10},{4,12},{6,14},{8,0},{10,2},{12,4},{14,6},{16,24},{18,... | collective-permute-start | bytes 786440 | tf_op jit(solution)/shard_map/ppermute | solution.py:86
  153.0 8.3 %collective-permute-start.22 = (bf16[2,64,1024]{2,1,0:T(8,128)(2,1)S(1)}, bf16[2,64,1024]{2,1,0:T(8,128)(2,1)S(1)}, u32[]{:S(2)}, u32[]{:S(2)}) collective-permute-start(bf16[2,64,1024]{2,1,0:T(8,128)(2,1)S(1)} %get-tuple-element.172), channel_id=1, source_target_pairs={{0,8},{2,10},{4,12},{6,14},{8,0},{10,2},{12,4},{14,6},{16,24},{18,... | collective-permute-start | bytes 786440 | tf_op jit(solution)/shard_map/ppermute | solution.py:86
  153.1 4.7 %collective-permute-start.20 = (f32[23,1024]{1,0:T(8,128)S(1)}, f32[23,1024]{1,0:T(8,128)S(1)}, u32[]{:S(2)}, u32[]{:S(2)}) collective-permute-start(f32[23,1024]{1,0:T(8,128)S(1)} %add.314), channel_id=1, source_target_pairs={{0,4},{2,6},{4,0},{6,2},{8,12},{10,14},{12,8},{14,10},{16,20},{18,... | collective-permute-start | bytes 282632 | tf_op jit(solution)/shard_map/ppermute | solution.py:86
  161.3 6.4 %collective-permute-start.25 = (f32[23,1024]{1,0:T(8,128)S(1)}, f32[23,1024]{1,0:T(8,128)S(1)}, u32[]{:S(2)}, u32[]{:S(2)}) collective-permute-start(f32[23,1024]{1,0:T(8,128)S(1)} %add.321), channel_id=1, source_target_pairs={{0,2},{2,0},{4,6},{6,4},{8,10},{10,8},{12,14},{14,12},{16,18},{18,... | collective-permute-start | bytes 282632 | tf_op jit(solution)/shard_map/ppermute | solution.py:86
  164.5 5.9 %collective-permute-start.23 = (bf16[64,1024]{1,0:T(8,128)(2,1)S(1)}, bf16[64,1024]{1,0:T(8,128)(2,1)S(1)}, u32[]{:S(2)}, u32[]{:S(2)}) collective-permute-start(bf16[64,1024]{1,0:T(8,128)(2,1)S(1)} %dynamic-slice_bitcast_fusion.17), channel_id=1, source_target_pairs={{0,16},{2,18},{4,20},{6,22},{8,24},{10,26},{12,28},{14,30},{16,0},... | collective-permute-start | bytes 393224 | tf_op jit(solution)/shard_map/ppermute | solution.py:86
  164.9 9.7 %collective-permute-start.24 = (bf16[64,1024]{1,0:T(8,128)(2,1)S(1)}, bf16[64,1024]{1,0:T(8,128)(2,1)S(1)}, u32[]{:S(2)}, u32[]{:S(2)}) collective-permute-start(bf16[64,1024]{1,0:T(8,128)(2,1)S(1)} %dynamic-slice_bitcast_fusion.16), channel_id=1, source_target_pairs={{0,16},{2,18},{4,20},{6,22},{8,24},{10,26},{12,28},{14,30},{16,0},... | collective-permute-start | bytes 393224 | tf_op jit(solution)/shard_map/ppermute | solution.py:86
  168.4 7.3 %copy-start.1 = (bf16[5,1024]{1,0:T(8,128)(2,1)S(1)}, bf16[5,1024]{1,0:T(8,128)(2,1)}, u32[]{:S(2)}) copy-start(bf16[5,1024]{1,0:T(8,128)(2,1)} %param.11) | copy-start | bytes 30724
  (10 other events, 22.3 us)
Sparse Core Ops, SparseCore 0:
  11.9 13.2 all-gather.2
  57.9 10.3 all-gather.4
